TPU v7x, 32 devices: a whole 2x2x4 slice. The times are simulated.
32 devices in a mesh: blk: 8 (over z, x), batch: 4 (over y, core).
Axes of the slice: x: 2, y: 2, z: 4, core: 2. Of those that a mesh axis runs over, the one named last changes fastest.
Arguments:
- inputs: float32 [64, 128, 4096], P('batch', None, 'blk'), may hold values from -6 to 6
- weight_in: float32 [512, 128], replicated, may hold values from -0.5 to 0.5
- bias_in: float32 [512], replicated, may hold values from -3 to 3
- slope_in: float32 [512], replicated, may hold values from 0.05 to 0.6
- gain_in: float32 [512], replicated, may hold values from 0.25 to 1.75
- shift_in: float32 [512], replicated, may hold values from -3 to 3
- depthwise_weight: float32 [512, 3], replicated, may hold values from -3.5 to 3.5
- depthwise_bias: float32 [512], replicated, may hold values from -3 to 3
- slope_mid: float32 [512], replicated, may hold values from 0.05 to 0.6
- gain_mid: float32 [512], replicated, may hold values from 0.25 to 1.75
- shift_mid: float32 [512], replicated, may hold values from -3 to 3
- weight_res: float32 [128, 512], replicated, may hold values from -0.25 to 0.25
- bias_res: float32 [128], replicated, may hold values from -3 to 3
- weight_skip: float32 [128, 512], replicated, may hold values from -0.25 to 0.25
- bias_skip: float32 [128], replicated, may hold values from -3 to 3
- lengths: int32 [64], P('batch'), may hold values from 2049 to 4096, as said below
- cot_res: float32 [64, 128, 4096], P('batch', None, 'blk'), may hold values from -6 to 6
- cot_skip: float32 [64, 128, 4096], P('batch', None, 'blk'), may hold values from -6 to 6
Outputs:
- residual_out: float32 [64, 128, 4096], P('batch', None, 'blk')
- skip_out: float32 [64, 128, 4096], P('batch', None, 'blk')
- grad_inputs: float32 [64, 128, 4096], P('batch', None, 'blk')
- grad_weight_in: float32 [512, 128], replicated
- grad_bias_in: float32 [512], replicated
- grad_slope_in: float32 [512], replicated
- grad_gain_in: float32 [512], replicated
- grad_shift_in: float32 [512], replicated
- grad_weight_depth: float32 [512, 3], replicated
- grad_bias_depth: float32 [512], replicated
- grad_slope_mid: float32 [512], replicated
- grad_gain_mid: float32 [512], replicated
- grad_shift_mid: float32 [512], replicated
- grad_weight_res: float32 [128, 512], replicated
- grad_bias_res: float32 [128], replicated
- grad_weight_skip: float32 [128, 512], replicated
- grad_bias_skip: float32 [128], replicated
Inputs may be any that keep to these rules, and one draw needn't show every extreme that they name: `lengths`: in each aligned group of 16 consecutive items one item, which one drawn from the seed, has 4096 valid frames.
All inputs are finite; a program needn't handle non-finite values.
Results may differ from a plain program's by a relative error of at most 0.0003.
Values sent between devices are 32-bit elements; how exact they have to be, the bound alone decides.
No kernel may reach another device: no remote copies, remote signals or barrier semaphores. Data moves between devices by JAX's collectives and lax.ppermute only.
A program may use at most 256 MiB of HBM per device.

v0:
```python
import jax
import jax.numpy as jnp
from jax import lax
from jax.sharding import PartitionSpec as P

DILATION_STEP = 8


EPS = 1e-05


def prefix_2(value, axis, join, neutral):
    count, mine = (lax.axis_size(axis), lax.axis_index(axis))
    pieces = jax.tree.map(lambda part: lax.all_gather(part, axis), value)
    total = jax.tree.map(
        lambda part, zero: jnp.full_like(part, 0) + jnp.asarray(zero, part.dtype), value, neutral
    )

    def step(position, total):
        longer = join(total, jax.tree.map(lambda part: part[position], pieces))
        return jax.tree.map(lambda new, old: jnp.where(position < mine, new, old), longer, total)

    return lax.fori_loop(0, count - 1, step, total)


def spread(value, axis, source):
    kept = jnp.where(lax.axis_index(axis) == source, value, 0).astype(value.dtype)
    return lax.psum(kept, axis)


def with_halo(block, sides, width):
    for axis, dim in sides:
        count = lax.axis_size(axis)
        forward = [(i, i + 1) for i in range(count - 1)]
        backward = [(target, source) for source, target in forward]
        low = lax.ppermute(
            lax.slice_in_dim(block, block.shape[dim] - width, None, axis=dim), axis, forward
        )
        high = lax.ppermute(lax.slice_in_dim(block, 0, width, axis=dim), axis, backward)
        block = jnp.concatenate([low, block, high], axis=dim)
    return block


def smooth_act(value, slope):
    soft = jax.nn.silu(value)
    return soft + slope * (value - soft)


def smooth_slope(value, slope):
    sig = jax.nn.sigmoid(value)
    dsoft = sig * (1.0 + value * (1.0 - sig))
    return dsoft + slope * (1.0 - dsoft)


def add_pair(earlier, later):
    return (earlier[0] + later[0], earlier[1] + later[1])


def item_totals(first, second):
    prefix = prefix_2(
        (first, second), "blk", add_pair, (jnp.zeros_like(first), jnp.zeros_like(second))
    )
    ending = (prefix[0] + first, prefix[1] + second)
    return (
        spread(ending[0], "blk", lax.axis_size("blk") - 1),
        spread(ending[1], "blk", lax.axis_size("blk") - 1),
    )


def norm_forward(value, valid, count):
    masked = value * valid
    tot_sum, tot_sq = item_totals(
        jnp.sum(masked, axis=(1, 2)), jnp.sum(masked * value, axis=(1, 2))
    )
    mean = tot_sum / count
    var = tot_sq / count - mean * mean
    scale = lax.rsqrt(var + EPS)[:, None, None]
    return ((value - mean[:, None, None]) * scale, scale)


def norm_backward(dnormal, normal, scale, valid, count):
    sum_a, sum_b = item_totals(
        jnp.sum(dnormal, axis=(1, 2)), jnp.sum(dnormal * normal, axis=(1, 2))
    )
    mean_a = (sum_a / count)[:, None, None]
    mean_b = (sum_b / count)[:, None, None]
    return valid * scale * (dnormal - mean_a - normal * mean_b)


def local(
    inputs,
    weight_in,
    bias_in,
    slope_in,
    gain_in,
    shift_in,
    depthwise_weight,
    depthwise_bias,
    slope_mid,
    gain_mid,
    shift_mid,
    weight_res,
    bias_res,
    weight_skip,
    bias_skip,
    lengths,
    cot_res,
    cot_skip,
):
    hp = lax.Precision.HIGHEST
    time_extent = inputs.shape[2]
    width = weight_in.shape[0]
    frame = lax.axis_index("blk") * time_extent + lax.iota(jnp.int32, time_extent)
    valid = (frame[None, :] < lengths[:, None]).astype(jnp.float32)[:, None, :]
    count = lengths.astype(jnp.float32) * width

    def column(vec):
        return vec[None, :, None]

    upper = jnp.einsum("oc,ict->iot", weight_in, inputs, precision=hp) + column(bias_in)
    act_one = smooth_act(upper, column(slope_in))
    normal_one, scale_one = norm_forward(act_one, valid, count)
    normalized_input = valid * (column(gain_in) * normal_one + column(shift_in))
    extended_input = with_halo(normalized_input, (("blk", 2),), DILATION_STEP)
    before = extended_input[:, :, :time_extent]
    post_activation = extended_input[:, :, 2 * DILATION_STEP : 2 * DILATION_STEP + time_extent]
    depthwise_output = (
        column(depthwise_weight[:, 0]) * before
        + column(depthwise_weight[:, 1]) * normalized_input
        + column(depthwise_weight[:, 2]) * post_activation
        + column(depthwise_bias)
    )
    act_two = smooth_act(depthwise_output, column(slope_mid))
    normal_two, scale_two = norm_forward(act_two, valid, count)
    hidden = valid * (column(gain_mid) * normal_two + column(shift_mid))
    residual_out = (
        inputs + jnp.einsum("co,iot->ict", weight_res, hidden, precision=hp) + column(bias_res)
    )
    skip_out = jnp.einsum("co,iot->ict", weight_skip, hidden, precision=hp) + column(bias_skip)
    dres = valid * cot_res
    dskip = valid * cot_skip
    grad_weight_res = jnp.einsum("ict,iot->co", dres, hidden, precision=hp)
    grad_bias_res = jnp.sum(dres, axis=(0, 2))
    grad_weight_skip = jnp.einsum("ict,iot->co", dskip, hidden, precision=hp)
    grad_bias_skip = jnp.sum(dskip, axis=(0, 2))
    dhid = jnp.einsum("co,ict->iot", weight_res, dres, precision=hp) + jnp.einsum(
        "co,ict->iot", weight_skip, dskip, precision=hp
    )
    grad_gain_mid = jnp.sum(dhid * normal_two, axis=(0, 2))
    grad_shift_mid = jnp.sum(dhid, axis=(0, 2))
    dact_two = norm_backward(dhid * column(gain_mid), normal_two, scale_two, valid, count)
    grad_depthwise_output = dact_two * smooth_slope(depthwise_output, column(slope_mid))
    grad_slope_mid = jnp.sum(
        dact_two * (depthwise_output - jax.nn.silu(depthwise_output)), axis=(0, 2)
    )
    grad_extended_input = with_halo(grad_depthwise_output, (("blk", 2),), DILATION_STEP)
    grad_before = grad_extended_input[:, :, :time_extent]
    grad_post_activation = grad_extended_input[
        :, :, 2 * DILATION_STEP : 2 * DILATION_STEP + time_extent
    ]
    grad_weight_depth = jnp.stack(
        [
            jnp.sum(grad_depthwise_output * before, axis=(0, 2)),
            jnp.sum(grad_depthwise_output * normalized_input, axis=(0, 2)),
            jnp.sum(grad_depthwise_output * post_activation, axis=(0, 2)),
        ],
        axis=1,
    )
    grad_bias_depth = jnp.sum(grad_depthwise_output, axis=(0, 2))
    dnormed = valid * (
        column(depthwise_weight[:, 0]) * grad_post_activation
        + column(depthwise_weight[:, 1]) * grad_depthwise_output
        + column(depthwise_weight[:, 2]) * grad_before
    )
    grad_gain_in = jnp.sum(dnormed * normal_one, axis=(0, 2))
    grad_shift_in = jnp.sum(dnormed, axis=(0, 2))
    dact_one = norm_backward(dnormed * column(gain_in), normal_one, scale_one, valid, count)
    dupper = dact_one * smooth_slope(upper, column(slope_in))
    grad_slope_in = jnp.sum(dact_one * (upper - jax.nn.silu(upper)), axis=(0, 2))
    grad_weight_in = jnp.einsum("iot,ict->oc", dupper, inputs, precision=hp)
    grad_bias_in = jnp.sum(dupper, axis=(0, 2))
    grad_inputs = dres + jnp.einsum("oc,iot->ict", weight_in, dupper, precision=hp)
    grads = (
        grad_weight_in,
        grad_bias_in,
        grad_slope_in,
        grad_gain_in,
        grad_shift_in,
        grad_weight_depth,
        grad_bias_depth,
        grad_slope_mid,
        grad_gain_mid,
        grad_shift_mid,
        grad_weight_res,
        grad_bias_res,
        grad_weight_skip,
        grad_bias_skip,
    )
    summed = lax.psum(
        (
            grads[0],
            grads[1],
            grads[2],
            grads[3],
            grads[4],
            grads[5],
            grads[6],
            grads[7],
            grads[8],
            grads[9],
            grads[10],
            grads[11],
            grads[12],
            grads[13],
        ),
        ("blk", "batch"),
    )
    return (residual_out, skip_out, grad_inputs) + tuple(summed)


def solution(mesh):
    return jax.shard_map(
        local,
        mesh=mesh,
        in_specs=(
            P("batch", None, "blk"),
            P(),
            P(),
            P(),
            P(),
            P(),
            P(),
            P(),
            P(),
            P(),
            P(),
            P(),
            P(),
            P(),
            P(),
            P("batch"),
            P("batch", None, "blk"),
            P("batch", None, "blk"),
        ),
        out_specs=(
            P("batch", None, "blk"),
            P("batch", None, "blk"),
            P("batch", None, "blk"),
            P(),
            P(),
            P(),
            P(),
            P(),
            P(),
            P(),
            P(),
            P(),
            P(),
            P(),
            P(),
            P(),
            P(),
        ),
        check_vma=False,
    )
```

profile of v0, /device:TPU:0, one launch (start us, length us, event | category | flops | bytes accessed | tf_op | source)
XLA Modules:
  0.0 706.1 jit_solution(2101041160576544081)
XLA Ops:
  7.3 0.7 compare_convert_fusion
  8.0 1.2 dynamic-slice
  10.0 24.5 %fusion = (f32[16]{0:T(128)S(1)}, f32[16]{0:T(128)S(1)}, f32[16,512,512]{2,1,0:T(8,128)}) fusion(f32[16,512]{1,0:T(8,128)S(1)} %compare_convert_fusion, f32[512]{0:T(512)} %param.29, f32[512]{0:T(512)} %param.28, f32[16,128,512]{2,1,0:T(8,128)} %param.26, f32[512,128]{1,0:T(8,128)} %param.27), kind=kOutput, calls=%fused_computation.20 | convolution fusion | flops 6492782592 | bytes 21270656 | tf_op jit(solution)/shard_map/oc,ict->iot/dot_general | solution.py:120
  34.5 0.2 dynamic-update-slice
  34.7 0.2 dynamic-update-slice.1
  34.9 23.1 %all-reduce.17 = (f32[128]{0:T(128)S(1)}, f32[128]{0:T(128)S(1)}) all-reduce(f32[128]{0:T(128)S(1)} %dynamic-update-slice, f32[128]{0:T(128)S(1)} %dynamic-update-slice.1), channel_id=2, replica_groups=mesh['blk'=8,'batch'=4] {'blk'}, use_global_device_ids=true, to_apply=%add | all-reduce | flops 256 | bytes 2048
  58.0 0.1 reshape.147
  58.0 0.1 reshape.148
  58.1 0.3 while.64
  58.4 17.1 %all-reduce.16 = (f32[16]{0:T(128)S(1)}, f32[16]{0:T(128)S(1)}) all-reduce(f32[16]{0:T(128)S(1)} %broadcast_select_fusion.23, f32[16]{0:T(128)S(1)} %broadcast_select_fusion.22), channel_id=1, replica_groups=mesh['blk'=8,'batch'=4] {'blk'}, use_global_device_ids=true, to_apply=%region_4.5 | all-reduce | flops 32 | bytes 256 | tf_op jit(solution)/shard_map/psum | solution.py:28
  75.6 11.7 %add_multiply_fusion.3 = f32[16,512,512]{1,2,0:T(8,128)S(1)} fusion(f32[512]{0:T(512)S(1)} %copy-done.19, f32[16]{0:T(128)S(1)} %get-tuple-element.668, f32[16]{0:T(128)S(1)} %get-tuple-element.669, f32[512]{0:T(512)S(1)} %copy-done.9, f32[16,512]{1,0:T(8,128)S(1)} %compare_convert_fusion, f32[512]{0:T(512)S(1)} %copy-done.10, ...), kind=kLoop, calls=%fused_computation.61 | loop fusion | flops 54525952 | bytes 33595520 | tf_op jit(solution)/shard_map/mul | solution.py:123
  87.3 5.7 copy-done.1
  93.0 4.1 collective-permute-start
  97.1 1.5 collective-permute-start.1
  98.6 5.3 copy.37
  103.9 5.3 copy.38
  109.3 17.3 %fusion.22 = f32[16,512,512]{2,1,0:T(8,128)} fusion(f32[16,128,512]{1,2,0:T(8,128)} %copy.37, f32[16,512]{1,0:T(8,128)S(1)} %compare_convert_fusion, f32[128,512]{1,0:T(8,128)S(1)} %copy-done.7), kind=kOutput, calls=%fused_computation.79 | convolution fusion | flops 6443499520 | bytes 21266432 | tf_op jit(solution)/shard_map/co,ict->iot/dot_general | solution.py:146
  126.5 2.0 multiply_reduce_fusion.11
  128.6 23.4 %fusion.1 = (f32[16]{0:T(128)S(1)}, f32[16]{0:T(128)S(1)}, f32[16,512,512]{1,2,0:T(8,128)}) fusion(f32[16,512]{1,0:T(8,128)S(1)} %compare_convert_fusion, f32[512]{0:T(512)S(1)} %copy-done.15, f32[512]{0:T(512)S(1)} %copy-done.12, f32[16,512,8]{1,2,0:T(8,128)S(1)} %collective-permute-done.1, f32[16,512,512]{1,2,0:T(8,128)} %copy-done.1, ...), kind=kLoop, calls=%fused_computation.21 | loop fusion | flops 79691744 | bytes 34121856 | tf_op jit(solution)/shard_map/reduce_sum | solution.py:73
  152.0 0.2 dynamic-update-slice.3
  152.2 0.2 dynamic-update-slice.2
  152.4 19.7 %all-reduce.15 = (f32[128]{0:T(128)S(1)}, f32[128]{0:T(128)S(1)}) all-reduce(f32[128]{0:T(128)S(1)} %dynamic-update-slice.2, f32[128]{0:T(128)S(1)} %dynamic-update-slice.3), channel_id=4, replica_groups=mesh['blk'=8,'batch'=4] {'blk'}, use_global_device_ids=true, to_apply=%add.2 | all-reduce | flops 256 | bytes 2048
  172.1 0.1 reshape.149
  172.3 0.3 while.65
  172.6 5.3 copy.36
  177.9 17.3 %all-reduce.14 = (f32[16]{0:T(128)S(1)}, f32[16]{0:T(128)S(1)}) all-reduce(f32[16]{0:T(128)S(1)} %broadcast_select_fusion.21, f32[16]{0:T(128)S(1)} %broadcast_select_fusion.20), channel_id=1, replica_groups=mesh['blk'=8,'batch'=4] {'blk'}, use_global_device_ids=true, to_apply=%region_10.11 | all-reduce | flops 32 | bytes 256 | tf_op jit(solution)/shard_map/psum | solution.py:28
  195.3 26.9 %multiply_reduce_fusion.9 = (f32[16]{0:T(128)S(1)}, f32[16]{0:T(128)S(1)}, f32[16,512,512]{2,1,0:T(8,128)}) fusion(f32[16,512,512]{1,2,0:T(8,128)} %get-tuple-element.667, f32[16]{0:T(128)S(1)} %get-tuple-element.665, f32[16]{0:T(128)S(1)} %get-tuple-element.666, f32[512]{0:T(512)S(1)} %copy-done.13, f32[16,512,512]{2,1,0:T(8,128)} %fusion.22, ...), kind=kOutput, calls=%fused_computation.54 | convolution fusion | flops 6472859648 | bytes 54823168 | tf_op jit(solution)/shard_map/co,ict->iot/dot_general | solution.py:146
  222.2 0.2 dynamic-update-slice.5
  222.4 0.2 dynamic-update-slice.4
  222.6 19.1 %all-reduce.13 = (f32[128]{0:T(128)S(1)}, f32[128]{0:T(128)S(1)}) all-reduce(f32[128]{0:T(128)S(1)} %dynamic-update-slice.4, f32[128]{0:T(128)S(1)} %dynamic-update-slice.5), channel_id=6, replica_groups=mesh['blk'=8,'batch'=4] {'blk'}, use_global_device_ids=true, to_apply=%add.4 | all-reduce | flops 256 | bytes 2048
  241.7 0.1 reshape.151
  241.8 0.3 while.66
  242.2 17.1 %all-reduce.12 = (f32[16]{0:T(128)S(1)}, f32[16]{0:T(128)S(1)}) all-reduce(f32[16]{0:T(128)S(1)} %broadcast_select_fusion.18, f32[16]{0:T(128)S(1)} %broadcast_select_fusion.19), channel_id=1, replica_groups=mesh['blk'=8,'batch'=4] {'blk'}, use_global_device_ids=true, to_apply=%region_17.18 | all-reduce | flops 32 | bytes 256 | tf_op jit(solution)/shard_map/psum | solution.py:28
  259.4 33.3 %fusion.7 = (f32[512]{0:T(512)S(1)}, f32[512]{0:T(512)S(1)}, f32[16,512,512]{1,2,0:T(8,128)}) fusion(f32[16,512,512]{2,1,0:T(8,128)} %get-tuple-element.693, f32[16,512,512]{1,2,0:T(8,128)} %get-tuple-element.667, f32[16]{0:T(128)S(1)} %get-tuple-element.665, f32[16]{0:T(128)S(1)} %get-tuple-element.666, f32[512]{0:T(512)S(1)} %copy-done.12, ...), kind=kLoop, calls=%fused_computation.33 | loop fusion | flops 113245184 | bytes 67715328 | tf_op jit(solution)/shard_map/reduce_sum | solution.py:149
  292.6 19.1 %fusion.28 = f32[128,512]{1,0:T(8,128)} fusion(f32[16,512,512]{1,2,0:T(8,128)} %get-tuple-element.678, f32[16,128,512]{1,2,0:T(8,128)} %copy.37, f32[16,512]{1,0:T(8,128)S(1)} %compare_convert_fusion), kind=kOutput, calls=%fused_computation.85 | convolution fusion | flops 6443499520 | bytes 21266432 | tf_op jit(solution)/shard_map/ict,iot->co/dot_general | solution.py:142
  311.8 17.9 %fusion.31 = f32[128,512]{1,0:T(8,128)} fusion(f32[16,512,512]{1,2,0:T(8,128)} %get-tuple-element.678, f32[16,128,512]{1,2,0:T(8,128)S(1)} %copy-done.5, f32[16,512]{1,0:T(8,128)S(1)} %compare_convert_fusion), kind=kOutput, calls=%fused_computation.86 | convolution fusion | flops 6443499520 | bytes 21266432 | tf_op jit(solution)/shard_map/ict,iot->co/dot_general | solution.py:144
  329.7 33.8 %multiply_reduce_fusion.5 = (f32[512]{0:T(512)S(1)}, f32[512]{0:T(512)S(1)}, f32[512]{0:T(512)S(1)}, f32[16,512,512]{1,2,0:T(8,128)}) fusion(f32[16,512,512]{1,2,0:T(8,128)} %copy-done.1, f32[16,512,8]{1,2,0:T(8,128)S(1)} %collective-permute-done, f32[16,512,8]{1,2,0:T(8,128)S(1)} %collective-permute-done.1, f32[512]{0:T(512)S(1)} %copy-done.15, ...), kind=kLoop, calls=%fused_computation.46 | loop fusion | flops 134216192 | bytes 67684608 | tf_op jit(solution)/shard_map/reduce_sum | solution.py:163
  363.5 1.1 fusion.51
  364.6 1.3 collective-permute-start.2
  365.9 4.6 collective-permute-start.3
  370.5 18.7 %fusion.16 = f32[16,128,512]{1,2,0:T(8,128)} fusion(f32[16,128,512]{1,2,0:T(8,128)} %copy.36, f32[16,512,512]{1,2,0:T(8,128)} %get-tuple-element.678, f32[128]{0:T(128)S(1)} %copy-done.22, f32[128,512]{1,0:T(8,128)S(1)} %copy-done.7), kind=kOutput, calls=%fused_computation.70 | convolution fusion | flops 6444548096 | bytes 25428480 | tf_op jit(solution)/shard_map/co,iot->ict/dot_general | solution.py:137
  389.1 17.0 %add_bitcast_fusion = f32[16,128,512]{1,2,0:T(8,128)} fusion(f32[16,512,512]{1,2,0:T(8,128)} %get-tuple-element.678, f32[128]{0:T(128)S(1)} %copy-done.18, f32[128,512]{1,0:T(8,128)S(1)} %copy-done), kind=kOutput, calls=%fused_computation.71 | convolution fusion | flops 6443499520 | bytes 21234176 | tf_op jit(solution)/shard_map/co,iot->ict/dot_general | solution.py:139
  406.1 6.9 reduce_sum.207
  413.0 5.3 copy.44
  418.4 5.3 copy.45
  423.8 23.9 %multiply_reduce_fusion.6 = (f32[512]{0:T(512)S(1)}, f32[16]{0:T(128)S(1)}) fusion(f32[16]{0:T(128)S(1)} %get-tuple-element.668, f32[16]{0:T(128)S(1)} %get-tuple-element.669, f32[16,512,512]{1,2,0:T(8,128)} %get-tuple-element.662, f32[16,512,8]{1,2,0:T(8,128)S(1)} %collective-permute-done.3, f32[512]{0:T(512)S(1)} %bitcast.142, f32[512]{0:T(512)S(1)} %bitcast.149, ...), kind=kLoop, calls=%fused_computation.47 | loop fusion | flops 96468464 | bytes 34126016 | tf_op jit(solution)/shard_map/reduce_sum | solution.py:175
  447.7 0.2 dynamic-update-slice.7
  447.9 17.2 %fusion.47 = (f32[512]{0:T(512)S(1)}, f32[16]{0:T(128)S(1)}, f32[512]{0:T(512)S(1)}) fusion(f32[16,512,512]{1,2,0:T(8,128)} %get-tuple-element.662, f32[16,512,8]{1,2,0:T(8,128)S(1)} %collective-permute-done.3, f32[512]{0:T(512)S(1)} %bitcast.143, f32[512]{0:T(512)S(1)} %bitcast.150, f32[16,512,8]{1,2,0:T(8,128)S(1)} %collective-permute-done.2, ...), kind=kLoop, calls=%fused_computation.117 | loop fusion | flops 50330608 | bytes 17346624 | tf_op jit(solution)/shard_map/reduce_sum | solution.py:176
  465.1 0.2 dynamic-update-slice.6
  465.3 20.0 %all-reduce.11 = (f32[128]{0:T(128)S(1)}, f32[128]{0:T(128)S(1)}) all-reduce(f32[128]{0:T(128)S(1)} %dynamic-update-slice.6, f32[128]{0:T(128)S(1)} %dynamic-update-slice.7), channel_id=8, replica_groups=mesh['blk'=8,'batch'=4] {'blk'}, use_global_device_ids=true, to_apply=%add.6 | all-reduce | flops 256 | bytes 2048
  485.3 0.1 reshape.153
  485.4 0.1 reshape.154
  485.5 0.3 while.67
  485.8 17.1 %all-reduce.10 = (f32[16]{0:T(128)S(1)}, f32[16]{0:T(128)S(1)}) all-reduce(f32[16]{0:T(128)S(1)} %get-tuple-element.694, f32[16]{0:T(128)S(1)} %get-tuple-element.695), channel_id=1, replica_groups=mesh['blk'=8,'batch'=4] {'blk'}, use_global_device_ids=true, to_apply=%region_23.24 | all-reduce | flops 32 | bytes 256 | tf_op jit(solution)/shard_map/psum | solution.py:28
  502.9 31.4 %fusion.48 = (f32[512]{0:T(512)S(1)}, f32[16,512,512]{1,2,0:T(8,128)}) fusion(f32[16]{0:T(128)S(1)} %get-tuple-element.689, f32[16]{0:T(128)S(1)} %get-tuple-element.668, f32[16]{0:T(128)S(1)} %get-tuple-element.669, f32[512]{0:T(512)S(1)} %copy-done.10, f32[16,512,512]{2,1,0:T(8,128)} %get-tuple-element.692, f32[512]{0:T(512)S(1)} %copy-done.11, ...), kind=kLoop, calls=%fused_computation.118 | loop fusion | flops 134217216 | bytes 50936064 | tf_op jit(solution)/shard_map/reduce_sum | solution.py:181
  534.4 30.5 %convolution_bitcast_fusion = f32[512,128]{1,0:T(8,128)} fusion(f32[16,512,512]{1,2,0:T(8,128)} %get-tuple-element.664, f32[16,128,512]{2,1,0:T(8,128)S(1)} %copy-done.6), kind=kOutput, calls=%fused_computation.87 | convolution fusion | flops 6442450944 | bytes 21233664 | tf_op jit(solution)/shard_map/iot,ict->oc/dot_general | solution.py:180
  564.9 25.2 %multiply_reduce_fusion.7 = f32[512]{0:T(512)S(1)} fusion(f32[16,512,512]{2,1,0:T(8,128)} %get-tuple-element.692, f32[512]{0:T(512)S(1)} %copy-done.11, f32[16]{0:T(128)S(1)} %get-tuple-element.689, f32[16]{0:T(128)S(1)} %get-tuple-element.668, f32[16]{0:T(128)S(1)} %get-tuple-element.669, f32[16]{0:T(128)S(1)} %get-tuple-element.688, f32[512]{0:T(512)S(1)} %copy-done.9, ...), kind=kLoop, calls=%fused_computation.48 | loop fusion | flops 104857088 | bytes 34158848 | tf_op jit(solution)/shard_map/reduce_sum | solution.py:179
  590.1 17.4 %bitcast_add_fusion = f32[16,128,512]{1,2,0:T(8,128)} fusion(f32[16,128,512]{1,2,0:T(8,128)S(1)} %copy-done.3, f32[16,512,512]{1,2,0:T(8,128)} %get-tuple-element.664, f32[16,512]{1,0:T(8,128)S(1)} %compare_convert_fusion, f32[512,128]{1,0:T(8,128)S(1)} %copy-done.8), kind=kOutput, calls=%fused_computation.68 | convolution fusion | flops 6444548096 | bytes 25460736 | tf_op jit(solution)/shard_map/oc,iot->ict/dot_general | solution.py:182
  607.5 5.4 copy.46
  612.8 39.1 %all-reduce.8 = (f32[512]{0:T(512)}, f32[512]{0:T(512)}, f32[512]{0:T(512)}, f32[512]{0:T(512)}, f32[512,3]{0,1:T(4,128)}, /*index=5*/f32[512]{0:T(512)}, f32[51...) all-reduce(f32[512]{0:T(512)S(1)} %get-tuple-element.663, ...), channel_id=1, replica_groups=mesh['blk'=8,'batch'=4] {'blk','batch'}, use_global_device_ids=true, to_apply=%region_26.27 | all-reduce | flops 5888 | bytes 47104 | tf_op jit(solution)/shard_map/psum | solution.py:199
  651.9 42.0 %all-reduce.20.cloned.1.call-done = (f32[512,128]{1,0:T(8,128)}, f32[128,512]{1,0:T(8,128)}, f32[128,512]{1,0:T(8,128)}) async-done(((f32[512,128]{1,0:T(8,128)}, f32[128,512]{1,0:T(8,128)}, f32[128,512]{1,0:T(8,128)}), (f32[512,128]{1,0:T(8,128)}, f32[128,512]{1,0:T(8,128)}, f32[128,512]{1,0:T(8,128)})) %all-reduce.20.cloned.1.call-update) | async-done | bytes 786448 | tf_op jit(solution)/shard_map/psum | solution.py:199
  694.0 1.7 copy.101
  695.7 1.7 copy.102
  697.3 1.7 copy.103
  (113 shorter events, 1.1 us)
Async XLA Ops:
  7.2 188.0 %copy-start = (f32[128,512]{1,0:T(8,128)S(1)}, f32[128,512]{1,0:T(8,128)}, u32[]{:S(2)}) copy-start(f32[128,512]{1,0:T(8,128)} %param.39) | copy-start | bytes 786436
  7.2 686.8 %all-reduce.20.cloned.1.call-start = ((), (), s32[]{:S(2)}) async-start(), calls=%async_computation | async-start | bytes 1572864 | tf_op jit(solution)/shard_map/psum | solution.py:199
  9.9 65.6 %copy-start.14 = (s32[16]{0:T(128)S(1)}, s32[16]{0:T(128)}, u32[]{:S(2)}) copy-start(s32[16]{0:T(128)} %param.41) | copy-start | bytes 196
  9.9 65.6 %copy-start.9 = (f32[512]{0:T(512)S(1)}, f32[512]{0:T(512)}, u32[]{:S(2)}) copy-start(f32[512]{0:T(512)} %param.30) | copy-start | bytes 6148
  9.9 65.6 %copy-start.10 = (f32[512]{0:T(512)S(1)}, f32[512]{0:T(512)}, u32[]{:S(2)}) copy-start(f32[512]{0:T(512)} %param.29) | copy-start | bytes 6148
  10.0 65.6 %copy-start.11 = (f32[512]{0:T(512)S(1)}, f32[512]{0:T(512)}, u32[]{:S(2)}) copy-start(f32[512]{0:T(512)} %param.28) | copy-start | bytes 6148
  10.0 65.6 %copy-start.19 = (f32[512]{0:T(512)S(1)}, f32[512]{0:T(512)}, u32[]{:S(2)}) copy-start(f32[512]{0:T(512)} %param.31) | copy-start | bytes 6148
  87.3 5.7 copy-start.1
  93.0 16.2 %copy-start.7 = (f32[128,512]{1,0:T(8,128)S(1)}, f32[128,512]{1,0:T(8,128)}, u32[]{:S(2)}) copy-start(f32[128,512]{1,0:T(8,128)} %param.37) | copy-start | bytes 786436
  93.0 35.5 %collective-permute-start = (f32[16,512,8]{1,2,0:T(8,128)S(1)}, f32[16,512,8]{1,2,0:T(8,128)S(1)}, u32[]{:S(2)}, u32[]{:S(2)}) collective-permute-start(f32[16,512,8]{1,2,0:T(8,128)S(1)} %get-tuple-element.681), channel_id=1, source_target_pairs={{0,4},{4,8},{8,12},{12,16},{16,20},{20,24},{24,28},{1,5},{5,9},{9,... | collective-permute-start | bytes 786440 | tf_op jit(solution)/shard_map/ppermute | solution.py:36
  97.1 31.4 %collective-permute-start.1 = (f32[16,512,8]{1,2,0:T(8,128)S(1)}, f32[16,512,8]{1,2,0:T(8,128)S(1)}, u32[]{:S(2)}, u32[]{:S(2)}) collective-permute-start(f32[16,512,8]{1,2,0:T(8,128)S(1)} %get-tuple-element.682), channel_id=1, source_target_pairs={{4,0},{8,4},{12,8},{16,12},{20,16},{24,20},{28,24},{5,1},{9,5},{13... | collective-permute-start | bytes 786440 | tf_op jit(solution)/shard_map/ppermute | solution.py:39
  109.2 17.3 %copy-start.2 = (f32[16,128,512]{1,2,0:T(8,128)S(1)}, f32[16,128,512]{1,2,0:T(8,128)}, u32[]{:S(2)}) copy-start(f32[16,128,512]{1,2,0:T(8,128)} %copy.37) | copy-start | bytes 12582916
  109.2 17.3 %copy-start.4 = (f32[16,128,512]{1,2,0:T(8,128)S(1)}, f32[16,128,512]{1,2,0:T(8,128)}, u32[]{:S(2)}) copy-start(f32[16,128,512]{1,2,0:T(8,128)} %copy.38) | copy-start | bytes 12582916
  109.2 19.3 %copy-start.16 = (f32[512,3]{0,1:T(4,128)S(1)}, f32[512,3]{0,1:T(4,128)}, u32[]{:S(2)}) copy-start(f32[512,3]{0,1:T(4,128)} %param.32) | copy-start | bytes 18436
  109.2 19.3 %copy-start.12 = (f32[512]{0:T(512)S(1)}, f32[512]{0:T(512)}, u32[]{:S(2)}) copy-start(f32[512]{0:T(512)} %param.33) | copy-start | bytes 6148
  109.3 19.3 %copy-start.15 = (f32[512]{0:T(512)S(1)}, f32[512]{0:T(512)}, u32[]{:S(2)}) copy-start(f32[512]{0:T(512)} %param.34) | copy-start | bytes 6148
  128.6 66.7 %copy-start.13 = (f32[512]{0:T(512)S(1)}, f32[512]{0:T(512)}, u32[]{:S(2)}) copy-start(f32[512]{0:T(512)} %param.35) | copy-start | bytes 6148
  195.2 64.1 %copy-start.17 = (f32[512]{0:T(512)S(1)}, f32[512]{0:T(512)}, u32[]{:S(2)}) copy-start(f32[512]{0:T(512)} %param.36) | copy-start | bytes 6148
  292.6 19.2 %copy-start.5 = (f32[16,128,512]{1,2,0:T(8,128)S(1)}, f32[16,128,512]{1,2,0:T(8,128)}, u32[]{:S(2)}) copy-start(f32[16,128,512]{1,2,0:T(8,128)} %copy.38) | copy-start | bytes 12582916
  329.7 40.7 %copy-start.22 = (f32[128]{0:T(128)S(1)}, f32[128]{0:T(128)}, u32[]{:S(2)}) copy-start(f32[128]{0:T(128)} %param.38) | copy-start | bytes 1540
  363.5 25.6 %copy-start.18 = (f32[128]{0:T(128)S(1)}, f32[128]{0:T(128)}, u32[]{:S(2)}) copy-start(f32[128]{0:T(128)} %param.40) | copy-start | bytes 1540
  364.6 59.2 %collective-permute-start.2 = (f32[16,512,8]{1,2,0:T(8,128)S(1)}, f32[16,512,8]{1,2,0:T(8,128)S(1)}, u32[]{:S(2)}, u32[]{:S(2)}) collective-permute-start(f32[16,512,8]{1,2,0:T(8,128)S(1)} %get-tuple-element.679), channel_id=1, source_target_pairs={{4,0},{8,4},{12,8},{16,12},{20,16},{24,20},{28,24},{5,1},{9,5},{13... | collective-permute-start | bytes 786440 | tf_op jit(solution)/shard_map/ppermute | solution.py:39
  365.9 57.9 %collective-permute-start.3 = (f32[16,512,8]{1,2,0:T(8,128)S(1)}, f32[16,512,8]{1,2,0:T(8,128)S(1)}, u32[]{:S(2)}, u32[]{:S(2)}) collective-permute-start(f32[16,512,8]{1,2,0:T(8,128)S(1)} %get-tuple-element.680), channel_id=1, source_target_pairs={{0,4},{4,8},{8,12},{12,16},{16,20},{20,24},{24,28},{1,5},{5,9},{9,... | collective-permute-start | bytes 786440 | tf_op jit(solution)/shard_map/ppermute | solution.py:36
  502.9 31.4 %copy-start.6 = (f32[16,128,512]{2,1,0:T(8,128)S(1)}, f32[16,128,512]{2,1,0:T(8,128)}, u32[]{:S(2)}) copy-start(f32[16,128,512]{2,1,0:T(8,128)} %param.26) | copy-start | bytes 12582916
  564.9 25.2 %copy-start.3 = (f32[16,128,512]{1,2,0:T(8,128)S(1)}, f32[16,128,512]{1,2,0:T(8,128)}, u32[]{:S(2)}) copy-start(f32[16,128,512]{1,2,0:T(8,128)} %copy.37) | copy-start | bytes 12582916
  564.9 25.2 %copy-start.8 = (f32[512,128]{1,0:T(8,128)S(1)}, f32[512,128]{1,0:T(8,128)}, u32[]{:S(2)}) copy-start(f32[512,128]{1,0:T(8,128)} %param.27) | copy-start | bytes 786436
  590.1 22.8 %copy-start.20 = (f32[128]{0:T(128)S(1)}, f32[128]{0:T(128)}, u32[]{:S(2)}) copy-start(f32[128]{0:T(128)} %get-tuple-element.582) | copy-start | bytes 1540
  590.1 22.8 %copy-start.21 = (f32[128]{0:T(128)S(1)}, f32[128]{0:T(128)}, u32[]{:S(2)}) copy-start(f32[128]{0:T(128)} %get-tuple-element.583) | copy-start | bytes 1540
Sparse Core Ops, SparseCore 0:
  565.0 128.9 all-reduce.19
where the time goes:
time: 713 us; the launch traced here: 706 us
  other arithmetic  210 us (29%)
  blocking collectives  190 us (27%)
  matrix products  189 us (27%)
  local copies, waits for them, and re-layouts  47.4 us (7%)
  waiting for transfers between devices  42.1 us (6%)
  between operations  15.4 us (2%)
  starting transfers between devices  11.4 us (2%)
    unnamed x4, blocking collectives  82 us
    psum x4, blocking collectives, spread(): return lax.psum(kept, axis)  68.7 us
    unnamed x72, local copies, waits for them, and re-layouts  45.7 us
    psum x1, waiting for transfers between devices, local(): lax.psum((grads[0], grads[1], grads[2], grads[3], grads[4], grads[5], gra...  42 us
    psum x1, blocking collectives, local(): lax.psum((grads[0], grads[1], grads[2], grads[3], grads[4], grads[5], gra...  39.1 us
    reduce_sum x1, other arithmetic, local(): jnp.sum(grad_depthwise_output * before, axis=(0, 2))  33.8 us
    reduce_sum x1, other arithmetic, local(): grad_gain_mid = jnp.sum(dhid * normal_two, axis=(0, 2))  33.3 us
    reduce_sum x1, other arithmetic, local(): grad_bias_in = jnp.sum(dupper, axis=(0, 2))  31.4 us
  transfers between devices with their start and end apart: 5, of which 1 were waited for; matrix products, arithmetic and copies ran while one was open for 19% of the time, Pallas kernels for 0%

commit v1 on v0

v1 whole, which is shorter than its diff:
```python
import functools

import jax
import jax.numpy as jnp
from jax import lax
from jax.experimental import pallas as pl
from jax.experimental.pallas import tpu as pltpu
from jax.sharding import PartitionSpec as P

STEP = 8
HALO = 2 * STEP
EPS = 1e-05
LANE = 128
ROWS = 64
SECOND_ROWS = 128
THIRD_ROWS = 64
PIECE = 256
F32 = jnp.float32
BF16 = jnp.bfloat16
VMEM_LIMIT = 60 * 1024 * 1024


def split(value):
    high = value.astype(BF16)
    low = (value - high.astype(F32)).astype(BF16)
    return high, low


def product(left, right):
    return jnp.dot(left, right, preferred_element_type=F32)


def product_nt(left, right):
    return lax.dot_general(left, right, (((1,), (1,)), ((), ())), preferred_element_type=F32)


def tile(row):
    return jnp.broadcast_to(row, (8, LANE))


def load(ref, base, rows, lanes):
    return ref[pl.ds(base, rows), lanes].reshape(rows // 8, 8, LANE)


def frame_of(base, rows):
    shape = (rows // 8, 8, LANE)
    return lax.broadcasted_iota(jnp.int32, shape, 0) * 8 + lax.broadcasted_iota(jnp.int32, shape, 1) + base


def half_slopes(row):
    return tile(0.5 - 0.5 * row), tile(0.5 + 0.5 * row)


def act_half(half, c0, c1):
    return half * (c1 + c0 * jnp.tanh(half))


def act_parts(half, c0, c1):
    th = jnp.tanh(half)
    rest = half - half * th
    cut = c0 * rest
    return half - cut, (c1 + cut) + (c0 + cut) * th, rest


def total(value):
    return jnp.sum(jnp.sum(value, axis=0, keepdims=True), axis=1, keepdims=True)


def place(values):
    lane = lax.broadcasted_iota(jnp.int32, (1, LANE), 1)
    row = jnp.zeros((1, LANE), F32)
    for position, value in enumerate(values):
        row = jnp.where(lane == position, value, row)
    return row


def lane_tiles(width):
    return [slice(start, start + LANE) for start in range(0, width, LANE)]


def first_kernel(
    ends_ref, x_ref, w_in_ref, bias_ref, slope_ref, w_res_ref, w_skip_ref, gain_ref,
    half_ref, sums_ref, left_ref, right_ref, w_cat_ref, w_out_ref,
):
    group, cin, frames = x_ref.shape
    width = w_in_ref.shape[0]

    @pl.when(pl.program_id(0) == 0)
    def _():
        high, low = split(0.5 * w_in_ref[...].T)
        w_cat_ref[0:cin] = high
        w_cat_ref[cin : 2 * cin] = high
        w_cat_ref[2 * cin : 3 * cin] = low
        for number, ref in enumerate((w_res_ref, w_skip_ref)):
            high, low = split(ref[...] * gain_ref[...])
            start = number * cin
            w_out_ref[start : start + cin] = high
            w_out_ref[2 * cin + start : 3 * cin + start] = high
            w_out_ref[4 * cin + start : 5 * cin + start] = low

    step = min(PIECE, frames)
    for number in range(group):
        item = pl.program_id(0) * group + number
        end = ends_ref[item]
        first = second = jnp.zeros((8, LANE), F32)
        for start in range(0, frames, step):
            xt = x_ref[number, :, start : start + step].T
            if start == 0:
                left_ref[number] = xt[0:HALO]
            if start + step == frames:
                right_ref[number] = xt[step - HALO : step]
            high, low = split(xt)
            half = product(jnp.concatenate([high, low, high], axis=1), w_cat_ref[...]) + 0.5 * bias_ref[...]
            half_ref[number, start : start + step] = half
            valid = frame_of(start, step) < end
            for lanes in lane_tiles(width):
                c0, c1 = half_slopes(slope_ref[0:1, lanes])
                value = act_half(half[:, lanes].reshape(step // 8, 8, LANE), c0, c1)
                value = jnp.where(valid, value, 0.0)
                first = first + jnp.sum(value, axis=0)
                second = second + jnp.sum(value * value, axis=0)
        row = place((total(first), total(second)))
        for block in range(sums_ref.shape[0]):
            sums_ref[block, pl.ds(item, 1), :] = row


def at(base):
    return base if isinstance(base, int) else pl.multiple_of(base, 8)


def sweep(frames, rows, end, body, init, rest=None):
    if end is None:
        carry = init
        for base in range(0, frames, rows):
            carry = body(base, False, carry)
        return carry
    live = jnp.clip(end, 0, frames)
    full, some = lax.div(live, rows), lax.div(live + (rows - 1), rows)
    carry = lax.fori_loop(0, full, lambda n, c: body(pl.multiple_of(n * rows, rows), False, c), init)
    carry = lax.fori_loop(full, some, lambda n, c: body(pl.multiple_of(n * rows, rows), True, c), carry)
    if rest is not None:

        def clear(n, c):
            rest(pl.multiple_of(n * rows, rows))
            return c

        lax.fori_loop(some, frames // rows, clear, 0)
    return carry


def both_ways(full, run):
    pl.when(full)(lambda: run(True))
    pl.when(jnp.logical_not(full))(lambda: run(False))


def where_valid(valid, value):
    return value if valid is None else jnp.where(valid, value, 0.0)


def counts(ends_ref, origin_ref, items, width):
    row = lax.broadcasted_iota(jnp.int32, (items, 1), 0)
    lengths = jnp.zeros((items, 1), jnp.int32)
    for item in range(items):
        lengths = jnp.where(row == item, ends_ref[item] + origin_ref[0], lengths)
    return lengths.astype(F32) * float(width)


def first_norm(sums_ref, count):
    sums = jnp.sum(sums_ref[...], axis=0)
    mean = 2.0 * sums[:, 0:1] / count
    var = 4.0 * sums[:, 1:2] / count - mean * mean
    return mean, lax.rsqrt(var + EPS)


def second_kernel(
    ends_ref, origin_ref, sums_ref, from_left_ref, from_right_ref, half_ref, res_ref, skip_ref,
    w_cat_ref, w_out_ref, bias_ref, slope_ref, gain_ref, shift_ref, taps_ref, tap_bias_ref, slope_mid_ref,
    mid_ref, back_ref, left_ref, right_ref, out_ref,
    halo_ref, normal_ref, coef_ref,
):
    item = pl.program_id(0)
    items = out_ref.shape[1]
    cin, frames = res_ref.shape[1:]
    width = w_cat_ref.shape[1]
    end, origin = ends_ref[item], origin_ref[0]

    @pl.when(item == 0)
    def _():
        mean, scale = first_norm(sums_ref, counts(ends_ref, origin_ref, items, width))
        coef_ref[0] = jnp.broadcast_to(scale, (items, LANE))
        coef_ref[1] = jnp.broadcast_to(scale * mean, (items, LANE))
        for side, ref in enumerate((from_left_ref, from_right_ref)):
            high, low = split(ref[...].reshape(items * HALO, cin))
            value = product(jnp.concatenate([high, low, high], axis=1), w_cat_ref[...]) + 0.5 * bias_ref[...]
            halo_ref[side] = value.reshape(items, HALO, width)

    def run(full):
        rows = SECOND_ROWS if full and frames % SECOND_ROWS == 0 else ROWS
        d_high, d_low = split(jnp.concatenate([res_ref[0], skip_ref[0]], axis=0))
        high, low = d_high.T, d_low.T
        back_ref[0] = product(jnp.concatenate([high, low, high], axis=1), w_out_ref[...])
        left_ref[0] = back_ref[0, 0:STEP]
        right_ref[0] = back_ref[0, frames - STEP : frames]

        scale, scale_mean = coef_ref[0, pl.ds(item, 1), :], coef_ref[1, pl.ds(item, 1), :]
        window = jnp.clip(end - STEP, 0, frames - HALO)
        window = pl.multiple_of(lax.div(window, 8) * 8, 8)
        tots = [jnp.zeros((8, LANE), F32)] * 10
        for lanes in lane_tiles(width):
            c0, c1 = half_slopes(slope_ref[0:1, lanes])
            gain, shift = gain_ref[0:1, lanes], shift_ref[0:1, lanes]
            factor, offset = tile(2.0 * gain * scale), tile(shift - gain * scale_mean)

            def normed(half, valid):
                return where_valid(valid, factor * act_half(half, c0, c1) + offset)

            def store(base, count, value):
                normal_ref[pl.ds(base, count), lanes] = value.reshape(count, LANE)

            frame = frame_of(-HALO, HALO)
            store(0, HALO, normed(halo_ref[0, item, :, lanes].reshape(2, 8, LANE), (frame < end) & (frame >= -origin)))
            frame = frame_of(frames, HALO)
            store(HALO + frames, HALO, normed(halo_ref[1, item, :, lanes].reshape(2, 8, LANE), frame < end))

            def fill(base, masked, carry):
                valid = frame_of(base, rows) < end if masked else None
                store(at(base + HALO), rows, normed(load(half_ref.at[0], base, rows, lanes), valid))
                return carry

            def clear(base):
                normal_ref[pl.ds(at(base + HALO), rows), lanes] = jnp.zeros((rows, LANE), F32)

            sweep(frames, rows, None if full else end, fill, 0, clear)

            taps = [tile(0.5 * taps_ref[tap : tap + 1, lanes]) for tap in range(3)]
            tap_bias = tile(0.5 * tap_bias_ref[0:1, lanes])
            m0, m1 = half_slopes(slope_mid_ref[0:1, lanes])

            def conv(base, count):
                value = taps[0] * load(normal_ref, base, count, lanes)
                value = value + taps[1] * load(normal_ref, at(base + STEP), count, lanes)
                value = value + taps[2] * load(normal_ref, at(base + HALO), count, lanes) + tap_bias
                mid_ref[0, pl.ds(base, count), lanes] = value.reshape(count, LANE)
                return value

            conv(0, STEP)
            conv(frames + STEP, STEP)

            def gather(base, masked, carry):
                valid = frame_of(base, rows) < end if masked else None
                mid = conv(at(base + STEP), rows)
                act, grad, _ = act_parts(mid, m0, m1)
                back = where_valid(valid, load(back_ref.at[0], base, rows, lanes))
                act, grad = where_valid(valid, act), where_valid(valid, grad)
                ex, ez = grad * back, grad * act
                terms = (act, act * act, back, back * act, ex, grad, ez, ex * mid, grad * mid, ez * mid)
                return tuple(old + jnp.sum(new, axis=0) for old, new in zip(carry, terms))

            sums = sweep(frames, rows, None if full else end, gather, (jnp.zeros((8, LANE), F32),) * 10)

            def edge_sums(base, mask):
                mid = load(mid_ref.at[0], at(base + STEP), HALO, lanes)
                act, grad, _ = act_parts(mid, m0, m1)
                back = load(back_ref.at[0], base, HALO, lanes)
                return [jnp.sum(jnp.where(mask, term, 0.0), axis=0) for term in (grad * back, grad, grad * act)]

            frame = frame_of(0, HALO)
            low_sums = edge_sums(0, (frame < end) & (frame + origin < STEP))
            frame = frame_of(window, HALO)
            high_sums = edge_sums(window, (frame < end) & (frame >= end - STEP))
            w0, w1, w2 = (tile(taps_ref[tap : tap + 1, lanes]) for tap in range(3))
            for term in range(4):
                tots[term] = tots[term] + sums[term]
            for term in range(3):
                plain = sums[4 + term]
                edged = (w0 + w1 + w2) * plain - w0 * low_sums[term] - w2 * high_sums[term]
                tots[4 + term] = tots[4 + term] + gain * edged
                tots[7 + term] = (
                    tots[7 + term] + 2.0 * sums[7 + term] - tap_bias_ref[0:1, lanes] * plain - shift * edged
                )
        row = place([total(value) for value in tots])
        for block in range(out_ref.shape[0]):
            out_ref[block, pl.ds(item, 1), :] = row

    both_ways(end >= frames, run)


GRAD_ROWS = 16


def second_norm(mids_ref, count):
    mids = jnp.sum(mids_ref[...], axis=0)
    m = [mids[:, term : term + 1] for term in range(10)]
    mean = 2.0 * m[0] / count
    return m, mean, lax.rsqrt(4.0 * m[1] / count - mean * mean + EPS)


def flatten(flat_ref, grads_ref, half):
    height, width = grads_ref.shape
    tiles = lane_tiles(width)
    count = len(tiles) // 2
    for number, lanes in enumerate(tiles[half * count : (half + 1) * count]):
        flat_ref[number * height : (number + 1) * height] = grads_ref[:, lanes]
    used = height * count
    if used < flat_ref.shape[0]:
        flat_ref[used:] = jnp.zeros((flat_ref.shape[0] - used, LANE), F32)


def third_kernel(
    ends_ref, origin_ref, core_ref, sums_ref, mids_ref, x_ref, res_ref, skip_ref, half_ref, mid_ref, back_ref,
    from_left_ref, from_right_ref,
    slope_ref, gain_ref, shift_ref, taps_ref, slope_mid_ref,
    u_high_ref, u_low_ref, keep_ref, send_ref,
    grad_ref, coef_ref, vector_ref, grads_ref, z_high_ref, z_low_ref, cot_ref,
):
    item = pl.program_id(0)
    items = coef_ref.shape[1]
    cin, frames = x_ref.shape[1:]
    width = half_ref.shape[2]
    end, origin = ends_ref[item], origin_ref[0]

    @pl.when(item == 0)
    def _():
        count = counts(ends_ref, origin_ref, items, width)
        mean1, scale1 = first_norm(sums_ref, count)
        m, mean2, scale2 = second_norm(mids_ref, count)
        beta = scale2 * scale2 * (2.0 * m[3] - mean2 * m[2]) / count
        alpha = m[2] / count - mean2 * beta
        mean_a = scale2 * (m[4] - alpha * m[5] - 2.0 * beta * m[6]) / count
        mean_b = scale2 * (m[7] - alpha * m[8] - 2.0 * beta * m[9]) / count
        values = (
            scale1, scale1 * mean1, scale1 * (mean_a - mean1 * scale1 * mean_b), 2.0 * scale1 * scale1 * mean_b,
            scale2, scale2 * alpha, 2.0 * scale2 * beta, 2.0 * scale2, scale2 * mean2,
        )
        for number, value in enumerate(values):
            coef_ref[number] = jnp.broadcast_to(value, (items, LANE))
        vector_ref[...] = jnp.zeros(vector_ref.shape, F32)
        grads_ref[...] = jnp.zeros(grads_ref.shape, F32)
        cot_ref[...] = jnp.zeros(cot_ref.shape, F32)

    def run(full):
        rows = THIRD_ROWS if full else ROWS
        coefs = [tile(coef_ref[number, pl.ds(item, 1), :]) for number in range(9)]
        scale1, scale_mean1, dp_a, dp_b, dr_0, dr_a, dr_b, z_0, z_a = coefs
        both = jnp.concatenate([res_ref[0], skip_ref[0]], axis=0)
        d_high, d_low = split(both)
        lane = lax.broadcasted_iota(jnp.int32, (1, LANE), 1)
        cots = cot_ref[...]
        for lanes in lane_tiles(frames):
            piece = both[:, lanes]
            cots = cots + (piece if full else jnp.where(lane + lanes.start < end, piece, 0.0))
        cot_ref[...] = cots

        for lanes in lane_tiles(width):
            m0, m1 = half_slopes(slope_mid_ref[0:1, lanes])

            def middle(base, count, valid, back):
                act, slope, rest = act_parts(load(mid_ref.at[0], base, count, lanes), m0, m1)
                grad = (dr_0 * back - dr_a) - dr_b * act
                grad = where_valid(valid, grad)
                grad_ref[pl.ds(base, count), lanes] = (grad * slope).reshape(count, LANE)
                return act, grad * rest

            frame = frame_of(-STEP, STEP)
            middle(0, STEP, (frame < end) & (frame >= -origin), from_left_ref[0:1, :, lanes])
            middle(frames + STEP, STEP, frame_of(frames, STEP) < end, from_right_ref[0:1, :, lanes])

            def inner(base, masked, carry):
                valid = frame_of(base, rows) < end if masked else None
                act, term = middle(at(base + STEP), rows, valid, load(back_ref.at[0], base, rows, lanes))
                high, low = split(where_valid(valid, z_0 * act - z_a).reshape(rows, LANE))
                z_high_ref[pl.ds(base, rows), lanes] = high
                z_low_ref[pl.ds(base, rows), lanes] = low
                return carry + jnp.sum(term, axis=0)

            def inner_clear(base):
                grad_ref[pl.ds(at(base + STEP), rows), lanes] = jnp.zeros((rows, LANE), F32)
                z_high_ref[pl.ds(base, rows), lanes] = jnp.zeros((rows, LANE), BF16)
                z_low_ref[pl.ds(base, rows), lanes] = jnp.zeros((rows, LANE), BF16)

            vector_ref[8, :, lanes] += sweep(
                frames, rows, None if full else end, inner, jnp.zeros((8, LANE), F32), inner_clear
            )

            c0, c1 = half_slopes(slope_ref[0:1, lanes])
            gain, shift = gain_ref[0:1, lanes], shift_ref[0:1, lanes]
            taps = [tile(taps_ref[tap : tap + 1, lanes]) for tap in range(3)]
            outer = gain * scale1

            def body(base, masked, carry):
                valid = frame_of(base, rows) < end if masked else None
                ahead = load(grad_ref, at(base + HALO), rows, lanes)
                here = load(grad_ref, at(base + STEP), rows, lanes)
                behind = where_valid(valid, load(grad_ref, base, rows, lanes))
                act, slope, rest = act_parts(load(half_ref.at[0], base, rows, lanes), c0, c1)
                dn = taps[0] * ahead + taps[1] * here + taps[2] * behind
                dp = where_valid(valid, (outer * dn - dp_a) - dp_b * act)
                du = dp * slope
                high, low = split(du.reshape(rows, LANE))
                u_high_ref[0, pl.ds(base, rows), lanes] = high
                u_low_ref[0, pl.ds(base, rows), lanes] = low
                terms = (du, dp * rest, here, ahead * act, here * act, behind * act)
                return tuple(old + jnp.sum(new, axis=0) for old, new in zip(carry, terms))

            def clear(base):
                u_high_ref[0, pl.ds(base, rows), lanes] = jnp.zeros((rows, LANE), BF16)
                u_low_ref[0, pl.ds(base, rows), lanes] = jnp.zeros((rows, LANE), BF16)

            sums = sweep(frames, rows, None if full else end, body, (jnp.zeros((8, LANE), F32),) * 6, clear)
            window = pl.multiple_of(lax.div(jnp.clip(end, 0, frames - HALO), 8) * 8, 8)
            row = frame_of(window, HALO)
            inside = jnp.where((row >= end) & (row < end + STEP), load(grad_ref, window, HALO, lanes), 0.0)
            plains = (
                sums[2] - grad_ref[STEP:HALO, lanes] + grad_ref[frames + STEP : frames + HALO, lanes],
                sums[2],
                sums[2] - grad_ref[frames : frames + STEP, lanes] + grad_ref[0:STEP, lanes] - jnp.sum(inside, axis=0),
            )
            factor, offset = 2.0 * outer, shift - gain * scale_mean1
            vector_ref[0, :, lanes] += sums[0]
            vector_ref[1, :, lanes] += sums[1]
            gain_sum = shift_sum = jnp.zeros((8, LANE), F32)
            for tap in range(3):
                plain, times = plains[tap], sums[3 + tap]
                vector_ref[4 + tap, :, lanes] += factor * times + offset * plain
                gain_sum = gain_sum + taps[tap] * (2.0 * scale1 * times - scale_mean1 * plain)
                shift_sum = shift_sum + taps[tap] * plain
            vector_ref[2, :, lanes] += gain_sum
            vector_ref[3, :, lanes] += shift_sum
            vector_ref[7, :, lanes] += sums[2]

        z_high, z_low = z_high_ref[...], z_low_ref[...]
        grads_ref[0 : 2 * cin] += product(
            jnp.concatenate([d_high, d_low, d_high], axis=1), jnp.concatenate([z_high, z_high, z_low], axis=0)
        )
        u_high, u_low = u_high_ref[0], u_low_ref[0]
        x_high, x_low = split(x_ref[0])
        grads_ref[2 * cin : 3 * cin] += product(
            jnp.concatenate([x_high, x_low, x_high], axis=1), jnp.concatenate([u_high, u_high, u_low], axis=0)
        )

    both_ways(end >= frames, run)

    @pl.when(item == items - 1)
    def _():
        base = 3 * cin
        for row in range(9):
            grads_ref[base + row : base + row + 1] = jnp.sum(vector_ref[row], axis=0, keepdims=True)
        column = jnp.broadcast_to(jnp.sum(cot_ref[...], axis=1, keepdims=True), cot_ref.shape).T[0:1]
        grads_ref[base + 9 : base + 10] = jnp.zeros((1, width), F32)
        for number in range(2 * cin // LANE):
            grads_ref[base + 9 + number : base + 10 + number, 0:LANE] = column[:, number * LANE : (number + 1) * LANE]
            grads_ref[base + 9 + number : base + 10 + number, width // 2 : width // 2 + LANE] = column[
                :, number * LANE : (number + 1) * LANE
            ]
        for core in range(2):

            @pl.when(core_ref[0] == core)
            def _():
                flatten(keep_ref, grads_ref, core)
                flatten(send_ref, grads_ref, 1 - core)


def outer_kernel(
    ends_ref, origin_ref, mids_ref, x_ref, mid_ref, w_out_ref, w_res_ref, w_skip_ref, gain_ref, shift_ref, slope_ref,
    bias_res_ref, bias_skip_ref, res_out_ref, skip_out_ref, coef_ref, column_ref, wide_ref, turned_ref,
):
    items = coef_ref.shape[1]
    group, cin, frames = x_ref.shape
    width = w_out_ref.shape[1]

    @pl.when(pl.program_id(0) == 0)
    def _():
        _, mean, scale = second_norm(mids_ref, counts(ends_ref, origin_ref, items, width))
        high, low = w_out_ref[0 : 2 * cin].T, w_out_ref[4 * cin : 6 * cin].T
        turned_ref[0:width] = high
        turned_ref[width : 2 * width] = high
        turned_ref[2 * width : 3 * width] = low
        coef_ref[0] = jnp.broadcast_to(2.0 * scale, (items, LANE))
        coef_ref[1] = jnp.broadcast_to(scale * mean, (items, LANE))
        for number, (w_ref, b_ref) in enumerate(((w_res_ref, bias_res_ref), (w_skip_ref, bias_skip_ref))):
            rows = slice(number * cin, (number + 1) * cin)
            column_ref[0, rows] = jnp.broadcast_to(b_ref[...], (LANE, cin)).T
            for place_of, vector_of in ((1, shift_ref), (2, gain_ref)):
                value = jnp.sum(w_ref[...] * vector_of[...], axis=1, keepdims=True)
                column_ref[place_of, rows] = jnp.broadcast_to(value, (cin, LANE))

    lane = lax.broadcasted_iota(jnp.int32, (1, LANE), 1)
    for number in range(group):
        item = pl.program_id(0) * group + number
        end = ends_ref[item]
        z_0, z_a = coef_ref[0, pl.ds(item, 1), :], coef_ref[1, pl.ds(item, 1), :]
        for lanes in lane_tiles(width):
            m0, m1 = half_slopes(slope_ref[0:1, lanes])
            for base in range(0, frames, ROWS):
                act = act_half(load(mid_ref.at[number], base + STEP, ROWS, lanes), m0, m1)
                act = jnp.where(frame_of(base, ROWS) < end, act, 0.0)
                high, low = split(act.reshape(ROWS, LANE))
                spot = number % 2
                wide_ref[spot, base : base + ROWS, lanes] = high
                wide_ref[spot, base : base + ROWS, width + lanes.start : width + lanes.stop] = low
        r_high, r_low = wide_ref[spot, :, 0:width], wide_ref[spot, :, width:]
        out = product(jnp.concatenate([r_high, r_low, r_high], axis=1), turned_ref[...]).T
        inside = column_ref[1] - z_a * column_ref[2]
        for lanes in lane_tiles(frames):
            wide = column_ref[0] + jnp.where(lane + lanes.start < end, inside, 0.0) + z_0 * out[:, lanes]
            res_out_ref[number, :, lanes] = wide[0:cin] + x_ref[number, :, lanes]
            skip_out_ref[number, :, lanes] = wide[cin : 2 * cin]


def inner_kernel(ends_ref, res_ref, u_high_ref, u_low_ref, w_cat_ref, x_grad_ref, turned_ref):
    group, cin, frames = res_ref.shape

    @pl.when(pl.program_id(0) == 0)
    def _():
        turned_ref[:, 0:cin] = w_cat_ref[0:cin].T
        turned_ref[:, cin : 2 * cin] = w_cat_ref[2 * cin : 3 * cin].T

    lane = lax.broadcasted_iota(jnp.int32, (1, LANE), 1)
    for number in range(group):
        end = ends_ref[pl.program_id(0) * group + number]
        pair = product(u_high_ref[number], turned_ref[...])
        x_grad = (pair[:, 0:cin] + pair[:, cin : 2 * cin] + product(u_low_ref[number], turned_ref[:, 0:cin])).T
        for lanes in lane_tiles(frames):
            valid = lane + lanes.start < end
            x_grad_ref[number, :, lanes] = jnp.where(valid, res_ref[number, :, lanes], 0.0) + 2.0 * x_grad[:, lanes]


def last_kernel(
    core_ref, mine_ref, theirs_ref, w_res_ref, w_skip_ref, gain_ref, shift_ref,
    w_in_out, bias_in_out, slope_in_out, gain_in_out, shift_in_out, taps_out, tap_bias_out, slope_mid_out,
    gain_mid_out, shift_mid_out, w_res_out, bias_res_out, w_skip_out, bias_skip_out,
):
    cin, width = w_res_ref.shape
    height = 3 * cin + GRAD_ROWS
    base = 3 * cin
    vectors = ((0, bias_in_out), (1, slope_in_out), (2, gain_in_out), (3, shift_in_out), (7, tap_bias_out), (8, slope_mid_out))
    groups = ((w_res_ref, w_res_out), (w_skip_ref, w_skip_out))
    columns = []
    for number, bias_out in enumerate((bias_res_out, bias_skip_out)):
        row = mine_ref[base + 9 + number : base + 10 + number]
        bias_out[...] = row
        columns.append(jnp.broadcast_to(row, (cin, cin)).T[:, 0:1])
    tiles = lane_tiles(width)
    count = len(tiles) // 2

    def place_half(ref, half):
        for number, lanes in enumerate(tiles[half * count : (half + 1) * count]):
            grads = ref.at[number * height : (number + 1) * height]
            w_in_out[lanes] = grads[2 * cin : 3 * cin].T
            for row, out in vectors:
                out[:, lanes] = grads[base + row : base + row + 1]
            taps_out[:, lanes] = grads[base + 4 : base + 7]
            gain_sum = shift_sum = jnp.zeros((1, LANE), F32)
            for group, (w_ref, w_out) in enumerate(groups):
                products = grads[group * cin : (group + 1) * cin]
                column = columns[group]
                w_out[:, lanes] = gain_ref[:, lanes] * products + shift_ref[:, lanes] * column
                gain_sum = gain_sum + jnp.sum(w_ref[:, lanes] * products, axis=0, keepdims=True)
                shift_sum = shift_sum + jnp.sum(w_ref[:, lanes] * column, axis=0, keepdims=True)
            gain_mid_out[:, lanes] = gain_sum
            shift_mid_out[:, lanes] = shift_sum

    for core in range(2):

        @pl.when(core_ref[0] == core)
        def _():
            place_half(mine_ref, core)
            place_half(theirs_ref, 1 - core)


def whole(array, space=pltpu.VMEM):
    if space is pltpu.SMEM:
        return pl.BlockSpec(memory_space=pltpu.SMEM)
    return pl.BlockSpec(array.shape, lambda item: (0,) * len(array.shape))


def per_item(array, group=1, offset=0):
    return pl.BlockSpec((group,) + array.shape[1:], lambda item: (item + offset, 0, 0))


def sds(*shape, dtype=F32):
    return jax.ShapeDtypeStruct(shape, dtype)


def cost(flops, size):
    return pl.CostEstimate(flops=flops, bytes_accessed=size, transcendentals=0)


def params():
    return pltpu.CompilerParams(dimension_semantics=("arbitrary",), vmem_limit_bytes=VMEM_LIMIT)


def exchange(pieces, axes):
    return lax.all_to_all(pieces, axes, 0, 0)


def local(
    inputs, weight_in, bias_in, slope_in, gain_in, shift_in, depthwise_weight, depthwise_bias, slope_mid, gain_mid,
    shift_mid, weight_res, bias_res, weight_skip, bias_skip, lengths, cot_res, cot_skip,
):
    items, cin, frames = inputs.shape
    width = weight_in.shape[0]
    blocks = lax.axis_size("blk")
    origin = (lax.axis_index("blk") * frames).astype(jnp.int32).reshape(1)
    core = lax.axis_index("core").astype(jnp.int32).reshape(1)
    ends = lengths - origin[0]
    bias_in, slope_in, gain_in, shift_in, tap_bias, slope_mid, gain_mid, shift_mid, bias_res, bias_skip = (
        vector.reshape(1, -1)
        for vector in (
            bias_in, slope_in, gain_in, shift_in, depthwise_bias, slope_mid, gain_mid, shift_mid, bias_res, bias_skip
        )
    )
    taps = depthwise_weight.T
    ends_spec = whole(ends, pltpu.SMEM)

    half = sds(items, frames, width)
    halo = sds(items, HALO, cin)
    sums = sds(blocks, items, LANE)
    w_cat, w_out = sds(3 * cin, width, dtype=BF16), sds(6 * cin, width, dtype=BF16)
    weights = (weight_in, bias_in, slope_in, weight_res, weight_skip, gain_mid)
    pair = 2 if items % 2 == 0 else 1
    quad = 4 if items % 4 == 0 else 1
    half, first_sums, to_left, to_right, w_cat, w_out = pl.pallas_call(
        first_kernel,
        grid=(items // pair,),
        in_specs=[ends_spec, per_item(inputs, pair)] + [whole(array) for array in weights],
        out_specs=[per_item(half, pair), whole(sums), per_item(halo, pair), per_item(halo, pair), whole(w_cat), whole(w_out)],
        out_shape=[half, sums, halo, halo, w_cat, w_out],
        compiler_params=params(),
    )(ends, inputs, *weights)

    forward = [(block, block + 1) for block in range(blocks - 1)]
    backward = [(target, source) for source, target in forward]
    first_sums = exchange(first_sums, "blk")
    from_left = lax.ppermute(to_right, "blk", forward)
    from_right = lax.ppermute(to_left, "blk", backward)

    mid, edge = sds(items, frames + HALO, width), sds(items, STEP, width)
    small = (first_sums, from_left, from_right)
    weights = (w_cat, w_out, bias_in, slope_in, gain_in, shift_in, taps, tap_bias, slope_mid)
    rounded = sds(items, frames, width, dtype=BF16)
    mid, back, to_left, to_right, mid_sums = pl.pallas_call(
        second_kernel,
        grid=(items,),
        in_specs=[ends_spec, ends_spec]
        + [whole(array) for array in small]
        + [per_item(half), per_item(cot_res), per_item(cot_skip)]
        + [whole(array) for array in weights],
        out_specs=[per_item(mid), per_item(half), per_item(edge), per_item(edge), whole(sums)],
        out_shape=[mid, sds(*half.shape), edge, edge, sums],
        scratch_shapes=[
            pltpu.VMEM((2, items, HALO, width), F32),
            pltpu.VMEM((frames + 2 * HALO, width), F32),
            pltpu.VMEM((2, items, LANE), F32),
        ],
        compiler_params=params(),
    )(ends, origin, *small, half, cot_res, cot_skip, *weights)
    from_left = lax.ppermute(to_right, "blk", forward)
    from_right = lax.ppermute(to_left, "blk", backward)
    mid_sums = exchange(mid_sums, "blk")

    small = (first_sums, mid_sums)
    large = (inputs, cot_res, cot_skip, half, mid, back, from_left, from_right)
    weights = (slope_in, gain_in, shift_in, taps, slope_mid)
    height = 3 * cin + GRAD_ROWS
    chips = blocks * lax.axis_size("side")
    piece = -(-height * (width // LANE) // (2 * chips * 8)) * 8
    flat = sds(chips * piece, LANE)
    u_high, u_low, keep, send = pl.pallas_call(
        third_kernel,
        grid=(items,),
        in_specs=[ends_spec] * 3
        + [whole(array) for array in small]
        + [per_item(array) for array in large]
        + [whole(array) for array in weights],
        out_specs=[per_item(rounded)] * 2 + [whole(flat)] * 2,
        out_shape=[rounded] * 2 + [flat] * 2,
        scratch_shapes=[
            pltpu.VMEM((frames + HALO, width), F32),
            pltpu.VMEM((9, items, LANE), F32),
            pltpu.VMEM((9, 8, width), F32),
            pltpu.VMEM((height, width), F32),
            pltpu.VMEM((frames, width), BF16),
            pltpu.VMEM((frames, width), BF16),
            pltpu.VMEM((2 * cin, LANE), F32),
        ],
        compiler_params=params(),
        cost_estimate=cost(18 * items * frames * cin * width, items * frames * width * 20),
    )(ends, origin, core, *small, *large, *weights)

    swap = [(0, 1), (1, 0)]
    keep = keep + lax.ppermute(send, "core", swap)
    keep, mid = lax.optimization_barrier((keep, mid))
    pieces = exchange(keep.reshape(chips, piece, LANE), ("blk", "side"))

    wide = sds(*inputs.shape)
    large = (inputs, mid)
    weights = (w_out, weight_res, weight_skip, gain_mid, shift_mid, slope_mid, bias_res, bias_skip)
    residual_out, skip_out = pl.pallas_call(
        outer_kernel,
        grid=(items // quad,),
        in_specs=[ends_spec] * 2
        + [whole(mid_sums)]
        + [per_item(array, quad) for array in large]
        + [whole(array) for array in weights],
        out_specs=[per_item(wide, quad)] * 2,
        out_shape=[wide] * 2,
        scratch_shapes=[pltpu.VMEM((2, items, LANE), F32), pltpu.VMEM((3, 2 * cin, LANE), F32)]
        + [pltpu.VMEM((2, frames, 2 * width), BF16), pltpu.VMEM((3 * width, 2 * cin), BF16)],
        compiler_params=params(),
        cost_estimate=cost(12 * items * frames * cin * width, items * frames * width * 8),
    )(ends, origin, mid_sums, *large, *weights)
    pieces, residual_out, u_high = lax.optimization_barrier((pieces, residual_out, u_high))
    mine = exchange(jnp.broadcast_to(jnp.sum(pieces, axis=0), pieces.shape), ("blk", "side")).reshape(-1, LANE)
    large = (cot_res, u_high, u_low)
    grad_inputs = pl.pallas_call(
        inner_kernel,
        grid=(items // quad,),
        in_specs=[ends_spec] + [per_item(array, quad) for array in large] + [whole(w_cat)],
        out_specs=per_item(wide, quad),
        out_shape=wide,
        scratch_shapes=[pltpu.VMEM((width, 2 * cin), BF16)],
        compiler_params=params(),
        cost_estimate=cost(6 * items * frames * cin * width, items * frames * width * 6),
    )(ends, *large, w_cat)
    mine, grad_inputs = lax.optimization_barrier((mine, grad_inputs))
    theirs = lax.ppermute(mine, "core", swap)
    vector, short = sds(1, width), sds(1, cin)
    ends_of = (
        sds(width, cin), vector, vector, vector, vector, sds(3, width), vector, vector, vector, vector,
        sds(cin, width), short, sds(cin, width), short,
    )
    tail = pl.pallas_call(
        last_kernel,
        in_specs=[pl.BlockSpec(memory_space=pltpu.SMEM)] + [pl.BlockSpec(memory_space=pltpu.VMEM)] * 6,
        out_shape=ends_of,
    )(core, mine, theirs, weight_res, weight_skip, gain_mid, shift_mid)
    tail = [
        value if number in (0, 10, 12) else value.T if number == 5 else value.reshape(-1)
        for number, value in enumerate(tail)
    ]
    return (residual_out, skip_out, grad_inputs) + tuple(tail)


def solution(mesh):
    devices = mesh.devices
    split_mesh = jax.sharding.Mesh(devices.reshape(devices.shape[0], -1, 2), ("blk", "side", "core"))
    batch = ("side", "core")
    items = P(batch, None, "blk")
    return jax.shard_map(
        local,
        mesh=split_mesh,
        in_specs=(items,) + (P(),) * 14 + (P(batch), items, items),
        out_specs=(items,) * 3 + (P(),) * 14,
        check_vma=False,
    )
```

time: 713 us -> 198 us (0.28)
  other arithmetic: 210 us -> 3.07 us
  matrix products: 189 us -> 0 us
  blocking collectives: 190 us -> 14 us
  Pallas kernels: 0 us -> 138 us
  local copies, waits for them, and re-layouts: 47.4 us -> 3.05 us
  waiting for transfers between devices: 42.1 us -> 12.6 us
  between operations: 15.4 us -> 0.84 us
  starting transfers between devices: 11.4 us -> 25.6 us
    reduce_sum x9 -> x1, other arithmetic: 197 us -> 0.03 us  [local(): jnp.sum(pieces, axis=0)]
    dot_general x9 -> x0, matrix products: 189 us -> none  [the longest x1 30.5 us: local(): grad_weight_in = jnp.einsum('iot,ict->oc', dupper, inputs, precision=hp)]
    pallas_call x0 -> x6, Pallas kernels: none -> 138 us  [the longest x1 51.5 us: local(): pl.pallas_call(third_kernel, grid=(items,), in_specs=[ends_spec] * 3 + [w...]
    psum x5 -> x0, blocking collectives: 108 us -> none  [the longest x4 68.7 us: spread(): return lax.psum(kept, axis)]
    unnamed x4 -> x0, blocking collectives: 82 us -> none
    unnamed x72 -> x14, local copies, waits for them, and re-layouts: 45.7 us -> 2.25 us
    psum x1 -> x0, waiting for transfers between devices: 42 us -> none  [local(): lax.psum((grads[0], grads[1], grads[2], grads[3], grads[4], grads[5], gra...]
    all_to_all x0 -> x3, starting transfers between devices: none -> 15.9 us  [exchange(): return lax.all_to_all(pieces, axes, 0, 0)]
  transfers between devices with their start and end apart: 5 -> 9, of which waited for: 1 -> 4; matrix products, arithmetic and copies ran while one was open for 19% -> 0% of each run, Pallas kernels for 0% -> 16%
where the time goes in v1:
time: 198 us; the launch traced here: 197 us
  Pallas kernels  138 us (70%)
  starting transfers between devices  25.6 us (13%)
  blocking collectives  14 us (7%)
  waiting for transfers between devices  12.6 us (6%)
  other arithmetic  3.07 us (2%)
  local copies, waits for them, and re-layouts  3.05 us (2%)
    pallas_call x1, Pallas kernels, local(): pl.pallas_call(third_kernel, grid=(items,), in_specs=[ends_spec] * 3 + [w...  51.5 us
    pallas_call x1, Pallas kernels, local(): pl.pallas_call(second_kernel, grid=(items,), in_specs=[ends_spec, ends_sp...  39.3 us
    pallas_call x1, Pallas kernels, local(): pl.pallas_call(outer_kernel, grid=(items // quad,), in_specs=[ends_spec]...  19 us
    all_to_all x3, starting transfers between devices, exchange(): return lax.all_to_all(pieces, axes, 0, 0)  15.9 us
    all_to_all x1, blocking collectives, exchange(): return lax.all_to_all(pieces, axes, 0, 0)  14 us
    pallas_call x1, Pallas kernels, local(): pl.pallas_call(first_kernel, grid=(items // pair,), in_specs=[ends_spec,...  13.2 us
    pallas_call x1, Pallas kernels, local(): pl.pallas_call(inner_kernel, grid=(items // quad,), in_specs=[ends_spec]...  12 us
    all_to_all x3, waiting for transfers between devices, exchange(): return lax.all_to_all(pieces, axes, 0, 0)  8.8 us
  transfers between devices with their start and end apart: 9, of which 4 were waited for; matrix products, arithmetic and copies ran while one was open for 0% of the time, Pallas kernels for 16%

profile of v1, /device:TPU:0, one launch (start us, length us, event | category | flops | bytes accessed | tf_op | source)
XLA Modules:
  0.0 196.7 jit_solution(11525881121137354725)
XLA Ops:
  0.7 1.2 broadcast_subtract_fusion.ends_ref
  1.8 13.2 %shard_map.305 = (f32[16,512,512]{2,1,0:T(8,128)}, f32[8,16,128]{2,1,0:T(8,128)}, f32[16,16,128]{2,1,0:T(8,128)}, f32[16,16,128]{2,1,0:T(8,128)}, bf16[384,512]{1,0:T(8,128)(2,1)}, /*index=5*/bf16[768,512]{1,0:T(8,128)(2,1)}) custom-call(s32[16]{0:T(128)} %broadcast_subtract_fusion.ends_ref, f32[16,128,512]{2,1,0:T(8,128)} %x_ref.5, f32[512,128]{1,0:T(8,128)} %w_in_ref.1, ...), custom_call_target="tpu_custom_call" | custom-call | tf_op jit(solution)/shard_map/pallas_call | solution.py:623
  15.0 4.8 %collective-permute-start = (f32[16,16,128]{2,1,0:T(8,128)}, f32[16,16,128]{2,1,0:T(8,128)S(1)}, u32[]{:S(2)}, u32[]{:S(2)}) collective-permute-start(f32[16,16,128]{2,1,0:T(8,128)} %get-tuple-element.56), channel_id=1, source_target_pairs={{0,4},{4,8},{8,12},{12,16},{16,20},{20,24},{24,28},{1,5},{5,9},{9,... | collective-permute-start | bytes 393224 | tf_op jit(solution)/shard_map/ppermute | solution.py:635
  19.9 1.3 collective-permute-start.1
  21.2 14.0 %all_to_all.20.sums_ref = f32[8,16,128]{2,1,0:T(8,128)} all-to-all(f32[8,16,128]{2,1,0:T(8,128)} %get-tuple-element.55), channel_id=1, replica_groups=mesh['blk'=8,'side'=2,'core'=2] {'blk'}, dimensions={0} | all-to-all | bytes 131072 | tf_op jit(solution)/shard_map/all_to_all | solution.py:594
  35.1 0.0 collective-permute-done.from_left_ref
  35.1 0.0 copy-start.5
  35.1 0.0 collective-permute-done.1.from_right_ref
  35.2 0.0 copy-start.6
  35.2 0.6 copy-done.5
  35.8 0.0 copy-done.6
  35.8 39.3 %shard_map.306 = (f32[16,528,512]{2,1,0:T(8,128)}, f32[16,512,512]{2,1,0:T(8,128)}, f32[16,8,512]{2,1,0:T(8,128)}, f32[16,8,512]{2,1,0:T(8,128)}, f32[8,16,128]{2,1,0:T(8,128)}) custom-call(s32[16]{0:T(128)} %broadcast_subtract_fusion.ends_ref, s32[1]{0:T(128)} %bitcast.origin_ref, f32[8,16,128]{2,1,0:T(8,128)} %all_to_all.20.sums_ref, ...), custom_call_target="tpu_custom_call" | custom-call | tf_op jit(solution)/shard_map/pallas_call | solution.py:642
  75.1 2.3 %collective-permute-start.2 = (f32[16,8,512]{2,1,0:T(8,128)}, f32[16,8,512]{2,1,0:T(8,128)S(1)}, u32[]{:S(2)}, u32[]{:S(2)}) collective-permute-start(f32[16,8,512]{2,1,0:T(8,128)} %get-tuple-element.64), channel_id=1, source_target_pairs={{0,4},{4,8},{8,12},{12,16},{16,20},{20,24},{24,28},{1,5},{5,9},{9,... | collective-permute-start | bytes 786440 | tf_op jit(solution)/shard_map/ppermute | solution.py:658
  77.5 1.3 collective-permute-start.3
  78.8 5.4 %all-to-all-start.1 = ((f32[8,16,128]{2,1,0:T(8,128)}), f32[8,16,128]{2,1,0:T(8,128)S(1)}, u32[]{:S(2)}, u32[]{:S(2)}) async-start(f32[8,16,128]{2,1,0:T(8,128)} %get-tuple-element.61), calls=%async_computation.1 | async-start | bytes 131072 | tf_op jit(solution)/shard_map/all_to_all | solution.py:594
  84.2 6.9 %all-to-all-done.1.mids_ref = f32[8,16,128]{2,1,0:T(8,128)S(1)} async-done(((f32[8,16,128]{2,1,0:T(8,128)}), f32[8,16,128]{2,1,0:T(8,128)S(1)}, u32[]{:S(2)}, u32[]{:S(2)}) %all-to-all-start.1) | async-done | bytes 65568 | tf_op jit(solution)/shard_map/all_to_all | solution.py:594
  91.1 0.0 copy-start.4
  91.1 0.0 collective-permute-done.2.from_left_ref
  91.1 0.0 copy-start.2
  91.1 0.0 collective-permute-done.3.from_right_ref
  91.1 0.0 copy-start.3
  91.1 0.6 copy-done.4
  91.7 0.1 copy-done.2
  91.8 0.1 copy-done.3
  91.9 51.5 %shard_map.307 = (bf16[16,512,512]{2,1,0:T(8,128)(2,1)}, bf16[16,512,512]{2,1,0:T(8,128)(2,1)}, f32[896,128]{1,0:T(8,128)}, f32[896,128]{1,0:T(8,128)}) custom-call(s32[16]{0:T(128)} %broadcast_subtract_fusion.ends_ref, s32[1]{0:T(128)} %bitcast.origin_ref, s32[1]{0:T(128)} %bitcast.1.core_ref, f32[8,16,128]{2,1,0:T(8,128)} %all_to_all.20.sums_ref, ...), custom_call_target="tpu_custom_call" | custom-call | flops 9663676416 | bytes 83886080 | tf_op jit(solution)/shard_map/pallas_call | solution.py:669
  143.4 0.1 collective-permute-start.4
  143.5 2.0 %collective-permute-done.4 = f32[896,128]{1,0:T(8,128)S(1)} collective-permute-done((f32[896,128]{1,0:T(8,128)}, f32[896,128]{1,0:T(8,128)S(1)}, u32[]{:S(2)}, u32[]{:S(2)}) %collective-permute-start.4) | collective-permute-done | bytes 458784 | tf_op jit(solution)/shard_map/ppermute | solution.py:692
  145.5 1.9 add.3
  147.4 3.7 %all-to-all-start.2 = ((f32[16,56,128]{2,1,0:T(8,128)}), f32[16,56,128]{2,1,0:T(8,128)S(1)}, u32[]{:S(2)}, u32[]{:S(2)}) async-start(f32[16,56,128]{2,1,0:T(8,128)} %bitcast.10), calls=%async_computation.2 | async-start | bytes 917504 | tf_op jit(solution)/shard_map/all_to_all | solution.py:594
  151.1 19.0 %shard_map.308 = (f32[16,128,512]{2,1,0:T(8,128)}, f32[16,128,512]{2,1,0:T(8,128)}) custom-call(s32[16]{0:T(128)} %broadcast_subtract_fusion.ends_ref, s32[1]{0:T(128)} %bitcast.origin_ref, f32[8,16,128]{2,1,0:T(8,128)} %copy-done.4, f32[16,128,512]{2,1,0:T(8,128)} %x_ref.5, f32[16,528,512]{2,1,0:T(8,128)} %get-tuple-element.69.mid_ref, ...), custom_call_target="tpu_custom_call" | custom-call | flops 6442450944 | bytes 33554432 | tf_op jit(solution)/shard_map/pallas_call | solution.py:699
  170.1 0.0 all-to-all-done.2
  170.2 0.8 broadcast_in_dim.3
  171.0 6.7 %all-to-all-start.3 = ((f32[16,56,128]{2,1,0:T(8,128)}), f32[16,56,128]{2,1,0:T(8,128)S(1)}, u32[]{:S(2)}, u32[]{:S(2)}) async-start(f32[16,56,128]{2,1,0:T(8,128)} %broadcast_in_dim.3), calls=%async_computation.3 | async-start | bytes 917504 | tf_op jit(solution)/shard_map/all_to_all | solution.py:594
  177.7 12.0 %shard_map.309 = f32[16,128,512]{2,1,0:T(8,128)} custom-call(s32[16]{0:T(128)} %broadcast_subtract_fusion.ends_ref, f32[16,128,512]{2,1,0:T(8,128)} %res_ref.5, bf16[16,512,512]{2,1,0:T(8,128)(2,1)} %get-tuple-element.75.u_high_ref, bf16[16,512,512]{2,1,0:T(8,128)(2,1)} %get-tuple-element.76.u_low_ref, bf16[384,512]{1,0:T(8,128)(2,1)} %get-tuple-element.59.w_cat_ref), custom_call_target="tpu_custom_call" | custom-call | flops 3221225472 | bytes 25165824 | tf_op jit(solution)/shard_map/pallas_call | solution.py:716
  189.7 1.9 all-to-all-done.3
  191.6 0.0 copy-start
  191.6 0.0 collective-permute-start.5
  191.6 1.8 collective-permute-done.5.theirs_ref
  193.4 0.0 copy-done
  193.4 0.0 copy-start.1
  193.4 0.8 copy-done.1
  194.1 2.5 %shard_map.310 = (f32[512,128]{1,0:T(8,128)}, f32[1,512]{1,0:T(1,128)}, f32[1,512]{1,0:T(1,128)}, f32[1,512]{1,0:T(1,128)}, f32[1,512]{1,0:T(1,128)}, /*index=5*...) custom-call(s32[1]{0:T(128)} %bitcast.1.core_ref, ...), custom_call_target="tpu_custom_call" | custom-call | tf_op jit(solution)/shard_map/pallas_call | solution.py:733
  (1 shorter events, 0.0 us)
Async XLA Ops:
  15.0 20.1 %collective-permute-start = (f32[16,16,128]{2,1,0:T(8,128)}, f32[16,16,128]{2,1,0:T(8,128)S(1)}, u32[]{:S(2)}, u32[]{:S(2)}) collective-permute-start(f32[16,16,128]{2,1,0:T(8,128)} %get-tuple-element.56), channel_id=1, source_target_pairs={{0,4},{4,8},{8,12},{12,16},{16,20},{20,24},{24,28},{1,5},{5,9},{9,... | collective-permute-start | bytes 393224 | tf_op jit(solution)/shard_map/ppermute | solution.py:635
  19.9 15.3 %collective-permute-start.1 = (f32[16,16,128]{2,1,0:T(8,128)}, f32[16,16,128]{2,1,0:T(8,128)S(1)}, u32[]{:S(2)}, u32[]{:S(2)}) collective-permute-start(f32[16,16,128]{2,1,0:T(8,128)} %get-tuple-element.57), channel_id=1, source_target_pairs={{4,0},{8,4},{12,8},{16,12},{20,16},{24,20},{28,24},{5,1},{9,5},{13... | collective-permute-start | bytes 393224 | tf_op jit(solution)/shard_map/ppermute | solution.py:636
  35.1 0.7 copy-start.5
  35.2 0.7 copy-start.6
  75.1 15.9 %collective-permute-start.2 = (f32[16,8,512]{2,1,0:T(8,128)}, f32[16,8,512]{2,1,0:T(8,128)S(1)}, u32[]{:S(2)}, u32[]{:S(2)}) collective-permute-start(f32[16,8,512]{2,1,0:T(8,128)} %get-tuple-element.64), channel_id=1, source_target_pairs={{0,4},{4,8},{8,12},{12,16},{16,20},{20,24},{24,28},{1,5},{5,9},{9,... | collective-permute-start | bytes 786440 | tf_op jit(solution)/shard_map/ppermute | solution.py:658
  77.5 13.6 %collective-permute-start.3 = (f32[16,8,512]{2,1,0:T(8,128)}, f32[16,8,512]{2,1,0:T(8,128)S(1)}, u32[]{:S(2)}, u32[]{:S(2)}) collective-permute-start(f32[16,8,512]{2,1,0:T(8,128)} %get-tuple-element.65), channel_id=1, source_target_pairs={{4,0},{8,4},{12,8},{16,12},{20,16},{24,20},{28,24},{5,1},{9,5},{13... | collective-permute-start | bytes 786440 | tf_op jit(solution)/shard_map/ppermute | solution.py:659
  78.8 12.3 %all-to-all-start.1 = ((f32[8,16,128]{2,1,0:T(8,128)}), f32[8,16,128]{2,1,0:T(8,128)S(1)}, u32[]{:S(2)}, u32[]{:S(2)}) async-start(f32[8,16,128]{2,1,0:T(8,128)} %get-tuple-element.61), calls=%async_computation.1 | async-start | bytes 131072 | tf_op jit(solution)/shard_map/all_to_all | solution.py:594
  91.1 0.6 copy-start.4
  91.1 0.7 copy-start.2
  91.1 0.8 copy-start.3
  143.4 2.1 %collective-permute-start.4 = (f32[896,128]{1,0:T(8,128)}, f32[896,128]{1,0:T(8,128)S(1)}, u32[]{:S(2)}, u32[]{:S(2)}) collective-permute-start(f32[896,128]{1,0:T(8,128)} %get-tuple-element.67), channel_id=1, source_target_pairs={{0,1},{1,0},{2,3},{3,2},{4,5},{5,4},{6,7},{7,6},{8,9},{9,8},{10,11... | collective-permute-start | bytes 1376264 | tf_op jit(solution)/shard_map/ppermute | solution.py:692
  147.4 22.7 %all-to-all-start.2 = ((f32[16,56,128]{2,1,0:T(8,128)}), f32[16,56,128]{2,1,0:T(8,128)S(1)}, u32[]{:S(2)}, u32[]{:S(2)}) async-start(f32[16,56,128]{2,1,0:T(8,128)} %bitcast.10), calls=%async_computation.2 | async-start | bytes 917504 | tf_op jit(solution)/shard_map/all_to_all | solution.py:594
  171.0 20.6 %all-to-all-start.3 = ((f32[16,56,128]{2,1,0:T(8,128)}), f32[16,56,128]{2,1,0:T(8,128)S(1)}, u32[]{:S(2)}, u32[]{:S(2)}) async-start(f32[16,56,128]{2,1,0:T(8,128)} %broadcast_in_dim.3), calls=%async_computation.3 | async-start | bytes 917504 | tf_op jit(solution)/shard_map/all_to_all | solution.py:594
  191.6 1.8 copy-start
  191.6 1.8 collective-permute-start.5
  193.4 0.8 copy-start.1

commit v2 on v1

--- a/solution.py
+++ b/solution.py
@@ -13,8 +13,8 @@
 LANE = 128
 ROWS = 64
 SECOND_ROWS = 128
-THIRD_ROWS = 64
 PIECE = 256
+THIRD_ROWS = 128
 F32 = jnp.float32
 BF16 = jnp.bfloat16
 VMEM_LIMIT = 60 * 1024 * 1024
@@ -57,9 +57,10 @@
 
 def act_parts(half, c0, c1):
     th = jnp.tanh(half)
-    rest = half - half * th
-    cut = c0 * rest
-    return half - cut, (c1 + cut) + (c0 + cut) * th, rest
+    ratio = c1 + c0 * th
+    act = half * ratio
+    cut = half - act
+    return act, ratio + cut * (1.0 + th), cut
 
 
 def total(value):
@@ -79,8 +80,9 @@
 
 
 def first_kernel(
-    ends_ref, x_ref, w_in_ref, bias_ref, slope_ref, w_res_ref, w_skip_ref, gain_ref,
-    half_ref, sums_ref, left_ref, right_ref, w_cat_ref, w_out_ref,
+    ends_ref, x_ref, res_l_ref, res_r_ref, skip_l_ref, skip_r_ref, w_in_ref, bias_ref, slope_ref,
+    w_res_ref, w_skip_ref, gain_ref,
+    sums_ref, left_ref, right_ref, w_cat_ref, w_out_ref,
 ):
     group, cin, frames = x_ref.shape
     width = w_in_ref.shape[0]
@@ -91,6 +93,10 @@
         w_cat_ref[0:cin] = high
         w_cat_ref[cin : 2 * cin] = high
         w_cat_ref[2 * cin : 3 * cin] = low
+        row = lax.broadcasted_iota(jnp.int32, (LANE, width), 0)
+        bias = jnp.broadcast_to(0.5 * bias_ref[...], (LANE, width))
+        near = bias.astype(BF16).astype(F32)
+        w_cat_ref[3 * cin :] = jnp.where(row == 0, near, jnp.where(row == 1, bias - near, 0.0)).astype(BF16)
         for number, ref in enumerate((w_res_ref, w_skip_ref)):
             high, low = split(ref[...] * gain_ref[...])
             start = number * cin
@@ -104,14 +110,10 @@
         end = ends_ref[item]
         first = second = jnp.zeros((8, LANE), F32)
         for start in range(0, frames, step):
-            xt = x_ref[number, :, start : start + step].T
-            if start == 0:
-                left_ref[number] = xt[0:HALO]
-            if start + step == frames:
-                right_ref[number] = xt[step - HALO : step]
-            high, low = split(xt)
-            half = product(jnp.concatenate([high, low, high], axis=1), w_cat_ref[...]) + 0.5 * bias_ref[...]
-            half_ref[number, start : start + step] = half
+            xt = x_ref[number, :, start : start + step].astype(BF16).T
+            ones = jnp.ones((step, LANE), BF16)
+            weights = jnp.concatenate([w_cat_ref[0:cin], w_cat_ref[3 * cin :]], axis=0)
+            half = product(jnp.concatenate([xt, ones], axis=1), weights)
             valid = frame_of(start, step) < end
             for lanes in lane_tiles(width):
                 c0, c1 = half_slopes(slope_ref[0:1, lanes])
@@ -122,6 +124,12 @@
         row = place((total(first), total(second)))
         for block in range(sums_ref.shape[0]):
             sums_ref[block, pl.ds(item, 1), :] = row
+        left_ref[number, :, 0:cin] = x_ref[number, :, 0:LANE].T[0:HALO]
+        right_ref[number, :, 0:cin] = x_ref[number, :, frames - LANE : frames].T[LANE - HALO : LANE]
+        left_ref[number, 0:STEP, cin : 2 * cin] = res_l_ref[number].T[0:STEP]
+        left_ref[number, STEP:HALO, cin : 2 * cin] = skip_l_ref[number].T[0:STEP]
+        right_ref[number, 0:STEP, cin : 2 * cin] = res_r_ref[number].T[LANE - STEP : LANE]
+        right_ref[number, STEP:HALO, cin : 2 * cin] = skip_r_ref[number].T[LANE - STEP : LANE]
 
 
 def at(base):
@@ -173,34 +181,42 @@
 
 
 def second_kernel(
-    ends_ref, origin_ref, sums_ref, from_left_ref, from_right_ref, half_ref, res_ref, skip_ref,
-    w_cat_ref, w_out_ref, bias_ref, slope_ref, gain_ref, shift_ref, taps_ref, tap_bias_ref, slope_mid_ref,
-    mid_ref, back_ref, left_ref, right_ref, out_ref,
+    ends_ref, origin_ref, sums_ref, from_left_ref, from_right_ref, x_all, res_all, skip_all,
+    w_cat_ref, w_out_ref, slope_ref, gain_ref, shift_ref, taps_ref, tap_bias_ref, slope_mid_ref,
+    half_all, mid_all, back_all, edge_ref, out_ref,
     halo_ref, normal_ref, coef_ref,
 ):
-    item = pl.program_id(0)
     items = out_ref.shape[1]
-    cin, frames = res_ref.shape[1:]
-    width = w_cat_ref.shape[1]
-    end, origin = ends_ref[item], origin_ref[0]
-
-    @pl.when(item == 0)
+    group, frames, width = half_all.shape
+    cin = x_all.shape[1]
+    origin = origin_ref[0]
+
+    @pl.when(pl.program_id(0) == 0)
     def _():
         mean, scale = first_norm(sums_ref, counts(ends_ref, origin_ref, items, width))
         coef_ref[0] = jnp.broadcast_to(scale, (items, LANE))
         coef_ref[1] = jnp.broadcast_to(scale * mean, (items, LANE))
         for side, ref in enumerate((from_left_ref, from_right_ref)):
-            high, low = split(ref[...].reshape(items * HALO, cin))
-            value = product(jnp.concatenate([high, low, high], axis=1), w_cat_ref[...]) + 0.5 * bias_ref[...]
+            high, low = split(ref[:, :, 0:cin].reshape(items * HALO, cin))
+            ones = jnp.ones((items * HALO, LANE), BF16)
+            value = product(jnp.concatenate([high, low, high, ones], axis=1), w_cat_ref[...])
             halo_ref[side] = value.reshape(items, HALO, width)
-
-    def run(full):
+            cots = jnp.concatenate([ref[:, 0:STEP, cin : 2 * cin], ref[:, STEP:HALO, cin : 2 * cin]], axis=2)
+            high, low = split(cots.reshape(items * STEP, 2 * cin))
+            value = product(jnp.concatenate([high, low, high], axis=1), w_out_ref[...])
+            edge_ref[:, side * STEP : (side + 1) * STEP, :] = value.reshape(items, STEP, width)
+
+    def run(number, item, end, full):
+        half_ref, res_ref, skip_ref, mid_ref, back_ref = (
+            ref.at[number : number + 1] for ref in (half_all, res_all, skip_all, mid_all, back_all)
+        )
+        high, low = split(x_all[number].T)
+        ones = jnp.ones((frames, LANE), BF16)
+        half_ref[0] = product(jnp.concatenate([high, low, high, ones], axis=1), w_cat_ref[...])
         rows = SECOND_ROWS if full and frames % SECOND_ROWS == 0 else ROWS
         d_high, d_low = split(jnp.concatenate([res_ref[0], skip_ref[0]], axis=0))
         high, low = d_high.T, d_low.T
         back_ref[0] = product(jnp.concatenate([high, low, high], axis=1), w_out_ref[...])
-        left_ref[0] = back_ref[0, 0:STEP]
-        right_ref[0] = back_ref[0, frames - STEP : frames]
 
         scale, scale_mean = coef_ref[0, pl.ds(item, 1), :], coef_ref[1, pl.ds(item, 1), :]
         window = jnp.clip(end - STEP, 0, frames - HALO)
@@ -209,10 +225,12 @@
         for lanes in lane_tiles(width):
             c0, c1 = half_slopes(slope_ref[0:1, lanes])
             gain, shift = gain_ref[0:1, lanes], shift_ref[0:1, lanes]
-            factor, offset = tile(2.0 * gain * scale), tile(shift - gain * scale_mean)
+            factor, offset = 2.0 * gain * scale, shift - gain * scale_mean
+            hole = tile(-offset / factor)
 
             def normed(half, valid):
-                return where_valid(valid, factor * act_half(half, c0, c1) + offset)
+                value = act_half(half, c0, c1)
+                return value if valid is None else jnp.where(valid, value, hole)
 
             def store(base, count, value):
                 normal_ref[pl.ds(base, count), lanes] = value.reshape(count, LANE)
@@ -228,12 +246,13 @@
                 return carry
 
             def clear(base):
-                normal_ref[pl.ds(at(base + HALO), rows), lanes] = jnp.zeros((rows, LANE), F32)
+                normal_ref[pl.ds(at(base + HALO), rows), lanes] = jnp.broadcast_to(-offset / factor, (rows, LANE))
 
             sweep(frames, rows, None if full else end, fill, 0, clear)
 
-            taps = [tile(0.5 * taps_ref[tap : tap + 1, lanes]) for tap in range(3)]
-            tap_bias = tile(0.5 * tap_bias_ref[0:1, lanes])
+            rows_of = [0.5 * taps_ref[tap : tap + 1, lanes] for tap in range(3)]
+            taps = [tile(factor * row) for row in rows_of]
+            tap_bias = tile(0.5 * tap_bias_ref[0:1, lanes] + offset * (rows_of[0] + rows_of[1] + rows_of[2]))
             m0, m1 = half_slopes(slope_mid_ref[0:1, lanes])
 
             def conv(base, count):
@@ -250,8 +269,8 @@
                 valid = frame_of(base, rows) < end if masked else None
                 mid = conv(at(base + STEP), rows)
                 act, grad, _ = act_parts(mid, m0, m1)
-                back = where_valid(valid, load(back_ref.at[0], base, rows, lanes))
-                act, grad = where_valid(valid, act), where_valid(valid, grad)
+                back = load(back_ref.at[0], base, rows, lanes)
+                act, grad, back = where_valid(valid, act), where_valid(valid, grad), where_valid(valid, back)
                 ex, ez = grad * back, grad * act
                 terms = (act, act * act, back, back * act, ex, grad, ez, ex * mid, grad * mid, ez * mid)
                 return tuple(old + jnp.sum(new, axis=0) for old, new in zip(carry, terms))
@@ -278,11 +297,15 @@
                 tots[7 + term] = (
                     tots[7 + term] + 2.0 * sums[7 + term] - tap_bias_ref[0:1, lanes] * plain - shift * edged
                 )
+
         row = place([total(value) for value in tots])
         for block in range(out_ref.shape[0]):
             out_ref[block, pl.ds(item, 1), :] = row
 
-    both_ways(end >= frames, run)
+    for number in range(group):
+        item = pl.program_id(0) * group + number
+        end = ends_ref[item]
+        both_ways(end >= frames, functools.partial(run, number, item, end))
 
 
 GRAD_ROWS = 16
@@ -307,19 +330,17 @@
 
 
 def third_kernel(
-    ends_ref, origin_ref, core_ref, sums_ref, mids_ref, x_ref, res_ref, skip_ref, half_ref, mid_ref, back_ref,
-    from_left_ref, from_right_ref,
+    ends_ref, origin_ref, core_ref, sums_ref, mids_ref, x_all, res_all, skip_all, half_all, mid_all, back_all, edge_all,
     slope_ref, gain_ref, shift_ref, taps_ref, slope_mid_ref,
-    u_high_ref, u_low_ref, keep_ref, send_ref,
-    grad_ref, coef_ref, vector_ref, grads_ref, z_high_ref, z_low_ref, cot_ref,
+    r_high_all, r_low_all, u_high_all, u_low_all, keep_ref, send_ref,
+    grad_ref, coef_ref, vector_ref, grads_ref, cot_ref,
 ):
-    item = pl.program_id(0)
     items = coef_ref.shape[1]
-    cin, frames = x_ref.shape[1:]
-    width = half_ref.shape[2]
-    end, origin = ends_ref[item], origin_ref[0]
-
-    @pl.when(item == 0)
+    group, cin, frames = x_all.shape
+    width = half_all.shape[2]
+    origin = origin_ref[0]
+
+    @pl.when(pl.program_id(0) == 0)
     def _():
         count = counts(ends_ref, origin_ref, items, width)
         mean1, scale1 = first_norm(sums_ref, count)
@@ -330,7 +351,7 @@
         mean_b = scale2 * (m[7] - alpha * m[8] - 2.0 * beta * m[9]) / count
         values = (
             scale1, scale1 * mean1, scale1 * (mean_a - mean1 * scale1 * mean_b), 2.0 * scale1 * scale1 * mean_b,
-            scale2, scale2 * alpha, 2.0 * scale2 * beta, 2.0 * scale2, scale2 * mean2,
+            scale2, alpha, 2.0 * beta, scale2 * mean2,
         )
         for number, value in enumerate(values):
             coef_ref[number] = jnp.broadcast_to(value, (items, LANE))
@@ -338,47 +359,54 @@
         grads_ref[...] = jnp.zeros(grads_ref.shape, F32)
         cot_ref[...] = jnp.zeros(cot_ref.shape, F32)
 
-    def run(full):
+    def run(number, item, end, full):
+        x_ref, res_ref, skip_ref, half_ref, mid_ref, back_ref, edge_ref = (
+            ref.at[number : number + 1] for ref in (x_all, res_all, skip_all, half_all, mid_all, back_all, edge_all)
+        )
+        r_high_ref, r_low_ref, u_high_ref, u_low_ref = (
+            ref.at[number : number + 1] for ref in (r_high_all, r_low_all, u_high_all, u_low_all)
+        )
         rows = THIRD_ROWS if full else ROWS
-        coefs = [tile(coef_ref[number, pl.ds(item, 1), :]) for number in range(9)]
-        scale1, scale_mean1, dp_a, dp_b, dr_0, dr_a, dr_b, z_0, z_a = coefs
+        coefs = [tile(coef_ref[number, pl.ds(item, 1), :]) for number in range(8)]
+        scale1, scale_mean1, dp_a, dp_b, scale2, dr_a, dr_b, z_a = coefs
         both = jnp.concatenate([res_ref[0], skip_ref[0]], axis=0)
         d_high, d_low = split(both)
         lane = lax.broadcasted_iota(jnp.int32, (1, LANE), 1)
-        cots = cot_ref[...]
+        cots = jnp.zeros((2 * cin, LANE), F32)
         for lanes in lane_tiles(frames):
             piece = both[:, lanes]
             cots = cots + (piece if full else jnp.where(lane + lanes.start < end, piece, 0.0))
-        cot_ref[...] = cots
+        cot_ref[0] += cots
+        cot_ref[1] += z_a[0:1] * cots
 
         for lanes in lane_tiles(width):
             m0, m1 = half_slopes(slope_mid_ref[0:1, lanes])
 
             def middle(base, count, valid, back):
-                act, slope, rest = act_parts(load(mid_ref.at[0], base, count, lanes), m0, m1)
-                grad = (dr_0 * back - dr_a) - dr_b * act
+                act, slope, cut = act_parts(load(mid_ref.at[0], base, count, lanes), m0, m1)
+                grad = (back - dr_a) - dr_b * act
                 grad = where_valid(valid, grad)
                 grad_ref[pl.ds(base, count), lanes] = (grad * slope).reshape(count, LANE)
-                return act, grad * rest
+                return act, grad * cut
 
             frame = frame_of(-STEP, STEP)
-            middle(0, STEP, (frame < end) & (frame >= -origin), from_left_ref[0:1, :, lanes])
-            middle(frames + STEP, STEP, frame_of(frames, STEP) < end, from_right_ref[0:1, :, lanes])
+            middle(0, STEP, (frame < end) & (frame >= -origin), edge_ref[0:1, 0:STEP, lanes])
+            middle(frames + STEP, STEP, frame_of(frames, STEP) < end, edge_ref[0:1, STEP:HALO, lanes])
 
             def inner(base, masked, carry):
                 valid = frame_of(base, rows) < end if masked else None
                 act, term = middle(at(base + STEP), rows, valid, load(back_ref.at[0], base, rows, lanes))
-                high, low = split(where_valid(valid, z_0 * act - z_a).reshape(rows, LANE))
-                z_high_ref[pl.ds(base, rows), lanes] = high
-                z_low_ref[pl.ds(base, rows), lanes] = low
+                high, low = split(where_valid(valid, act).reshape(rows, LANE))
+                r_high_ref[0, pl.ds(base, rows), lanes] = high
+                r_low_ref[0, pl.ds(base, rows), lanes] = low
                 return carry + jnp.sum(term, axis=0)
 
             def inner_clear(base):
                 grad_ref[pl.ds(at(base + STEP), rows), lanes] = jnp.zeros((rows, LANE), F32)
-                z_high_ref[pl.ds(base, rows), lanes] = jnp.zeros((rows, LANE), BF16)
-                z_low_ref[pl.ds(base, rows), lanes] = jnp.zeros((rows, LANE), BF16)
-
-            vector_ref[8, :, lanes] += sweep(
+                r_high_ref[0, pl.ds(base, rows), lanes] = jnp.zeros((rows, LANE), BF16)
+                r_low_ref[0, pl.ds(base, rows), lanes] = jnp.zeros((rows, LANE), BF16)
+
+            vector_ref[8, :, lanes] += scale2 / m0 * sweep(
                 frames, rows, None if full else end, inner, jnp.zeros((8, LANE), F32), inner_clear
             )
 
@@ -386,66 +414,76 @@
             gain, shift = gain_ref[0:1, lanes], shift_ref[0:1, lanes]
             taps = [tile(taps_ref[tap : tap + 1, lanes]) for tap in range(3)]
             outer = gain * scale1
+            scaled = [tap * (outer * scale2) for tap in taps]
 
             def body(base, masked, carry):
                 valid = frame_of(base, rows) < end if masked else None
                 ahead = load(grad_ref, at(base + HALO), rows, lanes)
                 here = load(grad_ref, at(base + STEP), rows, lanes)
                 behind = where_valid(valid, load(grad_ref, base, rows, lanes))
-                act, slope, rest = act_parts(load(half_ref.at[0], base, rows, lanes), c0, c1)
-                dn = taps[0] * ahead + taps[1] * here + taps[2] * behind
-                dp = where_valid(valid, (outer * dn - dp_a) - dp_b * act)
+                act, slope, cut = act_parts(load(half_ref.at[0], base, rows, lanes), c0, c1)
+                dp = scaled[0] * ahead + scaled[1] * here + scaled[2] * behind
+                dp = where_valid(valid, (dp - dp_a) - dp_b * act)
                 du = dp * slope
                 high, low = split(du.reshape(rows, LANE))
                 u_high_ref[0, pl.ds(base, rows), lanes] = high
                 u_low_ref[0, pl.ds(base, rows), lanes] = low
-                terms = (du, dp * rest, here, ahead * act, here * act, behind * act)
+                terms = (dp * cut, here, ahead * act, here * act, behind * act)
                 return tuple(old + jnp.sum(new, axis=0) for old, new in zip(carry, terms))
 
             def clear(base):
                 u_high_ref[0, pl.ds(base, rows), lanes] = jnp.zeros((rows, LANE), BF16)
                 u_low_ref[0, pl.ds(base, rows), lanes] = jnp.zeros((rows, LANE), BF16)
 
-            sums = sweep(frames, rows, None if full else end, body, (jnp.zeros((8, LANE), F32),) * 6, clear)
+            sums = sweep(frames, rows, None if full else end, body, (jnp.zeros((8, LANE), F32),) * 5, clear)
             window = pl.multiple_of(lax.div(jnp.clip(end, 0, frames - HALO), 8) * 8, 8)
             row = frame_of(window, HALO)
             inside = jnp.where((row >= end) & (row < end + STEP), load(grad_ref, window, HALO, lanes), 0.0)
             plains = (
-                sums[2] - grad_ref[STEP:HALO, lanes] + grad_ref[frames + STEP : frames + HALO, lanes],
-                sums[2],
-                sums[2] - grad_ref[frames : frames + STEP, lanes] + grad_ref[0:STEP, lanes] - jnp.sum(inside, axis=0),
+                sums[1] - grad_ref[STEP:HALO, lanes] + grad_ref[frames + STEP : frames + HALO, lanes],
+                sums[1],
+                sums[1] - grad_ref[frames : frames + STEP, lanes] + grad_ref[0:STEP, lanes] - jnp.sum(inside, axis=0),
             )
             factor, offset = 2.0 * outer, shift - gain * scale_mean1
-            vector_ref[0, :, lanes] += sums[0]
-            vector_ref[1, :, lanes] += sums[1]
+            vector_ref[1, :, lanes] += sums[0] / c0
             gain_sum = shift_sum = jnp.zeros((8, LANE), F32)
             for tap in range(3):
-                plain, times = plains[tap], sums[3 + tap]
+                plain, times = scale2 * plains[tap], scale2 * sums[2 + tap]
                 vector_ref[4 + tap, :, lanes] += factor * times + offset * plain
                 gain_sum = gain_sum + taps[tap] * (2.0 * scale1 * times - scale_mean1 * plain)
                 shift_sum = shift_sum + taps[tap] * plain
             vector_ref[2, :, lanes] += gain_sum
             vector_ref[3, :, lanes] += shift_sum
-            vector_ref[7, :, lanes] += sums[2]
-
-        z_high, z_low = z_high_ref[...], z_low_ref[...]
-        grads_ref[0 : 2 * cin] += product(
-            jnp.concatenate([d_high, d_low, d_high], axis=1), jnp.concatenate([z_high, z_high, z_low], axis=0)
+            vector_ref[7, :, lanes] += scale2 * sums[1]
+
+        r_high, r_low = r_high_ref[0], r_low_ref[0]
+        mixed = product(
+            jnp.concatenate([d_high, d_low, d_high], axis=1), jnp.concatenate([r_high, r_high, r_low], axis=0)
         )
+        z_0 = 2.0 * scale2[0:1]
+        for lanes in lane_tiles(width):
+            grads_ref[0 : 2 * cin, lanes] += z_0 * mixed[:, lanes]
         u_high, u_low = u_high_ref[0], u_low_ref[0]
         x_high, x_low = split(x_ref[0])
-        grads_ref[2 * cin : 3 * cin] += product(
-            jnp.concatenate([x_high, x_low, x_high], axis=1), jnp.concatenate([u_high, u_high, u_low], axis=0)
+        rows_of = jnp.concatenate([x_high, x_low, x_high], axis=1)
+        ones = jnp.ones((GRAD_ROWS, frames), BF16)
+        ones = jnp.concatenate([ones, jnp.zeros((GRAD_ROWS, frames), BF16), ones], axis=1)
+        grads_ref[2 * cin : 3 * cin + GRAD_ROWS] += product(
+            jnp.concatenate([rows_of, ones], axis=0), jnp.concatenate([u_high, u_high, u_low], axis=0)
         )
 
-    both_ways(end >= frames, run)
-
-    @pl.when(item == items - 1)
+    for number in range(group):
+        item = pl.program_id(0) * group + number
+        end = ends_ref[item]
+        both_ways(end >= frames, functools.partial(run, number, item, end))
+
+    @pl.when(pl.program_id(0) == items // group - 1)
     def _():
         base = 3 * cin
-        for row in range(9):
+        grads_ref[0 : 2 * cin] = grads_ref[0 : 2 * cin] - jnp.sum(cot_ref[1], axis=1, keepdims=True)
+        for row in range(1, 9):
             grads_ref[base + row : base + row + 1] = jnp.sum(vector_ref[row], axis=0, keepdims=True)
-        column = jnp.broadcast_to(jnp.sum(cot_ref[...], axis=1, keepdims=True), cot_ref.shape).T[0:1]
+        column = jnp.broadcast_to(jnp.sum(cot_ref[0], axis=1, keepdims=True), (2 * cin, LANE)).T[0:1]
         grads_ref[base + 9 : base + 10] = jnp.zeros((1, width), F32)
         for number in range(2 * cin // LANE):
             grads_ref[base + 9 + number : base + 10 + number, 0:LANE] = column[:, number * LANE : (number + 1) * LANE]
@@ -461,67 +499,47 @@
 
 
 def outer_kernel(
-    ends_ref, origin_ref, mids_ref, x_ref, mid_ref, w_out_ref, w_res_ref, w_skip_ref, gain_ref, shift_ref, slope_ref,
-    bias_res_ref, bias_skip_ref, res_out_ref, skip_out_ref, coef_ref, column_ref, wide_ref, turned_ref,
+    ends_ref, origin_ref, mids_ref, x_ref, res_ref, r_high_ref, r_low_ref, u_high_ref, u_low_ref,
+    w_cat_ref, w_out_ref, w_res_ref, w_skip_ref, gain_ref, shift_ref, bias_res_ref, bias_skip_ref, *rest_refs, offset,
 ):
+    res_out_ref, skip_out_ref, x_grad_ref, coef_ref, column_ref, out_turned_ref, in_turned_ref = rest_refs[-7:]
     items = coef_ref.shape[1]
     group, cin, frames = x_ref.shape
-    width = w_out_ref.shape[1]
+    width = w_cat_ref.shape[1]
 
     @pl.when(pl.program_id(0) == 0)
     def _():
         _, mean, scale = second_norm(mids_ref, counts(ends_ref, origin_ref, items, width))
-        high, low = w_out_ref[0 : 2 * cin].T, w_out_ref[4 * cin : 6 * cin].T
-        turned_ref[0:width] = high
-        turned_ref[width : 2 * width] = high
-        turned_ref[2 * width : 3 * width] = low
         coef_ref[0] = jnp.broadcast_to(2.0 * scale, (items, LANE))
         coef_ref[1] = jnp.broadcast_to(scale * mean, (items, LANE))
+        high, low = w_out_ref[0 : 2 * cin].T, w_out_ref[4 * cin : 6 * cin].T
+        out_turned_ref[0:width] = high
+        out_turned_ref[width : 2 * width] = high
+        out_turned_ref[2 * width : 3 * width] = low
+        in_turned_ref[:, 0:cin] = w_cat_ref[0:cin].T
+        in_turned_ref[:, cin : 2 * cin] = w_cat_ref[2 * cin : 3 * cin].T
         for number, (w_ref, b_ref) in enumerate(((w_res_ref, bias_res_ref), (w_skip_ref, bias_skip_ref))):
             rows = slice(number * cin, (number + 1) * cin)
             column_ref[0, rows] = jnp.broadcast_to(b_ref[...], (LANE, cin)).T
-            for place_of, vector_of in ((1, shift_ref), (2, gain_ref)):
+            for spot, vector_of in ((1, shift_ref), (2, gain_ref)):
                 value = jnp.sum(w_ref[...] * vector_of[...], axis=1, keepdims=True)
-                column_ref[place_of, rows] = jnp.broadcast_to(value, (cin, LANE))
+                column_ref[spot, rows] = jnp.broadcast_to(value, (cin, LANE))
 
     lane = lax.broadcasted_iota(jnp.int32, (1, LANE), 1)
     for number in range(group):
-        item = pl.program_id(0) * group + number
+        item = offset + pl.program_id(0) * group + number
         end = ends_ref[item]
         z_0, z_a = coef_ref[0, pl.ds(item, 1), :], coef_ref[1, pl.ds(item, 1), :]
-        for lanes in lane_tiles(width):
-            m0, m1 = half_slopes(slope_ref[0:1, lanes])
-            for base in range(0, frames, ROWS):
-                act = act_half(load(mid_ref.at[number], base + STEP, ROWS, lanes), m0, m1)
-                act = jnp.where(frame_of(base, ROWS) < end, act, 0.0)
-                high, low = split(act.reshape(ROWS, LANE))
-                spot = number % 2
-                wide_ref[spot, base : base + ROWS, lanes] = high
-                wide_ref[spot, base : base + ROWS, width + lanes.start : width + lanes.stop] = low
-        r_high, r_low = wide_ref[spot, :, 0:width], wide_ref[spot, :, width:]
-        out = product(jnp.concatenate([r_high, r_low, r_high], axis=1), turned_ref[...]).T
+        r_high, r_low = r_high_ref[number], r_low_ref[number]
+        out = product(jnp.concatenate([r_high, r_low, r_high], axis=1), out_turned_ref[...]).T
+        pair = product(u_high_ref[number], in_turned_ref[...])
+        x_grad = (pair[:, 0:cin] + pair[:, cin : 2 * cin] + product(u_low_ref[number], in_turned_ref[:, 0:cin])).T
         inside = column_ref[1] - z_a * column_ref[2]
         for lanes in lane_tiles(frames):
-            wide = column_ref[0] + jnp.where(lane + lanes.start < end, inside, 0.0) + z_0 * out[:, lanes]
+            valid = lane + lanes.start < end
+            wide = column_ref[0] + jnp.where(valid, inside, 0.0) + z_0 * out[:, lanes]
             res_out_ref[number, :, lanes] = wide[0:cin] + x_ref[number, :, lanes]
             skip_out_ref[number, :, lanes] = wide[cin : 2 * cin]
-
-
-def inner_kernel(ends_ref, res_ref, u_high_ref, u_low_ref, w_cat_ref, x_grad_ref, turned_ref):
-    group, cin, frames = res_ref.shape
-
-    @pl.when(pl.program_id(0) == 0)
-    def _():
-        turned_ref[:, 0:cin] = w_cat_ref[0:cin].T
-        turned_ref[:, cin : 2 * cin] = w_cat_ref[2 * cin : 3 * cin].T
-
-    lane = lax.broadcasted_iota(jnp.int32, (1, LANE), 1)
-    for number in range(group):
-        end = ends_ref[pl.program_id(0) * group + number]
-        pair = product(u_high_ref[number], turned_ref[...])
-        x_grad = (pair[:, 0:cin] + pair[:, cin : 2 * cin] + product(u_low_ref[number], turned_ref[:, 0:cin])).T
-        for lanes in lane_tiles(frames):
-            valid = lane + lanes.start < end
             x_grad_ref[number, :, lanes] = jnp.where(valid, res_ref[number, :, lanes], 0.0) + 2.0 * x_grad[:, lanes]
 
 
@@ -576,6 +594,10 @@
 
 def per_item(array, group=1, offset=0):
     return pl.BlockSpec((group,) + array.shape[1:], lambda item: (item + offset, 0, 0))
+
+
+def edge_block(array, group, position):
+    return pl.BlockSpec((group, array.shape[1], LANE), lambda item: (item, 0, position))
 
 
 def sds(*shape, dtype=F32):
@@ -614,20 +636,23 @@
     ends_spec = whole(ends, pltpu.SMEM)
 
     half = sds(items, frames, width)
-    halo = sds(items, HALO, cin)
+    halo = sds(items, HALO, 2 * cin)
+    last = frames // LANE - 1
     sums = sds(blocks, items, LANE)
-    w_cat, w_out = sds(3 * cin, width, dtype=BF16), sds(6 * cin, width, dtype=BF16)
+    w_cat, w_out = sds(3 * cin + LANE, width, dtype=BF16), sds(6 * cin, width, dtype=BF16)
     weights = (weight_in, bias_in, slope_in, weight_res, weight_skip, gain_mid)
     pair = 2 if items % 2 == 0 else 1
     quad = 4 if items % 4 == 0 else 1
-    half, first_sums, to_left, to_right, w_cat, w_out = pl.pallas_call(
+    first_sums, to_left, to_right, w_cat, w_out = pl.pallas_call(
         first_kernel,
-        grid=(items // pair,),
-        in_specs=[ends_spec, per_item(inputs, pair)] + [whole(array) for array in weights],
-        out_specs=[per_item(half, pair), whole(sums), per_item(halo, pair), per_item(halo, pair), whole(w_cat), whole(w_out)],
-        out_shape=[half, sums, halo, halo, w_cat, w_out],
+        grid=(items // quad,),
+        in_specs=[ends_spec, per_item(inputs, quad)]
+        + [edge_block(array, quad, spot) for array in (cot_res, cot_skip) for spot in (0, last)]
+        + [whole(array) for array in weights],
+        out_specs=[whole(sums), per_item(halo, quad), per_item(halo, quad), whole(w_cat), whole(w_out)],
+        out_shape=[sums, halo, halo, w_cat, w_out],
         compiler_params=params(),
-    )(ends, inputs, *weights)
+    )(ends, inputs, cot_res, cot_res, cot_skip, cot_skip, *weights)
 
     forward = [(block, block + 1) for block in range(blocks - 1)]
     backward = [(target, source) for source, target in forward]
@@ -635,54 +660,52 @@
     from_left = lax.ppermute(to_right, "blk", forward)
     from_right = lax.ppermute(to_left, "blk", backward)
 
-    mid, edge = sds(items, frames + HALO, width), sds(items, STEP, width)
+    mid, edge = sds(items, frames + HALO, width), sds(items, HALO, width)
     small = (first_sums, from_left, from_right)
-    weights = (w_cat, w_out, bias_in, slope_in, gain_in, shift_in, taps, tap_bias, slope_mid)
+    weights = (w_cat, w_out, slope_in, gain_in, shift_in, taps, tap_bias, slope_mid)
     rounded = sds(items, frames, width, dtype=BF16)
-    mid, back, to_left, to_right, mid_sums = pl.pallas_call(
+    half, mid, back, edge, mid_sums = pl.pallas_call(
         second_kernel,
-        grid=(items,),
+        grid=(items // pair,),
         in_specs=[ends_spec, ends_spec]
         + [whole(array) for array in small]
-        + [per_item(half), per_item(cot_res), per_item(cot_skip)]
+        + [per_item(array, pair) for array in (inputs, cot_res, cot_skip)]
         + [whole(array) for array in weights],
-        out_specs=[per_item(mid), per_item(half), per_item(edge), per_item(edge), whole(sums)],
-        out_shape=[mid, sds(*half.shape), edge, edge, sums],
+        out_specs=[per_item(half, pair), per_item(mid, pair), per_item(half, pair), whole(edge), whole(sums)],
+        out_shape=[half, mid, half, edge, sums],
         scratch_shapes=[
             pltpu.VMEM((2, items, HALO, width), F32),
             pltpu.VMEM((frames + 2 * HALO, width), F32),
             pltpu.VMEM((2, items, LANE), F32),
         ],
         compiler_params=params(),
-    )(ends, origin, *small, half, cot_res, cot_skip, *weights)
-    from_left = lax.ppermute(to_right, "blk", forward)
-    from_right = lax.ppermute(to_left, "blk", backward)
+        cost_estimate=cost(20 * items * frames * cin * width, items * frames * width * 14),
+    )(ends, origin, *small, inputs, cot_res, cot_skip, *weights)
     mid_sums = exchange(mid_sums, "blk")
 
     small = (first_sums, mid_sums)
-    large = (inputs, cot_res, cot_skip, half, mid, back, from_left, from_right)
+    large = (inputs, cot_res, cot_skip, half, mid, back, edge)
     weights = (slope_in, gain_in, shift_in, taps, slope_mid)
+    wide = sds(*inputs.shape)
     height = 3 * cin + GRAD_ROWS
     chips = blocks * lax.axis_size("side")
     piece = -(-height * (width // LANE) // (2 * chips * 8)) * 8
     flat = sds(chips * piece, LANE)
-    u_high, u_low, keep, send = pl.pallas_call(
+    r_high, r_low, u_high, u_low, keep, send = pl.pallas_call(
         third_kernel,
-        grid=(items,),
+        grid=(items // pair,),
         in_specs=[ends_spec] * 3
         + [whole(array) for array in small]
-        + [per_item(array) for array in large]
+        + [per_item(array, pair) for array in large]
         + [whole(array) for array in weights],
-        out_specs=[per_item(rounded)] * 2 + [whole(flat)] * 2,
-        out_shape=[rounded] * 2 + [flat] * 2,
+        out_specs=[per_item(rounded, pair)] * 4 + [whole(flat)] * 2,
+        out_shape=[rounded] * 4 + [flat] * 2,
         scratch_shapes=[
             pltpu.VMEM((frames + HALO, width), F32),
-            pltpu.VMEM((9, items, LANE), F32),
+            pltpu.VMEM((8, items, LANE), F32),
             pltpu.VMEM((9, 8, width), F32),
             pltpu.VMEM((height, width), F32),
-            pltpu.VMEM((frames, width), BF16),
-            pltpu.VMEM((frames, width), BF16),
-            pltpu.VMEM((2 * cin, LANE), F32),
+            pltpu.VMEM((2, 2 * cin, LANE), F32),
         ],
         compiler_params=params(),
         cost_estimate=cost(18 * items * frames * cin * width, items * frames * width * 20),
@@ -690,40 +713,40 @@
 
     swap = [(0, 1), (1, 0)]
     keep = keep + lax.ppermute(send, "core", swap)
-    keep, mid = lax.optimization_barrier((keep, mid))
+    keep, r_high = lax.optimization_barrier((keep, r_high))
     pieces = exchange(keep.reshape(chips, piece, LANE), ("blk", "side"))
 
-    wide = sds(*inputs.shape)
-    large = (inputs, mid)
-    weights = (w_out, weight_res, weight_skip, gain_mid, shift_mid, slope_mid, bias_res, bias_skip)
-    residual_out, skip_out = pl.pallas_call(
-        outer_kernel,
-        grid=(items // quad,),
-        in_specs=[ends_spec] * 2
-        + [whole(mid_sums)]
-        + [per_item(array, quad) for array in large]
-        + [whole(array) for array in weights],
-        out_specs=[per_item(wide, quad)] * 2,
-        out_shape=[wide] * 2,
-        scratch_shapes=[pltpu.VMEM((2, items, LANE), F32), pltpu.VMEM((3, 2 * cin, LANE), F32)]
-        + [pltpu.VMEM((2, frames, 2 * width), BF16), pltpu.VMEM((3 * width, 2 * cin), BF16)],
-        compiler_params=params(),
-        cost_estimate=cost(12 * items * frames * cin * width, items * frames * width * 8),
-    )(ends, origin, mid_sums, *large, *weights)
-    pieces, residual_out, u_high = lax.optimization_barrier((pieces, residual_out, u_high))
+    weights = (w_cat, w_out, weight_res, weight_skip, gain_mid, shift_mid, bias_res, bias_skip)
+    count = items // 2
+
+    def outer(offset, size, earlier):
+        pair = 2 if size % 2 == 0 and offset % 2 == 0 else 1
+        large = (inputs, cot_res, r_high, r_low, u_high, u_low)
+        return pl.pallas_call(
+            functools.partial(outer_kernel, offset=offset),
+            grid=(size // pair,),
+            in_specs=[ends_spec, ends_spec, whole(mid_sums)]
+            + [per_item(array, pair, offset // pair) for array in large]
+            + [whole(array) for array in weights]
+            + [pl.BlockSpec(memory_space=pl.ANY)] * len(earlier),
+            out_specs=[per_item(wide, pair, offset // pair)] * 3,
+            out_shape=[wide] * 3,
+            scratch_shapes=[
+                pltpu.VMEM((2, items, LANE), F32),
+                pltpu.VMEM((3, 2 * cin, LANE), F32),
+                pltpu.VMEM((3 * width, 2 * cin), BF16),
+                pltpu.VMEM((width, 2 * cin), BF16),
+            ],
+            input_output_aliases={17: 0, 18: 1, 19: 2} if earlier else {},
+            compiler_params=params(),
+            cost_estimate=cost(12 * size * frames * cin * width, size * frames * width * 8),
+        )(ends, origin, mid_sums, *large, *weights, *earlier)
+
+    residual_out, skip_out, grad_inputs = outer(0, count, ())
+    pieces, residual_out = lax.optimization_barrier((pieces, residual_out))
     mine = exchange(jnp.broadcast_to(jnp.sum(pieces, axis=0), pieces.shape), ("blk", "side")).reshape(-1, LANE)
-    large = (cot_res, u_high, u_low)
-    grad_inputs = pl.pallas_call(
-        inner_kernel,
-        grid=(items // quad,),
-        in_specs=[ends_spec] + [per_item(array, quad) for array in large] + [whole(w_cat)],
-        out_specs=per_item(wide, quad),
-        out_shape=wide,
-        scratch_shapes=[pltpu.VMEM((width, 2 * cin), BF16)],
-        compiler_params=params(),
-        cost_estimate=cost(6 * items * frames * cin * width, items * frames * width * 6),
-    )(ends, *large, w_cat)
-    mine, grad_inputs = lax.optimization_barrier((mine, grad_inputs))
+    residual_out, skip_out, grad_inputs = outer(count, items - count, (residual_out, skip_out, grad_inputs))
+    mine, residual_out = lax.optimization_barrier((mine, residual_out))
     theirs = lax.ppermute(mine, "core", swap)
     vector, short = sds(1, width), sds(1, cin)
     ends_of = (

time: 198 us -> 185 us (0.934)
  starting transfers between devices: 25.6 us -> 19.8 us
  Pallas kernels: 138 us -> 133 us
    pallas_call x5, Pallas kernels: 135 us -> 130 us  [the longest x1 50.8 us: local(): pl.pallas_call(third_kernel, grid=(items // pair,), in_specs=[ends_spec]...]
    all_to_all x3, starting transfers between devices: 15.9 us -> 13.5 us  [exchange(): return lax.all_to_all(pieces, axes, 0, 0)]
    ppermute x2 -> x1, starting transfers between devices: 7.14 us -> 4.85 us  [local(): from_left = lax.ppermute(to_right, 'blk', forward)]
  transfers between devices with their start and end apart: 9 -> 7, of which waited for: 4 -> 5; matrix products, arithmetic and copies ran while one was open for 0% -> 0% of each run, Pallas kernels for 16% -> 15%
where the time goes in v2:
time: 185 us
  Pallas kernels  133 us (72%)
  starting transfers between devices  19.8 us (11%)
  blocking collectives  14 us (8%)
  waiting for transfers between devices  11 us (6%)
  other arithmetic  3.06 us (2%)
  local copies, waits for them, and re-layouts  2.96 us (2%)
    pallas_call x1, Pallas kernels, local(): pl.pallas_call(third_kernel, grid=(items // pair,), in_specs=[ends_spec]...  50.8 us
    pallas_call x1, Pallas kernels, local(): pl.pallas_call(second_kernel, grid=(items // pair,), in_specs=[ends_spec,...  42.3 us
    pallas_call x2, Pallas kernels, outer(): pl.pallas_call(functools.partial(outer_kernel, offset=offset), grid=(size...  27.6 us
    all_to_all x1, blocking collectives, exchange(): return lax.all_to_all(pieces, axes, 0, 0)  14 us
    all_to_all x3, starting transfers between devices, exchange(): return lax.all_to_all(pieces, axes, 0, 0)  13.5 us
    pallas_call x1, Pallas kernels, local(): pl.pallas_call(first_kernel, grid=(items // quad,), in_specs=[ends_spec,...  9.64 us
    all_to_all x3, waiting for transfers between devices, exchange(): return lax.all_to_all(pieces, axes, 0, 0)  7.16 us
    ppermute x1, starting transfers between devices, local(): from_left = lax.ppermute(to_right, 'blk', forward)  4.85 us
  transfers between devices with their start and end apart: 7, of which 5 were waited for; matrix products, arithmetic and copies ran while one was open for 0% of the time, Pallas kernels for 15%

profile of v2, /device:TPU:0, one launch (start us, length us, event | category | flops | bytes accessed | tf_op | source)
XLA Modules:
  0.0 184.6 jit_solution(4412630071080907919)
XLA Ops:
  0.7 1.2 broadcast_subtract_fusion.ends_ref
  1.8 9.6 %shard_map.305 = (f32[8,16,128]{2,1,0:T(8,128)}, f32[16,16,256]{2,1,0:T(8,128)}, f32[16,16,256]{2,1,0:T(8,128)}, bf16[512,512]{1,0:T(8,128)(2,1)}, bf16[768,512]{1,0:T(8,128)(2,1)}) custom-call(s32[16]{0:T(128)} %broadcast_subtract_fusion.ends_ref, f32[16,128,512]{2,1,0:T(8,128)} %x_ref.5, f32[16,128,512]{2,1,0:T(8,128)} %res_ref.3, ...), custom_call_target="tpu_custom_call" | custom-call | tf_op jit(solution)/shard_map/pallas_call | solution.py:646
  11.5 4.8 %collective-permute-start = (f32[16,16,256]{2,1,0:T(8,128)}, f32[16,16,256]{2,1,0:T(8,128)S(1)}, u32[]{:S(2)}, u32[]{:S(2)}) collective-permute-start(f32[16,16,256]{2,1,0:T(8,128)} %get-tuple-element.60), channel_id=1, source_target_pairs={{0,4},{4,8},{8,12},{12,16},{16,20},{20,24},{24,28},{1,5},{5,9},{9,... | collective-permute-start | bytes 786440 | tf_op jit(solution)/shard_map/ppermute | solution.py:660
  16.3 1.3 collective-permute-start.1
  17.6 14.0 %all_to_all.20.sums_ref = f32[8,16,128]{2,1,0:T(8,128)} all-to-all(f32[8,16,128]{2,1,0:T(8,128)} %get-tuple-element.59), channel_id=1, replica_groups=mesh['blk'=8,'side'=2,'core'=2] {'blk'}, dimensions={0} | all-to-all | bytes 131072 | tf_op jit(solution)/shard_map/all_to_all | solution.py:616
  31.6 0.0 collective-permute-done.from_left_ref
  31.6 0.0 copy-start.3
  31.6 0.0 collective-permute-done.1.from_right_ref
  31.6 0.0 copy-start.4
  31.6 0.7 copy-done.3
  32.3 0.1 copy-done.4
  32.4 42.3 %shard_map.306 = (f32[16,512,512]{2,1,0:T(8,128)}, f32[16,528,512]{2,1,0:T(8,128)}, f32[16,512,512]{2,1,0:T(8,128)}, f32[16,16,512]{2,1,0:T(8,128)}, f32[8,16,128]{2,1,0:T(8,128)}) custom-call(s32[16]{0:T(128)} %broadcast_subtract_fusion.ends_ref, s32[1]{0:T(128)} %bitcast.origin_ref, f32[8,16,128]{2,1,0:T(8,128)} %all_to_all.20.sums_ref, ...), custom_call_target="tpu_custom_call" | custom-call | flops 10737418240 | bytes 58720256 | tf_op jit(solution)/shard_map/pallas_call | solution.py:667
  74.7 3.5 %all-to-all-start.1 = ((f32[8,16,128]{2,1,0:T(8,128)}), f32[8,16,128]{2,1,0:T(8,128)S(1)}, u32[]{:S(2)}, u32[]{:S(2)}) async-start(f32[8,16,128]{2,1,0:T(8,128)} %get-tuple-element.64), calls=%async_computation.1 | async-start | bytes 131072 | tf_op jit(solution)/shard_map/all_to_all | solution.py:616
  78.3 6.7 %all-to-all-done.1.mids_ref = f32[8,16,128]{2,1,0:T(8,128)S(1)} async-done(((f32[8,16,128]{2,1,0:T(8,128)}), f32[8,16,128]{2,1,0:T(8,128)S(1)}, u32[]{:S(2)}, u32[]{:S(2)}) %all-to-all-start.1) | async-done | bytes 65568 | tf_op jit(solution)/shard_map/all_to_all | solution.py:616
  84.9 0.0 copy-start.1
  84.9 0.6 copy-done.1
  85.5 50.8 %shard_map.307 = (bf16[16,512,512]{2,1,0:T(8,128)(2,1)}, bf16[16,512,512]{2,1,0:T(8,128)(2,1)}, bf16[16,512,512]{2,1,0:T(8,128)(2,1)}, bf16[16,512,512]{2,1,0:T(...) custom-call(s32[16]{0:T(128)} %broadcast_subtract_fusion.ends_ref, s32[1]{0:T(128)} %bitcast.origin_ref, ...), custom_call_target="tpu_custom_call" | custom-call | flops 9663676416 | bytes 83886080 | tf_op jit(solution)/shard_map/pallas_call | solution.py:694
  136.4 0.1 collective-permute-start.2
  136.5 2.0 %collective-permute-done.2 = f32[896,128]{1,0:T(8,128)S(1)} collective-permute-done((f32[896,128]{1,0:T(8,128)}, f32[896,128]{1,0:T(8,128)S(1)}, u32[]{:S(2)}, u32[]{:S(2)}) %collective-permute-start.2) | collective-permute-done | bytes 458784 | tf_op jit(solution)/shard_map/ppermute | solution.py:715
  138.5 1.9 %add.3 = f32[896,128]{1,0:T(8,128)} add(f32[896,128]{1,0:T(8,128)} %get-tuple-element.69, f32[896,128]{1,0:T(8,128)S(1)} %collective-permute-done.2) | non-fusion elementwise | flops 114688 | bytes 1376256 | tf_op jit(solution)/shard_map/add | solution.py:715
  140.3 3.6 %all-to-all-start.2 = ((f32[16,56,128]{2,1,0:T(8,128)}), f32[16,56,128]{2,1,0:T(8,128)S(1)}, u32[]{:S(2)}, u32[]{:S(2)}) async-start(f32[16,56,128]{2,1,0:T(8,128)} %bitcast.10), calls=%async_computation.2 | async-start | bytes 917504 | tf_op jit(solution)/shard_map/all_to_all | solution.py:616
  143.9 13.8 %shard_map.308 = (f32[16,128,512]{2,1,0:T(8,128)}, f32[16,128,512]{2,1,0:T(8,128)}, f32[16,128,512]{2,1,0:T(8,128)}) custom-call(s32[16]{0:T(128)} %broadcast_subtract_fusion.ends_ref, s32[1]{0:T(128)} %bitcast.origin_ref, f32[8,16,128]{2,1,0:T(8,128)} %copy-done.1, f32[16,128,512]{2,1,0:T(8,128)} %x_ref.5, f32[16,128,512]{2,1,0:T(8,128)} %res_ref.3, ...), custom_call_target="tpu_custom_call" | custom-call | flops 3221225472 | bytes 16777216 | tf_op jit(solution)/shard_map/pallas_call | solution.py:725
  157.7 0.4 all-to-all-done.2
  158.2 0.8 broadcast_in_dim.3
  159.0 6.4 %all-to-all-start.3 = ((f32[16,56,128]{2,1,0:T(8,128)}), f32[16,56,128]{2,1,0:T(8,128)S(1)}, u32[]{:S(2)}, u32[]{:S(2)}) async-start(f32[16,56,128]{2,1,0:T(8,128)} %broadcast_in_dim.3), calls=%async_computation.3 | async-start | bytes 917504 | tf_op jit(solution)/shard_map/all_to_all | solution.py:616
  165.5 13.8 %shard_map.309 = (f32[16,128,512]{2,1,0:T(8,128)}, f32[16,128,512]{2,1,0:T(8,128)}, f32[16,128,512]{2,1,0:T(8,128)}) custom-call(s32[16]{0:T(128)} %broadcast_subtract_fusion.ends_ref, s32[1]{0:T(128)} %bitcast.origin_ref, f32[8,16,128]{2,1,0:T(8,128)} %copy-done.1, ...), custom_call_target="tpu_custom_call", output_to_operand_aliasing={{0}: (17, {}), {1}: (18, {}), {2}: (19, {})} | custom-call | flops 3221225472 | bytes 16777216 | tf_op jit(solution)/shard_map/pallas_call | solution.py:725
  179.3 0.1 all-to-all-done.3
  179.3 0.0 copy-start
  179.3 0.0 collective-permute-start.3
  179.4 1.8 collective-permute-done.3.theirs_ref
  181.2 0.0 copy-done
  181.2 0.0 copy-start.2
  181.2 0.8 copy-done.2
  181.9 2.5 %shard_map.310 = (f32[512,128]{1,0:T(8,128)}, f32[1,512]{1,0:T(1,128)}, f32[1,512]{1,0:T(1,128)}, f32[1,512]{1,0:T(1,128)}, f32[1,512]{1,0:T(1,128)}, /*index=5*...) custom-call(s32[1]{0:T(128)} %bitcast.1.core_ref, ...), custom_call_target="tpu_custom_call" | custom-call | tf_op jit(solution)/shard_map/pallas_call | solution.py:756
  (1 shorter events, 0.0 us)
Async XLA Ops:
  11.5 20.1 %collective-permute-start = (f32[16,16,256]{2,1,0:T(8,128)}, f32[16,16,256]{2,1,0:T(8,128)S(1)}, u32[]{:S(2)}, u32[]{:S(2)}) collective-permute-start(f32[16,16,256]{2,1,0:T(8,128)} %get-tuple-element.60), channel_id=1, source_target_pairs={{0,4},{4,8},{8,12},{12,16},{16,20},{20,24},{24,28},{1,5},{5,9},{9,... | collective-permute-start | bytes 786440 | tf_op jit(solution)/shard_map/ppermute | solution.py:660
  16.3 15.3 %collective-permute-start.1 = (f32[16,16,256]{2,1,0:T(8,128)}, f32[16,16,256]{2,1,0:T(8,128)S(1)}, u32[]{:S(2)}, u32[]{:S(2)}) collective-permute-start(f32[16,16,256]{2,1,0:T(8,128)} %get-tuple-element.61), channel_id=1, source_target_pairs={{4,0},{8,4},{12,8},{16,12},{20,16},{24,20},{28,24},{5,1},{9,5},{13... | collective-permute-start | bytes 786440 | tf_op jit(solution)/shard_map/ppermute | solution.py:661
  31.6 0.7 copy-start.3
  31.6 0.8 copy-start.4
  74.7 10.2 %all-to-all-start.1 = ((f32[8,16,128]{2,1,0:T(8,128)}), f32[8,16,128]{2,1,0:T(8,128)S(1)}, u32[]{:S(2)}, u32[]{:S(2)}) async-start(f32[8,16,128]{2,1,0:T(8,128)} %get-tuple-element.64), calls=%async_computation.1 | async-start | bytes 131072 | tf_op jit(solution)/shard_map/all_to_all | solution.py:616
  84.9 0.6 copy-start.1
  136.4 2.1 %collective-permute-start.2 = (f32[896,128]{1,0:T(8,128)}, f32[896,128]{1,0:T(8,128)S(1)}, u32[]{:S(2)}, u32[]{:S(2)}) collective-permute-start(f32[896,128]{1,0:T(8,128)} %get-tuple-element.70), channel_id=1, source_target_pairs={{0,1},{1,0},{2,3},{3,2},{4,5},{5,4},{6,7},{7,6},{8,9},{9,8},{10,11... | collective-permute-start | bytes 1376264 | tf_op jit(solution)/shard_map/ppermute | solution.py:715
  140.3 17.8 %all-to-all-start.2 = ((f32[16,56,128]{2,1,0:T(8,128)}), f32[16,56,128]{2,1,0:T(8,128)S(1)}, u32[]{:S(2)}, u32[]{:S(2)}) async-start(f32[16,56,128]{2,1,0:T(8,128)} %bitcast.10), calls=%async_computation.2 | async-start | bytes 917504 | tf_op jit(solution)/shard_map/all_to_all | solution.py:616
  159.0 20.3 %all-to-all-start.3 = ((f32[16,56,128]{2,1,0:T(8,128)}), f32[16,56,128]{2,1,0:T(8,128)S(1)}, u32[]{:S(2)}, u32[]{:S(2)}) async-start(f32[16,56,128]{2,1,0:T(8,128)} %broadcast_in_dim.3), calls=%async_computation.3 | async-start | bytes 917504 | tf_op jit(solution)/shard_map/all_to_all | solution.py:616
  179.3 1.9 %copy-start = (f32[16,56,128]{2,1,0:T(8,128)}, f32[16,56,128]{2,1,0:T(8,128)S(1)}, u32[]{:S(2)}) copy-start(f32[16,56,128]{2,1,0:T(8,128)S(1)} %all-to-all-done.3) | copy-start | bytes 1376260
  179.3 1.8 %collective-permute-start.3 = (f32[896,128]{1,0:T(8,128)S(1)}, f32[896,128]{1,0:T(8,128)S(1)}, u32[]{:S(2)}, u32[]{:S(2)}) collective-permute-start(f32[896,128]{1,0:T(8,128)S(1)} %bitcast.26), channel_id=1, source_target_pairs={{0,1},{1,0},{2,3},{3,2},{4,5},{5,4},{6,7},{7,6},{8,9},{9,8},{10,11... | collective-permute-start | bytes 1376264 | tf_op jit(solution)/shard_map/ppermute | solution.py:750
  181.2 0.8 copy-start.2

commit v3 on v2

--- a/solution.py
+++ b/solution.py
@@ -12,9 +12,9 @@
 EPS = 1e-05
 LANE = 128
 ROWS = 64
-SECOND_ROWS = 128
+SECOND_ROWS = 32
 PIECE = 256
-THIRD_ROWS = 128
+THIRD_ROWS = 32
 F32 = jnp.float32
 BF16 = jnp.bfloat16
 VMEM_LIMIT = 60 * 1024 * 1024

time: 185 us -> 185 us (level)
  starting transfers between devices: 19.8 us -> 22.9 us
  Pallas kernels: 133 us -> 131 us
    all_to_all x3, starting transfers between devices: 13.5 us -> 16.6 us  [exchange(): return lax.all_to_all(pieces, axes, 0, 0)]
    pallas_call x1, Pallas kernels: 50.8 us -> 48.3 us  [local(): pl.pallas_call(third_kernel, grid=(items // pair,), in_specs=[ends_spec]...]
  transfers between devices with their start and end apart: 7 -> 7, of which waited for: 5 -> 4; matrix products, arithmetic and copies ran while one was open for 0% -> 0% of each run, Pallas kernels for 15% -> 15%
where the time goes in v3:
time: 185 us; the launch traced here: 186 us
  Pallas kernels  131 us (71%)
  starting transfers between devices  22.9 us (12%)
  blocking collectives  14 us (8%)
  waiting for transfers between devices  10.9 us (6%)
  other arithmetic  3.06 us (2%)
  local copies, waits for them, and re-layouts  2.96 us (2%)
    pallas_call x1, Pallas kernels, local(): pl.pallas_call(third_kernel, grid=(items // pair,), in_specs=[ends_spec]...  48.3 us
    pallas_call x1, Pallas kernels, local(): pl.pallas_call(second_kernel, grid=(items // pair,), in_specs=[ends_spec,...  42.7 us
    pallas_call x2, Pallas kernels, outer(): pl.pallas_call(functools.partial(outer_kernel, offset=offset), grid=(size...  27.6 us
    all_to_all x3, starting transfers between devices, exchange(): return lax.all_to_all(pieces, axes, 0, 0)  16.6 us
    all_to_all x1, blocking collectives, exchange(): return lax.all_to_all(pieces, axes, 0, 0)  14 us
    pallas_call x1, Pallas kernels, local(): pl.pallas_call(first_kernel, grid=(items // quad,), in_specs=[ends_spec,...  9.64 us
    all_to_all x3, waiting for transfers between devices, exchange(): return lax.all_to_all(pieces, axes, 0, 0)  7.1 us
    ppermute x1, starting transfers between devices, local(): from_left = lax.ppermute(to_right, 'blk', forward)  4.85 us
  transfers between devices with their start and end apart: 7, of which 4 were waited for; matrix products, arithmetic and copies ran while one was open for 0% of the time, Pallas kernels for 15%

profile of v3, /device:TPU:0, one launch (start us, length us, event | category | flops | bytes accessed | tf_op | source)
XLA Modules:
  0.0 185.5 jit_solution(13263930494633407404)
XLA Ops:
  0.7 1.2 broadcast_subtract_fusion.ends_ref
  1.8 9.6 %shard_map.305 = (f32[8,16,128]{2,1,0:T(8,128)}, f32[16,16,256]{2,1,0:T(8,128)}, f32[16,16,256]{2,1,0:T(8,128)}, bf16[512,512]{1,0:T(8,128)(2,1)}, bf16[768,512]{1,0:T(8,128)(2,1)}) custom-call(s32[16]{0:T(128)} %broadcast_subtract_fusion.ends_ref, f32[16,128,512]{2,1,0:T(8,128)} %x_ref.5, f32[16,128,512]{2,1,0:T(8,128)} %res_ref.3, ...), custom_call_target="tpu_custom_call" | custom-call | tf_op jit(solution)/shard_map/pallas_call | solution.py:646
  11.5 4.8 %collective-permute-start = (f32[16,16,256]{2,1,0:T(8,128)}, f32[16,16,256]{2,1,0:T(8,128)S(1)}, u32[]{:S(2)}, u32[]{:S(2)}) collective-permute-start(f32[16,16,256]{2,1,0:T(8,128)} %get-tuple-element.60), channel_id=1, source_target_pairs={{0,4},{4,8},{8,12},{12,16},{16,20},{20,24},{24,28},{1,5},{5,9},{9,... | collective-permute-start | bytes 786440 | tf_op jit(solution)/shard_map/ppermute | solution.py:660
  16.3 1.3 collective-permute-start.1
  17.6 14.0 %all_to_all.20.sums_ref = f32[8,16,128]{2,1,0:T(8,128)} all-to-all(f32[8,16,128]{2,1,0:T(8,128)} %get-tuple-element.59), channel_id=1, replica_groups=mesh['blk'=8,'side'=2,'core'=2] {'blk'}, dimensions={0} | all-to-all | bytes 131072 | tf_op jit(solution)/shard_map/all_to_all | solution.py:616
  31.6 0.0 collective-permute-done.from_left_ref
  31.6 0.0 copy-start.3
  31.6 0.0 collective-permute-done.1.from_right_ref
  31.6 0.0 copy-start.4
  31.6 0.7 copy-done.3
  32.3 0.1 copy-done.4
  32.4 42.7 %shard_map.306 = (f32[16,512,512]{2,1,0:T(8,128)}, f32[16,528,512]{2,1,0:T(8,128)}, f32[16,512,512]{2,1,0:T(8,128)}, f32[16,16,512]{2,1,0:T(8,128)}, f32[8,16,128]{2,1,0:T(8,128)}) custom-call(s32[16]{0:T(128)} %broadcast_subtract_fusion.ends_ref, s32[1]{0:T(128)} %bitcast.origin_ref, f32[8,16,128]{2,1,0:T(8,128)} %all_to_all.20.sums_ref, ...), custom_call_target="tpu_custom_call" | custom-call | flops 10737418240 | bytes 58720256 | tf_op jit(solution)/shard_map/pallas_call | solution.py:667
  75.1 3.5 %all-to-all-start.1 = ((f32[8,16,128]{2,1,0:T(8,128)}), f32[8,16,128]{2,1,0:T(8,128)S(1)}, u32[]{:S(2)}, u32[]{:S(2)}) async-start(f32[8,16,128]{2,1,0:T(8,128)} %get-tuple-element.64), calls=%async_computation.1 | async-start | bytes 131072 | tf_op jit(solution)/shard_map/all_to_all | solution.py:616
  78.6 6.7 %all-to-all-done.1.mids_ref = f32[8,16,128]{2,1,0:T(8,128)S(1)} async-done(((f32[8,16,128]{2,1,0:T(8,128)}), f32[8,16,128]{2,1,0:T(8,128)S(1)}, u32[]{:S(2)}, u32[]{:S(2)}) %all-to-all-start.1) | async-done | bytes 65568 | tf_op jit(solution)/shard_map/all_to_all | solution.py:616
  85.4 0.0 copy-start.1
  85.4 0.6 copy-done.1
  86.0 48.3 %shard_map.307 = (bf16[16,512,512]{2,1,0:T(8,128)(2,1)}, bf16[16,512,512]{2,1,0:T(8,128)(2,1)}, bf16[16,512,512]{2,1,0:T(8,128)(2,1)}, bf16[16,512,512]{2,1,0:T(...) custom-call(s32[16]{0:T(128)} %broadcast_subtract_fusion.ends_ref, s32[1]{0:T(128)} %bitcast.origin_ref, ...), custom_call_target="tpu_custom_call" | custom-call | flops 9663676416 | bytes 83886080 | tf_op jit(solution)/shard_map/pallas_call | solution.py:694
  134.3 0.1 collective-permute-start.2
  134.4 2.0 %collective-permute-done.2 = f32[896,128]{1,0:T(8,128)S(1)} collective-permute-done((f32[896,128]{1,0:T(8,128)}, f32[896,128]{1,0:T(8,128)S(1)}, u32[]{:S(2)}, u32[]{:S(2)}) %collective-permute-start.2) | collective-permute-done | bytes 458784 | tf_op jit(solution)/shard_map/ppermute | solution.py:715
  136.4 1.9 %add.3 = f32[896,128]{1,0:T(8,128)} add(f32[896,128]{1,0:T(8,128)} %get-tuple-element.69, f32[896,128]{1,0:T(8,128)S(1)} %collective-permute-done.2) | non-fusion elementwise | flops 114688 | bytes 1376256 | tf_op jit(solution)/shard_map/add | solution.py:715
  138.3 6.6 %all-to-all-start.2 = ((f32[16,56,128]{2,1,0:T(8,128)}), f32[16,56,128]{2,1,0:T(8,128)S(1)}, u32[]{:S(2)}, u32[]{:S(2)}) async-start(f32[16,56,128]{2,1,0:T(8,128)} %bitcast.10), calls=%async_computation.2 | async-start | bytes 917504 | tf_op jit(solution)/shard_map/all_to_all | solution.py:616
  144.8 13.8 %shard_map.308 = (f32[16,128,512]{2,1,0:T(8,128)}, f32[16,128,512]{2,1,0:T(8,128)}, f32[16,128,512]{2,1,0:T(8,128)}) custom-call(s32[16]{0:T(128)} %broadcast_subtract_fusion.ends_ref, s32[1]{0:T(128)} %bitcast.origin_ref, f32[8,16,128]{2,1,0:T(8,128)} %copy-done.1, f32[16,128,512]{2,1,0:T(8,128)} %x_ref.5, f32[16,128,512]{2,1,0:T(8,128)} %res_ref.3, ...), custom_call_target="tpu_custom_call" | custom-call | flops 3221225472 | bytes 16777216 | tf_op jit(solution)/shard_map/pallas_call | solution.py:725
  158.7 0.4 all-to-all-done.2
  159.1 0.8 broadcast_in_dim.3
  159.9 6.5 %all-to-all-start.3 = ((f32[16,56,128]{2,1,0:T(8,128)}), f32[16,56,128]{2,1,0:T(8,128)S(1)}, u32[]{:S(2)}, u32[]{:S(2)}) async-start(f32[16,56,128]{2,1,0:T(8,128)} %broadcast_in_dim.3), calls=%async_computation.3 | async-start | bytes 917504 | tf_op jit(solution)/shard_map/all_to_all | solution.py:616
  166.4 13.8 %shard_map.309 = (f32[16,128,512]{2,1,0:T(8,128)}, f32[16,128,512]{2,1,0:T(8,128)}, f32[16,128,512]{2,1,0:T(8,128)}) custom-call(s32[16]{0:T(128)} %broadcast_subtract_fusion.ends_ref, s32[1]{0:T(128)} %bitcast.origin_ref, f32[8,16,128]{2,1,0:T(8,128)} %copy-done.1, ...), custom_call_target="tpu_custom_call", output_to_operand_aliasing={{0}: (17, {}), {1}: (18, {}), {2}: (19, {})} | custom-call | flops 3221225472 | bytes 16777216 | tf_op jit(solution)/shard_map/pallas_call | solution.py:725
  180.2 0.0 all-to-all-done.3
  180.3 0.0 copy-start
  180.3 0.1 collective-permute-start.3
  180.3 1.8 collective-permute-done.3.theirs_ref
  182.1 0.0 copy-done
  182.2 0.0 copy-start.2
  182.2 0.8 copy-done.2
  182.9 2.5 %shard_map.310 = (f32[512,128]{1,0:T(8,128)}, f32[1,512]{1,0:T(1,128)}, f32[1,512]{1,0:T(1,128)}, f32[1,512]{1,0:T(1,128)}, f32[1,512]{1,0:T(1,128)}, /*index=5*...) custom-call(s32[1]{0:T(128)} %bitcast.1.core_ref, ...), custom_call_target="tpu_custom_call" | custom-call | tf_op jit(solution)/shard_map/pallas_call | solution.py:756
  (1 shorter events, 0.0 us)
Async XLA Ops:
  11.5 20.1 %collective-permute-start = (f32[16,16,256]{2,1,0:T(8,128)}, f32[16,16,256]{2,1,0:T(8,128)S(1)}, u32[]{:S(2)}, u32[]{:S(2)}) collective-permute-start(f32[16,16,256]{2,1,0:T(8,128)} %get-tuple-element.60), channel_id=1, source_target_pairs={{0,4},{4,8},{8,12},{12,16},{16,20},{20,24},{24,28},{1,5},{5,9},{9,... | collective-permute-start | bytes 786440 | tf_op jit(solution)/shard_map/ppermute | solution.py:660
  16.3 15.3 %collective-permute-start.1 = (f32[16,16,256]{2,1,0:T(8,128)}, f32[16,16,256]{2,1,0:T(8,128)S(1)}, u32[]{:S(2)}, u32[]{:S(2)}) collective-permute-start(f32[16,16,256]{2,1,0:T(8,128)} %get-tuple-element.61), channel_id=1, source_target_pairs={{4,0},{8,4},{12,8},{16,12},{20,16},{24,20},{28,24},{5,1},{9,5},{13... | collective-permute-start | bytes 786440 | tf_op jit(solution)/shard_map/ppermute | solution.py:661
  31.6 0.7 copy-start.3
  31.6 0.8 copy-start.4
  75.1 10.3 %all-to-all-start.1 = ((f32[8,16,128]{2,1,0:T(8,128)}), f32[8,16,128]{2,1,0:T(8,128)S(1)}, u32[]{:S(2)}, u32[]{:S(2)}) async-start(f32[8,16,128]{2,1,0:T(8,128)} %get-tuple-element.64), calls=%async_computation.1 | async-start | bytes 131072 | tf_op jit(solution)/shard_map/all_to_all | solution.py:616
  85.4 0.6 copy-start.1
  134.3 2.1 %collective-permute-start.2 = (f32[896,128]{1,0:T(8,128)}, f32[896,128]{1,0:T(8,128)S(1)}, u32[]{:S(2)}, u32[]{:S(2)}) collective-permute-start(f32[896,128]{1,0:T(8,128)} %get-tuple-element.70), channel_id=1, source_target_pairs={{0,1},{1,0},{2,3},{3,2},{4,5},{5,4},{6,7},{7,6},{8,9},{9,8},{10,11... | collective-permute-start | bytes 1376264 | tf_op jit(solution)/shard_map/ppermute | solution.py:715
  138.3 20.8 %all-to-all-start.2 = ((f32[16,56,128]{2,1,0:T(8,128)}), f32[16,56,128]{2,1,0:T(8,128)S(1)}, u32[]{:S(2)}, u32[]{:S(2)}) async-start(f32[16,56,128]{2,1,0:T(8,128)} %bitcast.10), calls=%async_computation.2 | async-start | bytes 917504 | tf_op jit(solution)/shard_map/all_to_all | solution.py:616
  159.9 20.4 %all-to-all-start.3 = ((f32[16,56,128]{2,1,0:T(8,128)}), f32[16,56,128]{2,1,0:T(8,128)S(1)}, u32[]{:S(2)}, u32[]{:S(2)}) async-start(f32[16,56,128]{2,1,0:T(8,128)} %broadcast_in_dim.3), calls=%async_computation.3 | async-start | bytes 917504 | tf_op jit(solution)/shard_map/all_to_all | solution.py:616
  180.3 1.9 %copy-start = (f32[16,56,128]{2,1,0:T(8,128)}, f32[16,56,128]{2,1,0:T(8,128)S(1)}, u32[]{:S(2)}) copy-start(f32[16,56,128]{2,1,0:T(8,128)S(1)} %all-to-all-done.3) | copy-start | bytes 1376260
  180.3 1.9 %collective-permute-start.3 = (f32[896,128]{1,0:T(8,128)S(1)}, f32[896,128]{1,0:T(8,128)S(1)}, u32[]{:S(2)}, u32[]{:S(2)}) collective-permute-start(f32[896,128]{1,0:T(8,128)S(1)} %bitcast.26), channel_id=1, source_target_pairs={{0,1},{1,0},{2,3},{3,2},{4,5},{5,4},{6,7},{7,6},{8,9},{9,8},{10,11... | collective-permute-start | bytes 1376264 | tf_op jit(solution)/shard_map/ppermute | solution.py:750
  182.2 0.8 copy-start.2

commit v4 on v3

--- a/solution.py
+++ b/solution.py
@@ -12,7 +12,7 @@
 EPS = 1e-05
 LANE = 128
 ROWS = 64
-SECOND_ROWS = 32
+SECOND_ROWS = 128
 PIECE = 256
 THIRD_ROWS = 32
 F32 = jnp.float32
@@ -80,7 +80,7 @@
 
 
 def first_kernel(
-    ends_ref, x_ref, res_l_ref, res_r_ref, skip_l_ref, skip_r_ref, w_in_ref, bias_ref, slope_ref,
+    lengths_ref, origin_ref, x_ref, res_l_ref, res_r_ref, skip_l_ref, skip_r_ref, w_in_ref, bias_ref, slope_ref,
     w_res_ref, w_skip_ref, gain_ref,
     sums_ref, left_ref, right_ref, w_cat_ref, w_out_ref,
 ):
@@ -107,7 +107,7 @@
     step = min(PIECE, frames)
     for number in range(group):
         item = pl.program_id(0) * group + number
-        end = ends_ref[item]
+        end = lengths_ref[item] - origin_ref[0]
         first = second = jnp.zeros((8, LANE), F32)
         for start in range(0, frames, step):
             xt = x_ref[number, :, start : start + step].astype(BF16).T
@@ -165,11 +165,11 @@
     return value if valid is None else jnp.where(valid, value, 0.0)
 
 
-def counts(ends_ref, origin_ref, items, width):
+def counts(lengths_ref, items, width):
     row = lax.broadcasted_iota(jnp.int32, (items, 1), 0)
     lengths = jnp.zeros((items, 1), jnp.int32)
     for item in range(items):
-        lengths = jnp.where(row == item, ends_ref[item] + origin_ref[0], lengths)
+        lengths = jnp.where(row == item, lengths_ref[item], lengths)
     return lengths.astype(F32) * float(width)
 
 
@@ -181,9 +181,9 @@
 
 
 def second_kernel(
-    ends_ref, origin_ref, sums_ref, from_left_ref, from_right_ref, x_all, res_all, skip_all,
+    lengths_ref, origin_ref, sums_ref, from_left_ref, from_right_ref, x_all, res_all, skip_all,
     w_cat_ref, w_out_ref, slope_ref, gain_ref, shift_ref, taps_ref, tap_bias_ref, slope_mid_ref,
-    half_all, mid_all, back_all, edge_ref, out_ref,
+    half_all, mid_all, back_all, edge_ref, out_ref, d_high_ref, d_low_ref, x_high_ref, x_low_ref, cot_ref,
     halo_ref, normal_ref, coef_ref,
 ):
     items = out_ref.shape[1]
@@ -193,7 +193,7 @@
 
     @pl.when(pl.program_id(0) == 0)
     def _():
-        mean, scale = first_norm(sums_ref, counts(ends_ref, origin_ref, items, width))
+        mean, scale = first_norm(sums_ref, counts(lengths_ref, items, width))
         coef_ref[0] = jnp.broadcast_to(scale, (items, LANE))
         coef_ref[1] = jnp.broadcast_to(scale * mean, (items, LANE))
         for side, ref in enumerate((from_left_ref, from_right_ref)):
@@ -210,11 +210,23 @@
         half_ref, res_ref, skip_ref, mid_ref, back_ref = (
             ref.at[number : number + 1] for ref in (half_all, res_all, skip_all, mid_all, back_all)
         )
-        high, low = split(x_all[number].T)
+        x_high, x_low = split(x_all[number])
+        x_high_ref[number] = x_high
+        x_low_ref[number] = x_low
+        high, low = x_high.T, x_low.T
         ones = jnp.ones((frames, LANE), BF16)
         half_ref[0] = product(jnp.concatenate([high, low, high, ones], axis=1), w_cat_ref[...])
         rows = SECOND_ROWS if full and frames % SECOND_ROWS == 0 else ROWS
-        d_high, d_low = split(jnp.concatenate([res_ref[0], skip_ref[0]], axis=0))
+        both = jnp.concatenate([res_ref[0], skip_ref[0]], axis=0)
+        lane = lax.broadcasted_iota(jnp.int32, (1, LANE), 1)
+        cots = jnp.zeros((2 * cin, LANE), F32)
+        for lanes in lane_tiles(frames):
+            piece = both[:, lanes]
+            cots = cots + (piece if full else jnp.where(lane + lanes.start < end, piece, 0.0))
+        cot_ref[number] = cots
+        d_high, d_low = split(both)
+        d_high_ref[number] = d_high
+        d_low_ref[number] = d_low
         high, low = d_high.T, d_low.T
         back_ref[0] = product(jnp.concatenate([high, low, high], axis=1), w_out_ref[...])
 
@@ -304,7 +316,7 @@
 
     for number in range(group):
         item = pl.program_id(0) * group + number
-        end = ends_ref[item]
+        end = lengths_ref[item] - origin_ref[0]
         both_ways(end >= frames, functools.partial(run, number, item, end))
 
 
@@ -330,19 +342,20 @@
 
 
 def third_kernel(
-    ends_ref, origin_ref, core_ref, sums_ref, mids_ref, x_all, res_all, skip_all, half_all, mid_all, back_all, edge_all,
+    lengths_ref, origin_ref, core_ref, sums_ref, mids_ref, x_high_all, x_low_all, d_high_all, d_low_all, cots_all,
+    half_all, mid_all, back_all, edge_all,
     slope_ref, gain_ref, shift_ref, taps_ref, slope_mid_ref,
     r_high_all, r_low_all, u_high_all, u_low_all, keep_ref, send_ref,
     grad_ref, coef_ref, vector_ref, grads_ref, cot_ref,
 ):
     items = coef_ref.shape[1]
-    group, cin, frames = x_all.shape
+    group, cin, frames = x_high_all.shape
     width = half_all.shape[2]
     origin = origin_ref[0]
 
     @pl.when(pl.program_id(0) == 0)
     def _():
-        count = counts(ends_ref, origin_ref, items, width)
+        count = counts(lengths_ref, items, width)
         mean1, scale1 = first_norm(sums_ref, count)
         m, mean2, scale2 = second_norm(mids_ref, count)
         beta = scale2 * scale2 * (2.0 * m[3] - mean2 * m[2]) / count
@@ -360,8 +373,8 @@
         cot_ref[...] = jnp.zeros(cot_ref.shape, F32)
 
     def run(number, item, end, full):
-        x_ref, res_ref, skip_ref, half_ref, mid_ref, back_ref, edge_ref = (
-            ref.at[number : number + 1] for ref in (x_all, res_all, skip_all, half_all, mid_all, back_all, edge_all)
+        half_ref, mid_ref, back_ref, edge_ref = (
+            ref.at[number : number + 1] for ref in (half_all, mid_all, back_all, edge_all)
         )
         r_high_ref, r_low_ref, u_high_ref, u_low_ref = (
             ref.at[number : number + 1] for ref in (r_high_all, r_low_all, u_high_all, u_low_all)
@@ -369,13 +382,8 @@
         rows = THIRD_ROWS if full else ROWS
         coefs = [tile(coef_ref[number, pl.ds(item, 1), :]) for number in range(8)]
         scale1, scale_mean1, dp_a, dp_b, scale2, dr_a, dr_b, z_a = coefs
-        both = jnp.concatenate([res_ref[0], skip_ref[0]], axis=0)
-        d_high, d_low = split(both)
-        lane = lax.broadcasted_iota(jnp.int32, (1, LANE), 1)
-        cots = jnp.zeros((2 * cin, LANE), F32)
-        for lanes in lane_tiles(frames):
-            piece = both[:, lanes]
-            cots = cots + (piece if full else jnp.where(lane + lanes.start < end, piece, 0.0))
+        d_high, d_low = d_high_all[number], d_low_all[number]
+        cots = cots_all[number]
         cot_ref[0] += cots
         cot_ref[1] += z_a[0:1] * cots
 
@@ -464,7 +472,7 @@
         for lanes in lane_tiles(width):
             grads_ref[0 : 2 * cin, lanes] += z_0 * mixed[:, lanes]
         u_high, u_low = u_high_ref[0], u_low_ref[0]
-        x_high, x_low = split(x_ref[0])
+        x_high, x_low = x_high_all[number], x_low_all[number]
         rows_of = jnp.concatenate([x_high, x_low, x_high], axis=1)
         ones = jnp.ones((GRAD_ROWS, frames), BF16)
         ones = jnp.concatenate([ones, jnp.zeros((GRAD_ROWS, frames), BF16), ones], axis=1)
@@ -474,7 +482,7 @@
 
     for number in range(group):
         item = pl.program_id(0) * group + number
-        end = ends_ref[item]
+        end = lengths_ref[item] - origin_ref[0]
         both_ways(end >= frames, functools.partial(run, number, item, end))
 
     @pl.when(pl.program_id(0) == items // group - 1)
@@ -499,7 +507,7 @@
 
 
 def outer_kernel(
-    ends_ref, origin_ref, mids_ref, x_ref, res_ref, r_high_ref, r_low_ref, u_high_ref, u_low_ref,
+    lengths_ref, origin_ref, mids_ref, x_ref, res_ref, r_high_ref, r_low_ref, u_high_ref, u_low_ref,
     w_cat_ref, w_out_ref, w_res_ref, w_skip_ref, gain_ref, shift_ref, bias_res_ref, bias_skip_ref, *rest_refs, offset,
 ):
     res_out_ref, skip_out_ref, x_grad_ref, coef_ref, column_ref, out_turned_ref, in_turned_ref = rest_refs[-7:]
@@ -509,7 +517,7 @@
 
     @pl.when(pl.program_id(0) == 0)
     def _():
-        _, mean, scale = second_norm(mids_ref, counts(ends_ref, origin_ref, items, width))
+        _, mean, scale = second_norm(mids_ref, counts(lengths_ref, items, width))
         coef_ref[0] = jnp.broadcast_to(2.0 * scale, (items, LANE))
         coef_ref[1] = jnp.broadcast_to(scale * mean, (items, LANE))
         high, low = w_out_ref[0 : 2 * cin].T, w_out_ref[4 * cin : 6 * cin].T
@@ -528,7 +536,7 @@
     lane = lax.broadcasted_iota(jnp.int32, (1, LANE), 1)
     for number in range(group):
         item = offset + pl.program_id(0) * group + number
-        end = ends_ref[item]
+        end = lengths_ref[item] - origin_ref[0]
         z_0, z_a = coef_ref[0, pl.ds(item, 1), :], coef_ref[1, pl.ds(item, 1), :]
         r_high, r_low = r_high_ref[number], r_low_ref[number]
         out = product(jnp.concatenate([r_high, r_low, r_high], axis=1), out_turned_ref[...]).T
@@ -586,9 +594,7 @@
             place_half(theirs_ref, 1 - core)
 
 
-def whole(array, space=pltpu.VMEM):
-    if space is pltpu.SMEM:
-        return pl.BlockSpec(memory_space=pltpu.SMEM)
+def whole(array):
     return pl.BlockSpec(array.shape, lambda item: (0,) * len(array.shape))
 
 
@@ -625,7 +631,6 @@
     blocks = lax.axis_size("blk")
     origin = (lax.axis_index("blk") * frames).astype(jnp.int32).reshape(1)
     core = lax.axis_index("core").astype(jnp.int32).reshape(1)
-    ends = lengths - origin[0]
     bias_in, slope_in, gain_in, shift_in, tap_bias, slope_mid, gain_mid, shift_mid, bias_res, bias_skip = (
         vector.reshape(1, -1)
         for vector in (
@@ -633,7 +638,7 @@
         )
     )
     taps = depthwise_weight.T
-    ends_spec = whole(ends, pltpu.SMEM)
+    ends_spec = pl.BlockSpec(memory_space=pltpu.SMEM)
 
     half = sds(items, frames, width)
     halo = sds(items, HALO, 2 * cin)
@@ -646,13 +651,13 @@
     first_sums, to_left, to_right, w_cat, w_out = pl.pallas_call(
         first_kernel,
         grid=(items // quad,),
-        in_specs=[ends_spec, per_item(inputs, quad)]
+        in_specs=[ends_spec, ends_spec, per_item(inputs, quad)]
         + [edge_block(array, quad, spot) for array in (cot_res, cot_skip) for spot in (0, last)]
         + [whole(array) for array in weights],
         out_specs=[whole(sums), per_item(halo, quad), per_item(halo, quad), whole(w_cat), whole(w_out)],
         out_shape=[sums, halo, halo, w_cat, w_out],
         compiler_params=params(),
-    )(ends, inputs, cot_res, cot_res, cot_skip, cot_skip, *weights)
+    )(lengths, origin, inputs, cot_res, cot_res, cot_skip, cot_skip, *weights)
 
     forward = [(block, block + 1) for block in range(blocks - 1)]
     backward = [(target, source) for source, target in forward]
@@ -664,15 +669,20 @@
     small = (first_sums, from_left, from_right)
     weights = (w_cat, w_out, slope_in, gain_in, shift_in, taps, tap_bias, slope_mid)
     rounded = sds(items, frames, width, dtype=BF16)
-    half, mid, back, edge, mid_sums = pl.pallas_call(
+    kept = (
+        sds(items, 2 * cin, frames, dtype=BF16), sds(items, 2 * cin, frames, dtype=BF16),
+        sds(items, cin, frames, dtype=BF16), sds(items, cin, frames, dtype=BF16), sds(items, 2 * cin, LANE),
+    )
+    half, mid, back, edge, mid_sums, d_high, d_low, x_high, x_low, cots = pl.pallas_call(
         second_kernel,
         grid=(items // pair,),
         in_specs=[ends_spec, ends_spec]
         + [whole(array) for array in small]
         + [per_item(array, pair) for array in (inputs, cot_res, cot_skip)]
         + [whole(array) for array in weights],
-        out_specs=[per_item(half, pair), per_item(mid, pair), per_item(half, pair), whole(edge), whole(sums)],
-        out_shape=[half, mid, half, edge, sums],
+        out_specs=[per_item(half, pair), per_item(mid, pair), per_item(half, pair), whole(edge), whole(sums)]
+        + [per_item(array, pair) for array in kept],
+        out_shape=[half, mid, half, edge, sums, *kept],
         scratch_shapes=[
             pltpu.VMEM((2, items, HALO, width), F32),
             pltpu.VMEM((frames + 2 * HALO, width), F32),
@@ -680,11 +690,11 @@
         ],
         compiler_params=params(),
         cost_estimate=cost(20 * items * frames * cin * width, items * frames * width * 14),
-    )(ends, origin, *small, inputs, cot_res, cot_skip, *weights)
+    )(lengths, origin, *small, inputs, cot_res, cot_skip, *weights)
     mid_sums = exchange(mid_sums, "blk")
 
     small = (first_sums, mid_sums)
-    large = (inputs, cot_res, cot_skip, half, mid, back, edge)
+    large = (x_high, x_low, d_high, d_low, cots, half, mid, back, edge)
     weights = (slope_in, gain_in, shift_in, taps, slope_mid)
     wide = sds(*inputs.shape)
     height = 3 * cin + GRAD_ROWS
@@ -709,7 +719,7 @@
         ],
         compiler_params=params(),
         cost_estimate=cost(18 * items * frames * cin * width, items * frames * width * 20),
-    )(ends, origin, core, *small, *large, *weights)
+    )(lengths, origin, core, *small, *large, *weights)
 
     swap = [(0, 1), (1, 0)]
     keep = keep + lax.ppermute(send, "core", swap)
@@ -740,7 +750,7 @@
             input_output_aliases={17: 0, 18: 1, 19: 2} if earlier else {},
             compiler_params=params(),
             cost_estimate=cost(12 * size * frames * cin * width, size * frames * width * 8),
-        )(ends, origin, mid_sums, *large, *weights, *earlier)
+        )(lengths, origin, mid_sums, *large, *weights, *earlier)
 
     residual_out, skip_out, grad_inputs = outer(0, count, ())
     pieces, residual_out = lax.optimization_barrier((pieces, residual_out))

time: 185 us -> 185 us (level); the launches traced: 186 us -> 184 us
  no operation moved by 1% of the time
where the time goes in v4:
time: 185 us; the launch traced here: 184 us
  Pallas kernels  132 us (71%)
  starting transfers between devices  21.2 us (11%)
  blocking collectives  14 us (8%)
  waiting for transfers between devices  11.1 us (6%)
  local copies, waits for them, and re-layouts  2.96 us (2%)
  other arithmetic  1.89 us (1%)
    pallas_call x1, Pallas kernels, local(): pl.pallas_call(third_kernel, grid=(items // pair,), in_specs=[ends_spec]...  48.2 us
    pallas_call x1, Pallas kernels, local(): pl.pallas_call(second_kernel, grid=(items // pair,), in_specs=[ends_spec,...  43.7 us
    pallas_call x2, Pallas kernels, outer(): pl.pallas_call(functools.partial(outer_kernel, offset=offset), grid=(size...  27.6 us
    all_to_all x3, starting transfers between devices, exchange(): return lax.all_to_all(pieces, axes, 0, 0)  14.9 us
    all_to_all x1, blocking collectives, exchange(): return lax.all_to_all(pieces, axes, 0, 0)  14 us
    pallas_call x1, Pallas kernels, local(): pl.pallas_call(first_kernel, grid=(items // quad,), in_specs=[ends_spec,...  9.64 us
    all_to_all x3, waiting for transfers between devices, exchange(): return lax.all_to_all(pieces, axes, 0, 0)  7.25 us
    ppermute x1, starting transfers between devices, local(): from_left = lax.ppermute(to_right, 'blk', forward)  4.88 us
  transfers between devices with their start and end apart: 7, of which 4 were waited for; matrix products, arithmetic and copies ran while one was open for 0% of the time, Pallas kernels for 15%

profile of v4, /device:TPU:0, one launch (start us, length us, event | category | flops | bytes accessed | tf_op | source)
XLA Modules:
  0.0 183.7 jit_solution(18331476897463972947)
XLA Ops:
  0.7 9.6 %shard_map.305 = (f32[8,16,128]{2,1,0:T(8,128)}, f32[16,16,256]{2,1,0:T(8,128)}, f32[16,16,256]{2,1,0:T(8,128)}, bf16[512,512]{1,0:T(8,128)(2,1)}, bf16[768,512]{1,0:T(8,128)(2,1)}) custom-call(s32[16]{0:T(128)} %lengths_ref.9, s32[1]{0:T(128)} %bitcast.origin_ref, f32[16,128,512]{2,1,0:T(8,128)} %x_ref.5, f32[16,128,512]{2,1,0:T(8,128)} %res_ref.3, ...), custom_call_target="tpu_custom_call" | custom-call | tf_op jit(solution)/shard_map/pallas_call | solution.py:651
  10.3 4.9 %collective-permute-start = (f32[16,16,256]{2,1,0:T(8,128)}, f32[16,16,256]{2,1,0:T(8,128)S(1)}, u32[]{:S(2)}, u32[]{:S(2)}) collective-permute-start(f32[16,16,256]{2,1,0:T(8,128)} %get-tuple-element.65), channel_id=1, source_target_pairs={{0,4},{4,8},{8,12},{12,16},{16,20},{20,24},{24,28},{1,5},{5,9},{9,... | collective-permute-start | bytes 786440 | tf_op jit(solution)/shard_map/ppermute | solution.py:665
  15.2 1.3 collective-permute-start.1
  16.5 14.0 %all_to_all.20.sums_ref = f32[8,16,128]{2,1,0:T(8,128)} all-to-all(f32[8,16,128]{2,1,0:T(8,128)} %get-tuple-element.64), channel_id=1, replica_groups=mesh['blk'=8,'side'=2,'core'=2] {'blk'}, dimensions={0} | all-to-all | bytes 131072 | tf_op jit(solution)/shard_map/all_to_all | solution.py:622
  30.5 0.0 collective-permute-done.from_left_ref
  30.5 0.0 copy-start.3
  30.5 0.0 collective-permute-done.1.from_right_ref
  30.5 0.0 copy-start.4
  30.5 0.7 copy-done.3
  31.2 0.1 copy-done.4
  31.3 43.7 %shard_map.306 = (f32[16,512,512]{2,1,0:T(8,128)}, f32[16,528,512]{2,1,0:T(8,128)}, f32[16,512,512]{2,1,0:T(8,128)}, f32[16,16,512]{2,1,0:T(8,128)}, f32[8,16,12...) custom-call(s32[16]{0:T(128)} %lengths_ref.9, ...), custom_call_target="tpu_custom_call" | custom-call | flops 10737418240 | bytes 58720256 | tf_op jit(solution)/shard_map/pallas_call | solution.py:676
  75.0 4.2 %all-to-all-start.1 = ((f32[8,16,128]{2,1,0:T(8,128)}), f32[8,16,128]{2,1,0:T(8,128)S(1)}, u32[]{:S(2)}, u32[]{:S(2)}) async-start(f32[8,16,128]{2,1,0:T(8,128)} %get-tuple-element.69), calls=%async_computation.1 | async-start | bytes 131072 | tf_op jit(solution)/shard_map/all_to_all | solution.py:622
  79.1 6.9 %all-to-all-done.1.mids_ref = f32[8,16,128]{2,1,0:T(8,128)S(1)} async-done(((f32[8,16,128]{2,1,0:T(8,128)}), f32[8,16,128]{2,1,0:T(8,128)S(1)}, u32[]{:S(2)}, u32[]{:S(2)}) %all-to-all-start.1) | async-done | bytes 65568 | tf_op jit(solution)/shard_map/all_to_all | solution.py:622
  86.1 0.0 copy-start.1
  86.1 0.6 copy-done.1
  86.7 48.2 %shard_map.307 = (bf16[16,512,512]{2,1,0:T(8,128)(2,1)}, bf16[16,512,512]{2,1,0:T(8,128)(2,1)}, bf16[16,512,512]{2,1,0:T(8,128)(2,1)}, bf16[16,512,512]{2,1,0:T(...) custom-call(s32[16]{0:T(128)} %lengths_ref.9, s32[1]{0:T(128)} %bitcast.origin_ref, s32[1]{0:T(128)} %bitcast.1.core_ref, ...), custom_call_target="tpu_custom_call" | custom-call | flops 9663676416 | bytes 83886080 | tf_op jit(solution)/shard_map/pallas_call | solution.py:704
  134.9 0.1 collective-permute-start.2
  134.9 2.0 %collective-permute-done.2 = f32[896,128]{1,0:T(8,128)S(1)} collective-permute-done((f32[896,128]{1,0:T(8,128)}, f32[896,128]{1,0:T(8,128)S(1)}, u32[]{:S(2)}, u32[]{:S(2)}) %collective-permute-start.2) | collective-permute-done | bytes 458784 | tf_op jit(solution)/shard_map/ppermute | solution.py:725
  137.0 1.9 %add.3 = f32[896,128]{1,0:T(8,128)} add(f32[896,128]{1,0:T(8,128)} %get-tuple-element.79, f32[896,128]{1,0:T(8,128)S(1)} %collective-permute-done.2) | non-fusion elementwise | flops 114688 | bytes 1376256 | tf_op jit(solution)/shard_map/add | solution.py:725
  138.8 4.2 %all-to-all-start.2 = ((f32[16,56,128]{2,1,0:T(8,128)}), f32[16,56,128]{2,1,0:T(8,128)S(1)}, u32[]{:S(2)}, u32[]{:S(2)}) async-start(f32[16,56,128]{2,1,0:T(8,128)} %bitcast.10), calls=%async_computation.2 | async-start | bytes 917504 | tf_op jit(solution)/shard_map/all_to_all | solution.py:622
  143.0 13.8 %shard_map.308 = (f32[16,128,512]{2,1,0:T(8,128)}, f32[16,128,512]{2,1,0:T(8,128)}, f32[16,128,512]{2,1,0:T(8,128)}) custom-call(s32[16]{0:T(128)} %lengths_ref.9, s32[1]{0:T(128)} %bitcast.origin_ref, f32[8,16,128]{2,1,0:T(8,128)} %copy-done.1, f32[16,128,512]{2,1,0:T(8,128)} %x_ref.5, f32[16,128,512]{2,1,0:T(8,128)} %res_ref.3, ...), custom_call_target="tpu_custom_call" | custom-call | flops 3221225472 | bytes 16777216 | tf_op jit(solution)/shard_map/pallas_call | solution.py:735
  156.8 0.3 all-to-all-done.2
  157.2 0.8 broadcast_in_dim.3
  158.0 6.6 %all-to-all-start.3 = ((f32[16,56,128]{2,1,0:T(8,128)}), f32[16,56,128]{2,1,0:T(8,128)S(1)}, u32[]{:S(2)}, u32[]{:S(2)}) async-start(f32[16,56,128]{2,1,0:T(8,128)} %broadcast_in_dim.3), calls=%async_computation.3 | async-start | bytes 917504 | tf_op jit(solution)/shard_map/all_to_all | solution.py:622
  164.6 13.8 %shard_map.309 = (f32[16,128,512]{2,1,0:T(8,128)}, f32[16,128,512]{2,1,0:T(8,128)}, f32[16,128,512]{2,1,0:T(8,128)}) custom-call(s32[16]{0:T(128)} %lengths_ref.9, s32[1]{0:T(128)} %bitcast.origin_ref, f32[8,16,128]{2,1,0:T(8,128)} %copy-done.1, f32[16,128,512]{2,1,0:T(8,128)} %x_ref.5, ...), custom_call_target="tpu_custom_call", output_to_operand_aliasing={{0}: (17, {}), {1}: (18, {}), {2}: (19, {})} | custom-call | flops 3221225472 | bytes 16777216 | tf_op jit(solution)/shard_map/pallas_call | solution.py:735
  178.4 0.0 all-to-all-done.3
  178.4 0.0 copy-start
  178.4 0.1 collective-permute-start.3
  178.5 1.8 collective-permute-done.3.theirs_ref
  180.3 0.0 copy-done
  180.3 0.0 copy-start.2
  180.3 0.8 copy-done.2
  181.0 2.5 %shard_map.310 = (f32[512,128]{1,0:T(8,128)}, f32[1,512]{1,0:T(1,128)}, f32[1,512]{1,0:T(1,128)}, f32[1,512]{1,0:T(1,128)}, f32[1,512]{1,0:T(1,128)}, /*index=5*...) custom-call(s32[1]{0:T(128)} %bitcast.1.core_ref, ...), custom_call_target="tpu_custom_call" | custom-call | tf_op jit(solution)/shard_map/pallas_call | solution.py:766
  (1 shorter events, 0.0 us)
Async XLA Ops:
  10.3 20.2 %collective-permute-start = (f32[16,16,256]{2,1,0:T(8,128)}, f32[16,16,256]{2,1,0:T(8,128)S(1)}, u32[]{:S(2)}, u32[]{:S(2)}) collective-permute-start(f32[16,16,256]{2,1,0:T(8,128)} %get-tuple-element.65), channel_id=1, source_target_pairs={{0,4},{4,8},{8,12},{12,16},{16,20},{20,24},{24,28},{1,5},{5,9},{9,... | collective-permute-start | bytes 786440 | tf_op jit(solution)/shard_map/ppermute | solution.py:665
  15.2 15.3 %collective-permute-start.1 = (f32[16,16,256]{2,1,0:T(8,128)}, f32[16,16,256]{2,1,0:T(8,128)S(1)}, u32[]{:S(2)}, u32[]{:S(2)}) collective-permute-start(f32[16,16,256]{2,1,0:T(8,128)} %get-tuple-element.66), channel_id=1, source_target_pairs={{4,0},{8,4},{12,8},{16,12},{20,16},{24,20},{28,24},{5,1},{9,5},{13... | collective-permute-start | bytes 786440 | tf_op jit(solution)/shard_map/ppermute | solution.py:666
  30.5 0.7 copy-start.3
  30.5 0.8 copy-start.4
  75.0 11.1 %all-to-all-start.1 = ((f32[8,16,128]{2,1,0:T(8,128)}), f32[8,16,128]{2,1,0:T(8,128)S(1)}, u32[]{:S(2)}, u32[]{:S(2)}) async-start(f32[8,16,128]{2,1,0:T(8,128)} %get-tuple-element.69), calls=%async_computation.1 | async-start | bytes 131072 | tf_op jit(solution)/shard_map/all_to_all | solution.py:622
  86.1 0.6 copy-start.1
  134.9 2.1 %collective-permute-start.2 = (f32[896,128]{1,0:T(8,128)}, f32[896,128]{1,0:T(8,128)S(1)}, u32[]{:S(2)}, u32[]{:S(2)}) collective-permute-start(f32[896,128]{1,0:T(8,128)} %get-tuple-element.80), channel_id=1, source_target_pairs={{0,1},{1,0},{2,3},{3,2},{4,5},{5,4},{6,7},{7,6},{8,9},{9,8},{10,11... | collective-permute-start | bytes 1376264 | tf_op jit(solution)/shard_map/ppermute | solution.py:725
  138.8 18.3 %all-to-all-start.2 = ((f32[16,56,128]{2,1,0:T(8,128)}), f32[16,56,128]{2,1,0:T(8,128)S(1)}, u32[]{:S(2)}, u32[]{:S(2)}) async-start(f32[16,56,128]{2,1,0:T(8,128)} %bitcast.10), calls=%async_computation.2 | async-start | bytes 917504 | tf_op jit(solution)/shard_map/all_to_all | solution.py:622
  158.0 20.4 %all-to-all-start.3 = ((f32[16,56,128]{2,1,0:T(8,128)}), f32[16,56,128]{2,1,0:T(8,128)S(1)}, u32[]{:S(2)}, u32[]{:S(2)}) async-start(f32[16,56,128]{2,1,0:T(8,128)} %broadcast_in_dim.3), calls=%async_computation.3 | async-start | bytes 917504 | tf_op jit(solution)/shard_map/all_to_all | solution.py:622
  178.4 1.9 %copy-start = (f32[16,56,128]{2,1,0:T(8,128)}, f32[16,56,128]{2,1,0:T(8,128)S(1)}, u32[]{:S(2)}) copy-start(f32[16,56,128]{2,1,0:T(8,128)S(1)} %all-to-all-done.3) | copy-start | bytes 1376260
  178.4 1.9 %collective-permute-start.3 = (f32[896,128]{1,0:T(8,128)S(1)}, f32[896,128]{1,0:T(8,128)S(1)}, u32[]{:S(2)}, u32[]{:S(2)}) collective-permute-start(f32[896,128]{1,0:T(8,128)S(1)} %bitcast.26), channel_id=1, source_target_pairs={{0,1},{1,0},{2,3},{3,2},{4,5},{5,4},{6,7},{7,6},{8,9},{9,8},{10,11... | collective-permute-start | bytes 1376264 | tf_op jit(solution)/shard_map/ppermute | solution.py:760
  180.3 0.8 copy-start.2

commit v5 on v3

--- a/solution.py
+++ b/solution.py
@@ -12,7 +12,7 @@
 EPS = 1e-05
 LANE = 128
 ROWS = 64
-SECOND_ROWS = 32
+SECOND_ROWS = 128
 PIECE = 256
 THIRD_ROWS = 32
 F32 = jnp.float32
@@ -80,7 +80,7 @@
 
 
 def first_kernel(
-    ends_ref, x_ref, res_l_ref, res_r_ref, skip_l_ref, skip_r_ref, w_in_ref, bias_ref, slope_ref,
+    lengths_ref, origin_ref, x_ref, res_l_ref, res_r_ref, skip_l_ref, skip_r_ref, w_in_ref, bias_ref, slope_ref,
     w_res_ref, w_skip_ref, gain_ref,
     sums_ref, left_ref, right_ref, w_cat_ref, w_out_ref,
 ):
@@ -107,7 +107,7 @@
     step = min(PIECE, frames)
     for number in range(group):
         item = pl.program_id(0) * group + number
-        end = ends_ref[item]
+        end = lengths_ref[item] - origin_ref[0]
         first = second = jnp.zeros((8, LANE), F32)
         for start in range(0, frames, step):
             xt = x_ref[number, :, start : start + step].astype(BF16).T
@@ -165,11 +165,11 @@
     return value if valid is None else jnp.where(valid, value, 0.0)
 
 
-def counts(ends_ref, origin_ref, items, width):
+def counts(lengths_ref, items, width):
     row = lax.broadcasted_iota(jnp.int32, (items, 1), 0)
     lengths = jnp.zeros((items, 1), jnp.int32)
     for item in range(items):
-        lengths = jnp.where(row == item, ends_ref[item] + origin_ref[0], lengths)
+        lengths = jnp.where(row == item, lengths_ref[item], lengths)
     return lengths.astype(F32) * float(width)
 
 
@@ -181,7 +181,7 @@
 
 
 def second_kernel(
-    ends_ref, origin_ref, sums_ref, from_left_ref, from_right_ref, x_all, res_all, skip_all,
+    lengths_ref, origin_ref, sums_ref, from_left_ref, from_right_ref, x_all, res_all, skip_all,
     w_cat_ref, w_out_ref, slope_ref, gain_ref, shift_ref, taps_ref, tap_bias_ref, slope_mid_ref,
     half_all, mid_all, back_all, edge_ref, out_ref,
     halo_ref, normal_ref, coef_ref,
@@ -193,7 +193,7 @@
 
     @pl.when(pl.program_id(0) == 0)
     def _():
-        mean, scale = first_norm(sums_ref, counts(ends_ref, origin_ref, items, width))
+        mean, scale = first_norm(sums_ref, counts(lengths_ref, items, width))
         coef_ref[0] = jnp.broadcast_to(scale, (items, LANE))
         coef_ref[1] = jnp.broadcast_to(scale * mean, (items, LANE))
         for side, ref in enumerate((from_left_ref, from_right_ref)):
@@ -304,7 +304,7 @@
 
     for number in range(group):
         item = pl.program_id(0) * group + number
-        end = ends_ref[item]
+        end = lengths_ref[item] - origin_ref[0]
         both_ways(end >= frames, functools.partial(run, number, item, end))
 
 
@@ -330,7 +330,7 @@
 
 
 def third_kernel(
-    ends_ref, origin_ref, core_ref, sums_ref, mids_ref, x_all, res_all, skip_all, half_all, mid_all, back_all, edge_all,
+    lengths_ref, origin_ref, core_ref, sums_ref, mids_ref, x_all, res_all, skip_all, half_all, mid_all, back_all, edge_all,
     slope_ref, gain_ref, shift_ref, taps_ref, slope_mid_ref,
     r_high_all, r_low_all, u_high_all, u_low_all, keep_ref, send_ref,
     grad_ref, coef_ref, vector_ref, grads_ref, cot_ref,
@@ -342,7 +342,7 @@
 
     @pl.when(pl.program_id(0) == 0)
     def _():
-        count = counts(ends_ref, origin_ref, items, width)
+        count = counts(lengths_ref, items, width)
         mean1, scale1 = first_norm(sums_ref, count)
         m, mean2, scale2 = second_norm(mids_ref, count)
         beta = scale2 * scale2 * (2.0 * m[3] - mean2 * m[2]) / count
@@ -456,25 +456,22 @@
             vector_ref[3, :, lanes] += shift_sum
             vector_ref[7, :, lanes] += scale2 * sums[1]
 
-        r_high, r_low = r_high_ref[0], r_low_ref[0]
-        mixed = product(
-            jnp.concatenate([d_high, d_low, d_high], axis=1), jnp.concatenate([r_high, r_high, r_low], axis=0)
-        )
+        mixed = product(jnp.concatenate([d_high, d_low], axis=0), r_high_ref[0])
+        mixed = mixed[0 : 2 * cin] + mixed[2 * cin : 4 * cin] + product(d_high, r_low_ref[0])
         z_0 = 2.0 * scale2[0:1]
         for lanes in lane_tiles(width):
             grads_ref[0 : 2 * cin, lanes] += z_0 * mixed[:, lanes]
-        u_high, u_low = u_high_ref[0], u_low_ref[0]
         x_high, x_low = split(x_ref[0])
-        rows_of = jnp.concatenate([x_high, x_low, x_high], axis=1)
-        ones = jnp.ones((GRAD_ROWS, frames), BF16)
-        ones = jnp.concatenate([ones, jnp.zeros((GRAD_ROWS, frames), BF16), ones], axis=1)
-        grads_ref[2 * cin : 3 * cin + GRAD_ROWS] += product(
-            jnp.concatenate([rows_of, ones], axis=0), jnp.concatenate([u_high, u_high, u_low], axis=0)
-        )
+        x_high = jnp.concatenate([x_high, jnp.ones((GRAD_ROWS, frames), BF16)], axis=0)
+        mixed = product(jnp.concatenate([x_high, x_low], axis=0), u_high_ref[0])
+        high_rows = cin + GRAD_ROWS
+        outer_sums = mixed[0:high_rows] + product(x_high, u_low_ref[0])
+        grads_ref[2 * cin : 3 * cin] += outer_sums[0:cin] + mixed[high_rows : high_rows + cin]
+        grads_ref[3 * cin : 3 * cin + GRAD_ROWS] += outer_sums[cin:high_rows]
 
     for number in range(group):
         item = pl.program_id(0) * group + number
-        end = ends_ref[item]
+        end = lengths_ref[item] - origin_ref[0]
         both_ways(end >= frames, functools.partial(run, number, item, end))
 
     @pl.when(pl.program_id(0) == items // group - 1)
@@ -499,7 +496,7 @@
 
 
 def outer_kernel(
-    ends_ref, origin_ref, mids_ref, x_ref, res_ref, r_high_ref, r_low_ref, u_high_ref, u_low_ref,
+    lengths_ref, origin_ref, mids_ref, x_ref, res_ref, r_high_ref, r_low_ref, u_high_ref, u_low_ref,
     w_cat_ref, w_out_ref, w_res_ref, w_skip_ref, gain_ref, shift_ref, bias_res_ref, bias_skip_ref, *rest_refs, offset,
 ):
     res_out_ref, skip_out_ref, x_grad_ref, coef_ref, column_ref, out_turned_ref, in_turned_ref = rest_refs[-7:]
@@ -509,7 +506,7 @@
 
     @pl.when(pl.program_id(0) == 0)
     def _():
-        _, mean, scale = second_norm(mids_ref, counts(ends_ref, origin_ref, items, width))
+        _, mean, scale = second_norm(mids_ref, counts(lengths_ref, items, width))
         coef_ref[0] = jnp.broadcast_to(2.0 * scale, (items, LANE))
         coef_ref[1] = jnp.broadcast_to(scale * mean, (items, LANE))
         high, low = w_out_ref[0 : 2 * cin].T, w_out_ref[4 * cin : 6 * cin].T
@@ -528,7 +525,7 @@
     lane = lax.broadcasted_iota(jnp.int32, (1, LANE), 1)
     for number in range(group):
         item = offset + pl.program_id(0) * group + number
-        end = ends_ref[item]
+        end = lengths_ref[item] - origin_ref[0]
         z_0, z_a = coef_ref[0, pl.ds(item, 1), :], coef_ref[1, pl.ds(item, 1), :]
         r_high, r_low = r_high_ref[number], r_low_ref[number]
         out = product(jnp.concatenate([r_high, r_low, r_high], axis=1), out_turned_ref[...]).T
@@ -586,9 +583,7 @@
             place_half(theirs_ref, 1 - core)
 
 
-def whole(array, space=pltpu.VMEM):
-    if space is pltpu.SMEM:
-        return pl.BlockSpec(memory_space=pltpu.SMEM)
+def whole(array):
     return pl.BlockSpec(array.shape, lambda item: (0,) * len(array.shape))
 
 
@@ -625,7 +620,6 @@
     blocks = lax.axis_size("blk")
     origin = (lax.axis_index("blk") * frames).astype(jnp.int32).reshape(1)
     core = lax.axis_index("core").astype(jnp.int32).reshape(1)
-    ends = lengths - origin[0]
     bias_in, slope_in, gain_in, shift_in, tap_bias, slope_mid, gain_mid, shift_mid, bias_res, bias_skip = (
         vector.reshape(1, -1)
         for vector in (
@@ -633,7 +627,7 @@
         )
     )
     taps = depthwise_weight.T
-    ends_spec = whole(ends, pltpu.SMEM)
+    ends_spec = pl.BlockSpec(memory_space=pltpu.SMEM)
 
     half = sds(items, frames, width)
     halo = sds(items, HALO, 2 * cin)
@@ -646,13 +640,13 @@
     first_sums, to_left, to_right, w_cat, w_out = pl.pallas_call(
         first_kernel,
         grid=(items // quad,),
-        in_specs=[ends_spec, per_item(inputs, quad)]
+        in_specs=[ends_spec, ends_spec, per_item(inputs, quad)]
         + [edge_block(array, quad, spot) for array in (cot_res, cot_skip) for spot in (0, last)]
         + [whole(array) for array in weights],
         out_specs=[whole(sums), per_item(halo, quad), per_item(halo, quad), whole(w_cat), whole(w_out)],
         out_shape=[sums, halo, halo, w_cat, w_out],
         compiler_params=params(),
-    )(ends, inputs, cot_res, cot_res, cot_skip, cot_skip, *weights)
+    )(lengths, origin, inputs, cot_res, cot_res, cot_skip, cot_skip, *weights)
 
     forward = [(block, block + 1) for block in range(blocks - 1)]
     backward = [(target, source) for source, target in forward]
@@ -680,7 +674,7 @@
         ],
         compiler_params=params(),
         cost_estimate=cost(20 * items * frames * cin * width, items * frames * width * 14),
-    )(ends, origin, *small, inputs, cot_res, cot_skip, *weights)
+    )(lengths, origin, *small, inputs, cot_res, cot_skip, *weights)
     mid_sums = exchange(mid_sums, "blk")
 
     small = (first_sums, mid_sums)
@@ -709,7 +703,7 @@
         ],
         compiler_params=params(),
         cost_estimate=cost(18 * items * frames * cin * width, items * frames * width * 20),
-    )(ends, origin, core, *small, *large, *weights)
+    )(lengths, origin, core, *small, *large, *weights)
 
     swap = [(0, 1), (1, 0)]
     keep = keep + lax.ppermute(send, "core", swap)
@@ -740,7 +734,7 @@
             input_output_aliases={17: 0, 18: 1, 19: 2} if earlier else {},
             compiler_params=params(),
             cost_estimate=cost(12 * size * frames * cin * width, size * frames * width * 8),
-        )(ends, origin, mid_sums, *large, *weights, *earlier)
+        )(lengths, origin, mid_sums, *large, *weights, *earlier)
 
     residual_out, skip_out, grad_inputs = outer(0, count, ())
     pieces, residual_out = lax.optimization_barrier((pieces, residual_out))

time: 185 us -> 184 us (level)
  no operation moved by 1% of the time
where the time goes in v5:
time: 184 us; the launch traced here: 183 us
  Pallas kernels  131 us (71%)
  starting transfers between devices  22.2 us (12%)
  blocking collectives  14 us (8%)
  waiting for transfers between devices  10.8 us (6%)
  local copies, waits for them, and re-layouts  2.96 us (2%)
  other arithmetic  1.89 us (1%)
    pallas_call x1, Pallas kernels, local(): pl.pallas_call(third_kernel, grid=(items // pair,), in_specs=[ends_spec]...  48.5 us
    pallas_call x1, Pallas kernels, local(): pl.pallas_call(second_kernel, grid=(items // pair,), in_specs=[ends_spec,...  42.3 us
    pallas_call x2, Pallas kernels, outer(): pl.pallas_call(functools.partial(outer_kernel, offset=offset), grid=(size...  27.6 us
    all_to_all x3, starting transfers between devices, exchange(): return lax.all_to_all(pieces, axes, 0, 0)  15.9 us
    all_to_all x1, blocking collectives, exchange(): return lax.all_to_all(pieces, axes, 0, 0)  14 us
    pallas_call x1, Pallas kernels, local(): pl.pallas_call(first_kernel, grid=(items // quad,), in_specs=[ends_spec,...  9.64 us
    all_to_all x3, waiting for transfers between devices, exchange(): return lax.all_to_all(pieces, axes, 0, 0)  7.01 us
    ppermute x1, starting transfers between devices, local(): from_left = lax.ppermute(to_right, 'blk', forward)  4.88 us
  transfers between devices with their start and end apart: 7, of which 4 were waited for; matrix products, arithmetic and copies ran while one was open for 0% of the time, Pallas kernels for 15%

profile of v5, /device:TPU:0, one launch (start us, length us, event | category | flops | bytes accessed | tf_op | source)
XLA Modules:
  0.0 183.3 jit_solution(3113043805253082887)
XLA Ops:
  0.7 9.6 %shard_map.305 = (f32[8,16,128]{2,1,0:T(8,128)}, f32[16,16,256]{2,1,0:T(8,128)}, f32[16,16,256]{2,1,0:T(8,128)}, bf16[512,512]{1,0:T(8,128)(2,1)}, bf16[768,512]{1,0:T(8,128)(2,1)}) custom-call(s32[16]{0:T(128)} %lengths_ref.9, s32[1]{0:T(128)} %bitcast.origin_ref, f32[16,128,512]{2,1,0:T(8,128)} %x_ref.5, f32[16,128,512]{2,1,0:T(8,128)} %res_ref.3, ...), custom_call_target="tpu_custom_call" | custom-call | tf_op jit(solution)/shard_map/pallas_call | solution.py:640
  10.3 4.9 %collective-permute-start = (f32[16,16,256]{2,1,0:T(8,128)}, f32[16,16,256]{2,1,0:T(8,128)S(1)}, u32[]{:S(2)}, u32[]{:S(2)}) collective-permute-start(f32[16,16,256]{2,1,0:T(8,128)} %get-tuple-element.60), channel_id=1, source_target_pairs={{0,4},{4,8},{8,12},{12,16},{16,20},{20,24},{24,28},{1,5},{5,9},{9,... | collective-permute-start | bytes 786440 | tf_op jit(solution)/shard_map/ppermute | solution.py:654
  15.2 1.3 collective-permute-start.1
  16.5 14.0 %all_to_all.20.sums_ref = f32[8,16,128]{2,1,0:T(8,128)} all-to-all(f32[8,16,128]{2,1,0:T(8,128)} %get-tuple-element.59), channel_id=1, replica_groups=mesh['blk'=8,'side'=2,'core'=2] {'blk'}, dimensions={0} | all-to-all | bytes 131072 | tf_op jit(solution)/shard_map/all_to_all | solution.py:611
  30.5 0.0 collective-permute-done.from_left_ref
  30.5 0.0 copy-start.3
  30.5 0.0 collective-permute-done.1.from_right_ref
  30.5 0.0 copy-start.4
  30.5 0.7 copy-done.3
  31.2 0.1 copy-done.4
  31.3 42.3 %shard_map.306 = (f32[16,512,512]{2,1,0:T(8,128)}, f32[16,528,512]{2,1,0:T(8,128)}, f32[16,512,512]{2,1,0:T(8,128)}, f32[16,16,512]{2,1,0:T(8,128)}, f32[8,16,128]{2,1,0:T(8,128)}) custom-call(s32[16]{0:T(128)} %lengths_ref.9, s32[1]{0:T(128)} %bitcast.origin_ref, f32[8,16,128]{2,1,0:T(8,128)} %all_to_all.20.sums_ref, f32[16,16,256]{2,1,0:T(8,128)} %copy-done.3, ...), custom_call_target="tpu_custom_call" | custom-call | flops 10737418240 | bytes 58720256 | tf_op jit(solution)/shard_map/pallas_call | solution.py:661
  73.6 3.5 %all-to-all-start.1 = ((f32[8,16,128]{2,1,0:T(8,128)}), f32[8,16,128]{2,1,0:T(8,128)S(1)}, u32[]{:S(2)}, u32[]{:S(2)}) async-start(f32[8,16,128]{2,1,0:T(8,128)} %get-tuple-element.64), calls=%async_computation.1 | async-start | bytes 131072 | tf_op jit(solution)/shard_map/all_to_all | solution.py:611
  77.1 6.7 %all-to-all-done.1.mids_ref = f32[8,16,128]{2,1,0:T(8,128)S(1)} async-done(((f32[8,16,128]{2,1,0:T(8,128)}), f32[8,16,128]{2,1,0:T(8,128)S(1)}, u32[]{:S(2)}, u32[]{:S(2)}) %all-to-all-start.1) | async-done | bytes 65568 | tf_op jit(solution)/shard_map/all_to_all | solution.py:611
  83.8 0.0 copy-start.1
  83.8 0.6 copy-done.1
  84.4 48.5 %shard_map.307 = (bf16[16,512,512]{2,1,0:T(8,128)(2,1)}, bf16[16,512,512]{2,1,0:T(8,128)(2,1)}, bf16[16,512,512]{2,1,0:T(8,128)(2,1)}, bf16[16,512,512]{2,1,0:T(...) custom-call(s32[16]{0:T(128)} %lengths_ref.9, s32[1]{0:T(128)} %bitcast.origin_ref, s32[1]{0:T(128)} %bitcast.1.core_ref, ...), custom_call_target="tpu_custom_call" | custom-call | flops 9663676416 | bytes 83886080 | tf_op jit(solution)/shard_map/pallas_call | solution.py:688
  132.9 0.1 collective-permute-start.2
  133.0 2.0 %collective-permute-done.2 = f32[896,128]{1,0:T(8,128)S(1)} collective-permute-done((f32[896,128]{1,0:T(8,128)}, f32[896,128]{1,0:T(8,128)S(1)}, u32[]{:S(2)}, u32[]{:S(2)}) %collective-permute-start.2) | collective-permute-done | bytes 458784 | tf_op jit(solution)/shard_map/ppermute | solution.py:709
  135.0 1.9 %add.3 = f32[896,128]{1,0:T(8,128)} add(f32[896,128]{1,0:T(8,128)} %get-tuple-element.69, f32[896,128]{1,0:T(8,128)S(1)} %collective-permute-done.2) | non-fusion elementwise | flops 114688 | bytes 1376256 | tf_op jit(solution)/shard_map/add | solution.py:709
  136.8 5.8 %all-to-all-start.2 = ((f32[16,56,128]{2,1,0:T(8,128)}), f32[16,56,128]{2,1,0:T(8,128)S(1)}, u32[]{:S(2)}, u32[]{:S(2)}) async-start(f32[16,56,128]{2,1,0:T(8,128)} %bitcast.10), calls=%async_computation.2 | async-start | bytes 917504 | tf_op jit(solution)/shard_map/all_to_all | solution.py:611
  142.7 13.8 %shard_map.308 = (f32[16,128,512]{2,1,0:T(8,128)}, f32[16,128,512]{2,1,0:T(8,128)}, f32[16,128,512]{2,1,0:T(8,128)}) custom-call(s32[16]{0:T(128)} %lengths_ref.9, s32[1]{0:T(128)} %bitcast.origin_ref, f32[8,16,128]{2,1,0:T(8,128)} %copy-done.1, f32[16,128,512]{2,1,0:T(8,128)} %x_ref.5, f32[16,128,512]{2,1,0:T(8,128)} %res_ref.3, ...), custom_call_target="tpu_custom_call" | custom-call | flops 3221225472 | bytes 16777216 | tf_op jit(solution)/shard_map/pallas_call | solution.py:719
  156.5 0.3 all-to-all-done.2
  156.9 0.8 broadcast_in_dim.3
  157.7 6.6 %all-to-all-start.3 = ((f32[16,56,128]{2,1,0:T(8,128)}), f32[16,56,128]{2,1,0:T(8,128)S(1)}, u32[]{:S(2)}, u32[]{:S(2)}) async-start(f32[16,56,128]{2,1,0:T(8,128)} %broadcast_in_dim.3), calls=%async_computation.3 | async-start | bytes 917504 | tf_op jit(solution)/shard_map/all_to_all | solution.py:611
  164.2 13.8 %shard_map.309 = (f32[16,128,512]{2,1,0:T(8,128)}, f32[16,128,512]{2,1,0:T(8,128)}, f32[16,128,512]{2,1,0:T(8,128)}) custom-call(s32[16]{0:T(128)} %lengths_ref.9, s32[1]{0:T(128)} %bitcast.origin_ref, f32[8,16,128]{2,1,0:T(8,128)} %copy-done.1, f32[16,128,512]{2,1,0:T(8,128)} %x_ref.5, ...), custom_call_target="tpu_custom_call", output_to_operand_aliasing={{0}: (17, {}), {1}: (18, {}), {2}: (19, {})} | custom-call | flops 3221225472 | bytes 16777216 | tf_op jit(solution)/shard_map/pallas_call | solution.py:719
  178.1 0.0 all-to-all-done.3
  178.1 0.0 copy-start
  178.1 0.1 collective-permute-start.3
  178.2 1.8 collective-permute-done.3.theirs_ref
  180.0 0.0 copy-done
  180.0 0.0 copy-start.2
  180.0 0.8 copy-done.2
  180.7 2.5 %shard_map.310 = (f32[512,128]{1,0:T(8,128)}, f32[1,512]{1,0:T(1,128)}, f32[1,512]{1,0:T(1,128)}, f32[1,512]{1,0:T(1,128)}, f32[1,512]{1,0:T(1,128)}, /*index=5*...) custom-call(s32[1]{0:T(128)} %bitcast.1.core_ref, ...), custom_call_target="tpu_custom_call" | custom-call | tf_op jit(solution)/shard_map/pallas_call | solution.py:750
  (1 shorter events, 0.0 us)
Async XLA Ops:
  10.3 20.2 %collective-permute-start = (f32[16,16,256]{2,1,0:T(8,128)}, f32[16,16,256]{2,1,0:T(8,128)S(1)}, u32[]{:S(2)}, u32[]{:S(2)}) collective-permute-start(f32[16,16,256]{2,1,0:T(8,128)} %get-tuple-element.60), channel_id=1, source_target_pairs={{0,4},{4,8},{8,12},{12,16},{16,20},{20,24},{24,28},{1,5},{5,9},{9,... | collective-permute-start | bytes 786440 | tf_op jit(solution)/shard_map/ppermute | solution.py:654
  15.2 15.3 %collective-permute-start.1 = (f32[16,16,256]{2,1,0:T(8,128)}, f32[16,16,256]{2,1,0:T(8,128)S(1)}, u32[]{:S(2)}, u32[]{:S(2)}) collective-permute-start(f32[16,16,256]{2,1,0:T(8,128)} %get-tuple-element.61), channel_id=1, source_target_pairs={{4,0},{8,4},{12,8},{16,12},{20,16},{24,20},{28,24},{5,1},{9,5},{13... | collective-permute-start | bytes 786440 | tf_op jit(solution)/shard_map/ppermute | solution.py:655
  30.5 0.7 copy-start.3
  30.5 0.8 copy-start.4
  73.6 10.2 %all-to-all-start.1 = ((f32[8,16,128]{2,1,0:T(8,128)}), f32[8,16,128]{2,1,0:T(8,128)S(1)}, u32[]{:S(2)}, u32[]{:S(2)}) async-start(f32[8,16,128]{2,1,0:T(8,128)} %get-tuple-element.64), calls=%async_computation.1 | async-start | bytes 131072 | tf_op jit(solution)/shard_map/all_to_all | solution.py:611
  83.8 0.6 copy-start.1
  132.9 2.1 %collective-permute-start.2 = (f32[896,128]{1,0:T(8,128)}, f32[896,128]{1,0:T(8,128)S(1)}, u32[]{:S(2)}, u32[]{:S(2)}) collective-permute-start(f32[896,128]{1,0:T(8,128)} %get-tuple-element.70), channel_id=1, source_target_pairs={{0,1},{1,0},{2,3},{3,2},{4,5},{5,4},{6,7},{7,6},{8,9},{9,8},{10,11... | collective-permute-start | bytes 1376264 | tf_op jit(solution)/shard_map/ppermute | solution.py:709
  136.8 20.0 %all-to-all-start.2 = ((f32[16,56,128]{2,1,0:T(8,128)}), f32[16,56,128]{2,1,0:T(8,128)S(1)}, u32[]{:S(2)}, u32[]{:S(2)}) async-start(f32[16,56,128]{2,1,0:T(8,128)} %bitcast.10), calls=%async_computation.2 | async-start | bytes 917504 | tf_op jit(solution)/shard_map/all_to_all | solution.py:611
  157.7 20.4 %all-to-all-start.3 = ((f32[16,56,128]{2,1,0:T(8,128)}), f32[16,56,128]{2,1,0:T(8,128)S(1)}, u32[]{:S(2)}, u32[]{:S(2)}) async-start(f32[16,56,128]{2,1,0:T(8,128)} %broadcast_in_dim.3), calls=%async_computation.3 | async-start | bytes 917504 | tf_op jit(solution)/shard_map/all_to_all | solution.py:611
  178.1 1.9 %copy-start = (f32[16,56,128]{2,1,0:T(8,128)}, f32[16,56,128]{2,1,0:T(8,128)S(1)}, u32[]{:S(2)}) copy-start(f32[16,56,128]{2,1,0:T(8,128)S(1)} %all-to-all-done.3) | copy-start | bytes 1376260
  178.1 1.9 %collective-permute-start.3 = (f32[896,128]{1,0:T(8,128)S(1)}, f32[896,128]{1,0:T(8,128)S(1)}, u32[]{:S(2)}, u32[]{:S(2)}) collective-permute-start(f32[896,128]{1,0:T(8,128)S(1)} %bitcast.26), channel_id=1, source_target_pairs={{0,1},{1,0},{2,3},{3,2},{4,5},{5,4},{6,7},{7,6},{8,9},{9,8},{10,11... | collective-permute-start | bytes 1376264 | tf_op jit(solution)/shard_map/ppermute | solution.py:744
  180.0 0.8 copy-start.2

commit v6 on v5

--- a/solution.py
+++ b/solution.py
@@ -456,18 +456,21 @@
             vector_ref[3, :, lanes] += shift_sum
             vector_ref[7, :, lanes] += scale2 * sums[1]
 
-        mixed = product(jnp.concatenate([d_high, d_low], axis=0), r_high_ref[0])
-        mixed = mixed[0 : 2 * cin] + mixed[2 * cin : 4 * cin] + product(d_high, r_low_ref[0])
+        r_high, r_low = r_high_ref[0], r_low_ref[0]
+        mixed = product(
+            jnp.concatenate([d_high, d_low, d_high], axis=1), jnp.concatenate([r_high, r_high, r_low], axis=0)
+        )
         z_0 = 2.0 * scale2[0:1]
         for lanes in lane_tiles(width):
             grads_ref[0 : 2 * cin, lanes] += z_0 * mixed[:, lanes]
+        u_high, u_low = u_high_ref[0], u_low_ref[0]
         x_high, x_low = split(x_ref[0])
-        x_high = jnp.concatenate([x_high, jnp.ones((GRAD_ROWS, frames), BF16)], axis=0)
-        mixed = product(jnp.concatenate([x_high, x_low], axis=0), u_high_ref[0])
-        high_rows = cin + GRAD_ROWS
-        outer_sums = mixed[0:high_rows] + product(x_high, u_low_ref[0])
-        grads_ref[2 * cin : 3 * cin] += outer_sums[0:cin] + mixed[high_rows : high_rows + cin]
-        grads_ref[3 * cin : 3 * cin + GRAD_ROWS] += outer_sums[cin:high_rows]
+        rows_of = jnp.concatenate([x_high, x_low, x_high], axis=1)
+        ones = jnp.ones((GRAD_ROWS, frames), BF16)
+        ones = jnp.concatenate([ones, jnp.zeros((GRAD_ROWS, frames), BF16), ones], axis=1)
+        grads_ref[2 * cin : 3 * cin + GRAD_ROWS] += product(
+            jnp.concatenate([rows_of, ones], axis=0), jnp.concatenate([u_high, u_high, u_low], axis=0)
+        )
 
     for number in range(group):
         item = pl.program_id(0) * group + number
@@ -636,14 +639,13 @@
     w_cat, w_out = sds(3 * cin + LANE, width, dtype=BF16), sds(6 * cin, width, dtype=BF16)
     weights = (weight_in, bias_in, slope_in, weight_res, weight_skip, gain_mid)
     pair = 2 if items % 2 == 0 else 1
-    quad = 4 if items % 4 == 0 else 1
     first_sums, to_left, to_right, w_cat, w_out = pl.pallas_call(
         first_kernel,
-        grid=(items // quad,),
-        in_specs=[ends_spec, ends_spec, per_item(inputs, quad)]
-        + [edge_block(array, quad, spot) for array in (cot_res, cot_skip) for spot in (0, last)]
+        grid=(items // pair,),
+        in_specs=[ends_spec, ends_spec, per_item(inputs, pair)]
+        + [edge_block(array, pair, spot) for array in (cot_res, cot_skip) for spot in (0, last)]
         + [whole(array) for array in weights],
-        out_specs=[whole(sums), per_item(halo, quad), per_item(halo, quad), whole(w_cat), whole(w_out)],
+        out_specs=[whole(sums), per_item(halo, pair), per_item(halo, pair), whole(w_cat), whole(w_out)],
         out_shape=[sums, halo, halo, w_cat, w_out],
         compiler_params=params(),
     )(lengths, origin, inputs, cot_res, cot_res, cot_skip, cot_skip, *weights)

time: 184 us -> 184 us (level)
  starting transfers between devices: 22.2 us -> 19.8 us
    all_to_all x3, starting transfers between devices: 15.9 us -> 13.5 us  [exchange(): return lax.all_to_all(pieces, axes, 0, 0)]
    pallas_call x1, Pallas kernels: 9.64 us -> 11.5 us  [local(): pl.pallas_call(first_kernel, grid=(items // pair,), in_specs=[ends_spec,...]
where the time goes in v6:
time: 184 us; the launch traced here: 183 us
  Pallas kernels  132 us (72%)
  starting transfers between devices  19.8 us (11%)
  blocking collectives  14 us (8%)
  waiting for transfers between devices  11 us (6%)
  local copies, waits for them, and re-layouts  2.96 us (2%)
  other arithmetic  1.89 us (1%)
    pallas_call x1, Pallas kernels, local(): pl.pallas_call(third_kernel, grid=(items // pair,), in_specs=[ends_spec]...  48.2 us
    pallas_call x1, Pallas kernels, local(): pl.pallas_call(second_kernel, grid=(items // pair,), in_specs=[ends_spec,...  42.3 us
    pallas_call x2, Pallas kernels, outer(): pl.pallas_call(functools.partial(outer_kernel, offset=offset), grid=(size...  27.6 us
    all_to_all x1, blocking collectives, exchange(): return lax.all_to_all(pieces, axes, 0, 0)  14 us
    all_to_all x3, starting transfers between devices, exchange(): return lax.all_to_all(pieces, axes, 0, 0)  13.5 us
    pallas_call x1, Pallas kernels, local(): pl.pallas_call(first_kernel, grid=(items // pair,), in_specs=[ends_spec,...  11.5 us
    all_to_all x3, waiting for transfers between devices, exchange(): return lax.all_to_all(pieces, axes, 0, 0)  7.16 us
    ppermute x1, starting transfers between devices, local(): from_left = lax.ppermute(to_right, 'blk', forward)  4.87 us
  transfers between devices with their start and end apart: 7, of which 4 were waited for; matrix products, arithmetic and copies ran while one was open for 0% of the time, Pallas kernels for 15%

profile of v6, /device:TPU:0, one launch (start us, length us, event | category | flops | bytes accessed | tf_op | source)
XLA Modules:
  0.0 182.7 jit_solution(15189933817381904924)
XLA Ops:
  0.7 11.5 %shard_map.305 = (f32[8,16,128]{2,1,0:T(8,128)}, f32[16,16,256]{2,1,0:T(8,128)}, f32[16,16,256]{2,1,0:T(8,128)}, bf16[512,512]{1,0:T(8,128)(2,1)}, bf16[768,512]{1,0:T(8,128)(2,1)}) custom-call(s32[16]{0:T(128)} %lengths_ref.9, s32[1]{0:T(128)} %bitcast.origin_ref, f32[16,128,512]{2,1,0:T(8,128)} %x_ref.5, f32[16,128,512]{2,1,0:T(8,128)} %res_ref.3, ...), custom_call_target="tpu_custom_call" | custom-call | tf_op jit(solution)/shard_map/pallas_call | solution.py:642
  12.2 4.9 %collective-permute-start = (f32[16,16,256]{2,1,0:T(8,128)}, f32[16,16,256]{2,1,0:T(8,128)S(1)}, u32[]{:S(2)}, u32[]{:S(2)}) collective-permute-start(f32[16,16,256]{2,1,0:T(8,128)} %get-tuple-element.60), channel_id=1, source_target_pairs={{0,4},{4,8},{8,12},{12,16},{16,20},{20,24},{24,28},{1,5},{5,9},{9,... | collective-permute-start | bytes 786440 | tf_op jit(solution)/shard_map/ppermute | solution.py:656
  17.1 1.3 collective-permute-start.1
  18.4 14.0 %all_to_all.20.sums_ref = f32[8,16,128]{2,1,0:T(8,128)} all-to-all(f32[8,16,128]{2,1,0:T(8,128)} %get-tuple-element.59), channel_id=1, replica_groups=mesh['blk'=8,'side'=2,'core'=2] {'blk'}, dimensions={0} | all-to-all | bytes 131072 | tf_op jit(solution)/shard_map/all_to_all | solution.py:614
  32.3 0.0 collective-permute-done.from_left_ref
  32.3 0.0 copy-start.3
  32.3 0.0 collective-permute-done.1.from_right_ref
  32.3 0.0 copy-start.4
  32.4 0.7 copy-done.3
  33.0 0.1 copy-done.4
  33.1 42.3 %shard_map.306 = (f32[16,512,512]{2,1,0:T(8,128)}, f32[16,528,512]{2,1,0:T(8,128)}, f32[16,512,512]{2,1,0:T(8,128)}, f32[16,16,512]{2,1,0:T(8,128)}, f32[8,16,128]{2,1,0:T(8,128)}) custom-call(s32[16]{0:T(128)} %lengths_ref.9, s32[1]{0:T(128)} %bitcast.origin_ref, f32[8,16,128]{2,1,0:T(8,128)} %all_to_all.20.sums_ref, f32[16,16,256]{2,1,0:T(8,128)} %copy-done.3, ...), custom_call_target="tpu_custom_call" | custom-call | flops 10737418240 | bytes 58720256 | tf_op jit(solution)/shard_map/pallas_call | solution.py:663
  75.4 3.5 %all-to-all-start.1 = ((f32[8,16,128]{2,1,0:T(8,128)}), f32[8,16,128]{2,1,0:T(8,128)S(1)}, u32[]{:S(2)}, u32[]{:S(2)}) async-start(f32[8,16,128]{2,1,0:T(8,128)} %get-tuple-element.64), calls=%async_computation.1 | async-start | bytes 131072 | tf_op jit(solution)/shard_map/all_to_all | solution.py:614
  79.0 6.7 %all-to-all-done.1.mids_ref = f32[8,16,128]{2,1,0:T(8,128)S(1)} async-done(((f32[8,16,128]{2,1,0:T(8,128)}), f32[8,16,128]{2,1,0:T(8,128)S(1)}, u32[]{:S(2)}, u32[]{:S(2)}) %all-to-all-start.1) | async-done | bytes 65568 | tf_op jit(solution)/shard_map/all_to_all | solution.py:614
  85.7 0.0 copy-start.1
  85.7 0.6 copy-done.1
  86.3 48.2 %shard_map.307 = (bf16[16,512,512]{2,1,0:T(8,128)(2,1)}, bf16[16,512,512]{2,1,0:T(8,128)(2,1)}, bf16[16,512,512]{2,1,0:T(8,128)(2,1)}, bf16[16,512,512]{2,1,0:T(...) custom-call(s32[16]{0:T(128)} %lengths_ref.9, s32[1]{0:T(128)} %bitcast.origin_ref, s32[1]{0:T(128)} %bitcast.1.core_ref, ...), custom_call_target="tpu_custom_call" | custom-call | flops 9663676416 | bytes 83886080 | tf_op jit(solution)/shard_map/pallas_call | solution.py:690
  134.5 0.1 collective-permute-start.2
  134.6 2.0 %collective-permute-done.2 = f32[896,128]{1,0:T(8,128)S(1)} collective-permute-done((f32[896,128]{1,0:T(8,128)}, f32[896,128]{1,0:T(8,128)S(1)}, u32[]{:S(2)}, u32[]{:S(2)}) %collective-permute-start.2) | collective-permute-done | bytes 458784 | tf_op jit(solution)/shard_map/ppermute | solution.py:711
  136.6 1.9 %add.3 = f32[896,128]{1,0:T(8,128)} add(f32[896,128]{1,0:T(8,128)} %get-tuple-element.69, f32[896,128]{1,0:T(8,128)S(1)} %collective-permute-done.2) | non-fusion elementwise | flops 114688 | bytes 1376256 | tf_op jit(solution)/shard_map/add | solution.py:711
  138.5 3.6 %all-to-all-start.2 = ((f32[16,56,128]{2,1,0:T(8,128)}), f32[16,56,128]{2,1,0:T(8,128)S(1)}, u32[]{:S(2)}, u32[]{:S(2)}) async-start(f32[16,56,128]{2,1,0:T(8,128)} %bitcast.10), calls=%async_computation.2 | async-start | bytes 917504 | tf_op jit(solution)/shard_map/all_to_all | solution.py:614
  142.0 13.8 %shard_map.308 = (f32[16,128,512]{2,1,0:T(8,128)}, f32[16,128,512]{2,1,0:T(8,128)}, f32[16,128,512]{2,1,0:T(8,128)}) custom-call(s32[16]{0:T(128)} %lengths_ref.9, s32[1]{0:T(128)} %bitcast.origin_ref, f32[8,16,128]{2,1,0:T(8,128)} %copy-done.1, f32[16,128,512]{2,1,0:T(8,128)} %x_ref.5, f32[16,128,512]{2,1,0:T(8,128)} %res_ref.3, ...), custom_call_target="tpu_custom_call" | custom-call | flops 3221225472 | bytes 16777216 | tf_op jit(solution)/shard_map/pallas_call | solution.py:721
  155.9 0.4 all-to-all-done.2
  156.3 0.8 broadcast_in_dim.3
  157.1 6.4 %all-to-all-start.3 = ((f32[16,56,128]{2,1,0:T(8,128)}), f32[16,56,128]{2,1,0:T(8,128)S(1)}, u32[]{:S(2)}, u32[]{:S(2)}) async-start(f32[16,56,128]{2,1,0:T(8,128)} %broadcast_in_dim.3), calls=%async_computation.3 | async-start | bytes 917504 | tf_op jit(solution)/shard_map/all_to_all | solution.py:614
  163.6 13.8 %shard_map.309 = (f32[16,128,512]{2,1,0:T(8,128)}, f32[16,128,512]{2,1,0:T(8,128)}, f32[16,128,512]{2,1,0:T(8,128)}) custom-call(s32[16]{0:T(128)} %lengths_ref.9, s32[1]{0:T(128)} %bitcast.origin_ref, f32[8,16,128]{2,1,0:T(8,128)} %copy-done.1, f32[16,128,512]{2,1,0:T(8,128)} %x_ref.5, ...), custom_call_target="tpu_custom_call", output_to_operand_aliasing={{0}: (17, {}), {1}: (18, {}), {2}: (19, {})} | custom-call | flops 3221225472 | bytes 16777216 | tf_op jit(solution)/shard_map/pallas_call | solution.py:721
  177.4 0.1 all-to-all-done.3
  177.5 0.0 copy-start
  177.5 0.0 collective-permute-start.3
  177.5 1.8 collective-permute-done.3.theirs_ref
  179.3 0.0 copy-done
  179.3 0.0 copy-start.2
  179.3 0.8 copy-done.2
  180.1 2.5 %shard_map.310 = (f32[512,128]{1,0:T(8,128)}, f32[1,512]{1,0:T(1,128)}, f32[1,512]{1,0:T(1,128)}, f32[1,512]{1,0:T(1,128)}, f32[1,512]{1,0:T(1,128)}, /*index=5*...) custom-call(s32[1]{0:T(128)} %bitcast.1.core_ref, ...), custom_call_target="tpu_custom_call" | custom-call | tf_op jit(solution)/shard_map/pallas_call | solution.py:752
  (1 shorter events, 0.0 us)
Async XLA Ops:
  12.2 20.1 %collective-permute-start = (f32[16,16,256]{2,1,0:T(8,128)}, f32[16,16,256]{2,1,0:T(8,128)S(1)}, u32[]{:S(2)}, u32[]{:S(2)}) collective-permute-start(f32[16,16,256]{2,1,0:T(8,128)} %get-tuple-element.60), channel_id=1, source_target_pairs={{0,4},{4,8},{8,12},{12,16},{16,20},{20,24},{24,28},{1,5},{5,9},{9,... | collective-permute-start | bytes 786440 | tf_op jit(solution)/shard_map/ppermute | solution.py:656
  17.1 15.3 %collective-permute-start.1 = (f32[16,16,256]{2,1,0:T(8,128)}, f32[16,16,256]{2,1,0:T(8,128)S(1)}, u32[]{:S(2)}, u32[]{:S(2)}) collective-permute-start(f32[16,16,256]{2,1,0:T(8,128)} %get-tuple-element.61), channel_id=1, source_target_pairs={{4,0},{8,4},{12,8},{16,12},{20,16},{24,20},{28,24},{5,1},{9,5},{13... | collective-permute-start | bytes 786440 | tf_op jit(solution)/shard_map/ppermute | solution.py:657
  32.3 0.7 copy-start.3
  32.3 0.8 copy-start.4
  75.4 10.2 %all-to-all-start.1 = ((f32[8,16,128]{2,1,0:T(8,128)}), f32[8,16,128]{2,1,0:T(8,128)S(1)}, u32[]{:S(2)}, u32[]{:S(2)}) async-start(f32[8,16,128]{2,1,0:T(8,128)} %get-tuple-element.64), calls=%async_computation.1 | async-start | bytes 131072 | tf_op jit(solution)/shard_map/all_to_all | solution.py:614
  85.7 0.6 copy-start.1
  134.5 2.1 %collective-permute-start.2 = (f32[896,128]{1,0:T(8,128)}, f32[896,128]{1,0:T(8,128)S(1)}, u32[]{:S(2)}, u32[]{:S(2)}) collective-permute-start(f32[896,128]{1,0:T(8,128)} %get-tuple-element.70), channel_id=1, source_target_pairs={{0,1},{1,0},{2,3},{3,2},{4,5},{5,4},{6,7},{7,6},{8,9},{9,8},{10,11... | collective-permute-start | bytes 1376264 | tf_op jit(solution)/shard_map/ppermute | solution.py:711
  138.5 17.8 %all-to-all-start.2 = ((f32[16,56,128]{2,1,0:T(8,128)}), f32[16,56,128]{2,1,0:T(8,128)S(1)}, u32[]{:S(2)}, u32[]{:S(2)}) async-start(f32[16,56,128]{2,1,0:T(8,128)} %bitcast.10), calls=%async_computation.2 | async-start | bytes 917504 | tf_op jit(solution)/shard_map/all_to_all | solution.py:614
  157.1 20.3 %all-to-all-start.3 = ((f32[16,56,128]{2,1,0:T(8,128)}), f32[16,56,128]{2,1,0:T(8,128)S(1)}, u32[]{:S(2)}, u32[]{:S(2)}) async-start(f32[16,56,128]{2,1,0:T(8,128)} %broadcast_in_dim.3), calls=%async_computation.3 | async-start | bytes 917504 | tf_op jit(solution)/shard_map/all_to_all | solution.py:614
  177.5 1.9 %copy-start = (f32[16,56,128]{2,1,0:T(8,128)}, f32[16,56,128]{2,1,0:T(8,128)S(1)}, u32[]{:S(2)}) copy-start(f32[16,56,128]{2,1,0:T(8,128)S(1)} %all-to-all-done.3) | copy-start | bytes 1376260
  177.5 1.9 %collective-permute-start.3 = (f32[896,128]{1,0:T(8,128)S(1)}, f32[896,128]{1,0:T(8,128)S(1)}, u32[]{:S(2)}, u32[]{:S(2)}) collective-permute-start(f32[896,128]{1,0:T(8,128)S(1)} %bitcast.26), channel_id=1, source_target_pairs={{0,1},{1,0},{2,3},{3,2},{4,5},{5,4},{6,7},{7,6},{8,9},{9,8},{10,11... | collective-permute-start | bytes 1376264 | tf_op jit(solution)/shard_map/ppermute | solution.py:746
  179.3 0.8 copy-start.2
